TPU v7x, 32 devices: a whole 2x2x4 slice. The times are simulated.
32 devices in a mesh: dp: 8 (over z, y), expert: 4 (over x, core).
Axes of the slice: x: 2, y: 2, z: 4, core: 2. Of those that a mesh axis runs over, the one named last changes fastest.
Arguments:
- residual_input: bfloat16 [8192, 1024], P(('dp', 'expert')), may hold values from -6 to 6
- prompt_token_length: int32 [48], replicated, may hold values from 1 to 1024, 8192 in all
- prompt_adapter_index: int32 [48], replicated, may hold values from 0 to 63
- adapter_table_row: int32 [64], replicated, may hold values from 0 to 63, each once
- adapter_norm_gain: bfloat16 [1024], replicated, may hold values from 0.5 to 1.5
- adapter_down_maps: bfloat16 [64, 16, 1024], P('expert'), may hold values from -0.1875 to 0.1875
- adapter_up_maps: bfloat16 [64, 16, 1024], P('expert'), may hold values from -1.5 to 1.5
- expert_norm_gain: bfloat16 [1024], replicated, may hold values from 0.5 to 1.5
- router: bfloat16 [1024, 4], replicated, may hold values from -0.1875 to 0.1875
- token_expert_index: int32 [8192, 2], P(('dp', 'expert')), may hold values from 0 to 3, all different within a row; in each aligned block of 256 rows (0 to 255, 256 to 511, ...) at most 160 rows name the same one
- expert_gate_up_weight: bfloat16 [4, 2, 1024, 2816], P('expert', None, None, 'dp'), may hold values from -0.1875 to 0.1875
- expert_down_weight: bfloat16 [4, 2816, 1024], P('expert', None, 'dp'), may hold values from -0.109375 to 0.109375
Outputs:
- layer_out: bfloat16 [8192, 1024], P(('dp', 'expert'))
Inputs may be any that keep to these rules, and one draw needn't show every extreme that they name: `prompt_token_length`: the lengths sum to 8192; the longest is exactly 1024. `adapter_table_row`: each adapter has its own row of adapter_down_maps and adapter_up_maps: a permutation. `token_expert_index`: the two ids of a token differ. Within the 256 rows of one device no expert is named by more than 160 rows, a bound that some block reaches.
All inputs are finite; a program needn't handle non-finite values.
Results may differ from a plain program's by a relative error of at most 0.0064.
Values may be sent and summed in bfloat16 or wider, within the bound.
No kernel may reach another device: no remote copies, remote signals or barrier semaphores. Data moves between devices by JAX's collectives and lax.ppermute only.
A program may use at most 128 MiB of HBM per device.

v0:
```python
import functools

import jax
import jax.numpy as jnp
from jax import lax
from jax.experimental import pallas as pl
from jax.experimental.pallas import tpu as pltpu
from jax.sharding import Mesh
from jax.sharding import PartitionSpec as P

CORES = 2
LANES = 128
EXTRA = 16
VMEM = 56 * 2**20


def from_offset(value, axis, size, offset):
    if offset % size == 0:
        return value
    return lax.ppermute(value, axis, [((i + offset) % size, i) for i in range(size)])


def together(*values):
    return lax.optimization_barrier(values)


def across(value, size, mask):
    return lax.ppermute(value, "line", [(i ^ mask, i) for i in range(size)]) if mask else value


def dot(a, b, rhs_dim=0):
    return lax.dot_general(a, b, (((1,), (rhs_dim,)), ((), ())), preferred_element_type=jnp.float32)


def rms_norm(values, gain):
    stat = jnp.mean(values * values, axis=-1, keepdims=True)
    return values * lax.rsqrt(stat + 1e-06) * gain.astype(jnp.float32)


def whole(array):
    return pl.BlockSpec(array.shape, lambda *_: (0,) * len(array.shape))


def brief():
    return pl.CostEstimate(flops=1, transcendentals=0, bytes_accessed=1)


def front_kernel(pieces, blocks, rows, base_ref, prompts_ref, owner_ref, gain_a_ref, gain_e_ref, router_ref, *refs):
    table_refs, refs = refs[: 2 * pieces], refs[2 * pieces :]
    token_refs, refs = refs[:blocks], refs[blocks:]
    mixed_ref, weight_ref, inner_refs = refs[0], refs[1], refs[2:]
    for k in range(blocks):
        at = base_ref[k] + lax.broadcasted_iota(jnp.int32, (rows, 1), 0)
        inside = (at >= prompts_ref[0:1, :]) & (at < prompts_ref[1:2, :])
        slot = jnp.sum(jnp.where(inside, prompts_ref[2:3, :], 0), axis=1, keepdims=True)
        floats = token_refs[k][0:rows, :].astype(jnp.float32)
        normed = rms_norm(floats, gain_a_ref[...]).astype(jnp.bfloat16)
        delta = jnp.zeros(floats.shape, jnp.float32)
        first = 0
        for p in range(pieces):
            down_ref, up_ref = table_refs[2 * p], table_refs[2 * p + 1]
            size = down_ref.shape[0]
            low = dot(normed, down_ref[...], 1)
            low = jnp.where(owner_ref[0:1, first : first + size] == slot, low, 0.0).astype(jnp.bfloat16)
            delta = delta + dot(low, up_ref[...])
            first += size
        mixed = (floats + 2.0 * delta).astype(jnp.bfloat16)
        if k == 0:
            mixed_ref[...] = mixed
        inner = rms_norm(mixed.astype(jnp.float32), gain_e_ref[...]).astype(jnp.bfloat16)
        inner_refs[k][...] = inner
        prob = jax.nn.sigmoid(dot(router_ref[...], inner, 1))
        expert = lax.broadcasted_iota(jnp.int32, (LANES, rows), 0).astype(jnp.float32)
        ids = token_refs[k][rows : rows + EXTRA, :].astype(jnp.float32)
        chosen = (ids[0:1, 0:rows] == expert) | (ids[1:2, 0:rows] == expert)
        weight_ref[k * rows : (k + 1) * rows, :] = jnp.where(chosen, prob, 0.0).T


def front(bases, prompts, owner, gain_a, gain_e, router, tables, tokens):
    rows = tokens[0].shape[0] - EXTRA
    width = tokens[0].shape[1]
    blocks = len(tokens)
    block = jax.ShapeDtypeStruct((rows, width), jnp.bfloat16)
    outs = [block, jax.ShapeDtypeStruct((blocks * rows, LANES), jnp.float32)] + [block] * blocks
    arrays = [prompts, owner, gain_a, gain_e, router, *tables, *tokens]
    mixed, weight, *inner = pl.pallas_call(
        functools.partial(front_kernel, len(tables) // 2, blocks, rows),
        out_shape=outs,
        grid=(1,),
        in_specs=[pl.BlockSpec(memory_space=pltpu.SMEM)] + [whole(a) for a in arrays],
        out_specs=[whole(a) for a in outs],
        compiler_params=pltpu.CompilerParams(vmem_limit_bytes=VMEM),
        cost_estimate=brief(),
        name="front",
    )(bases, *arrays)
    return mixed, weight, inner


def hidden(x, weight, gate, up):
    act = jax.nn.gelu(dot(x, gate, 1), approximate=True) * dot(x, up, 1) * weight
    return act.astype(jnp.bfloat16)


def final_kernel(los, lines, count, lo_ref, mixed_ref, *refs):
    out_ref = refs[-1]
    cols = mixed_ref.shape[1] // (los * lines)
    for j in range(los):
        parts = refs[j * count : (j + 1) * count]
        total = parts[0][...].astype(jnp.float32)
        for part in parts[1:]:
            total = total + part[...].astype(jnp.float32)
        for h in range(lines):
            first = (h * los + lax.rem(lo_ref[0] + j, los)) * cols
            place = pl.ds(pl.multiple_of(first, LANES), cols)
            own = mixed_ref[:, place].astype(jnp.float32)
            out_ref[:, place] = (own + total[:, h * cols : (h + 1) * cols]).astype(jnp.bfloat16)


def final(lines, lo, mixed, parts):
    los, count = len(parts), len(parts[0])
    rows, width = mixed.shape
    if width // (los * lines) % LANES:
        sums = [sum(p.astype(jnp.float32) for p in group).reshape(rows, lines, -1) for group in parts]
        total = jnp.roll(jnp.stack(sums, axis=2), lo[0], axis=2).reshape(rows, width)
        return (mixed.astype(jnp.float32) + total).astype(jnp.bfloat16)
    flat = [p for group in parts for p in group]
    return pl.pallas_call(
        functools.partial(final_kernel, los, lines, count),
        out_shape=jax.ShapeDtypeStruct(mixed.shape, jnp.bfloat16),
        grid=(1,),
        in_specs=[pl.BlockSpec(memory_space=pltpu.SMEM)] + [whole(a) for a in (mixed, *flat)],
        out_specs=whole(mixed),
        compiler_params=pltpu.CompilerParams(vmem_limit_bytes=VMEM // 4),
        cost_estimate=brief(),
        name="final",
    )(lo, mixed, *flat)


def on_device(
    sizes,
    residual_input,
    prompt_token_length,
    prompt_adapter_index,
    adapter_table_row,
    adapter_norm_gain,
    adapter_down_maps,
    adapter_up_maps,
    expert_norm_gain,
    router,
    token_expert_index,
    expert_gate_up_weight,
    expert_down_weight,
):
    lines, los, exs = sizes["line"], sizes["lo"], sizes["ex"]
    tok_rows, width = residual_input.shape
    num_experts = router.shape[1]
    line, lo, ex, core = (lax.axis_index(n) for n in ("line", "lo", "ex", "core"))

    down_rows = expert_down_weight.shape[1]
    cols = expert_down_weight.shape[2]
    slots, rank, _ = adapter_down_maps.shape
    shares = los if slots % los == 0 else 1
    share = slots // shares
    ex_far, lo_far = range(1, exs), range(1, los)

    ids = token_expert_index.T.astype(jnp.bfloat16)
    ids = jnp.pad(ids, ((0, EXTRA - ids.shape[0]), (0, width - tok_rows)))
    block = jnp.concatenate([residual_input, ids])
    maps = [m.reshape(slots * rank, width) for m in (adapter_down_maps, adapter_up_maps)]
    first = lo * share * rank if shares > 1 else 0
    sent = lax.dynamic_slice_in_dim(jnp.stack(maps), first, share * rank, axis=1)
    crossed = [from_offset(sent, "ex", exs, i) for i in ex_far]
    gate, up = expert_gate_up_weight[0, 0].T, expert_gate_up_weight[0, 1].T
    ups = {(0, j): from_offset(up, "lo", los, j) for j in lo_far}
    tokens = [across(block, lines, m) for m in range(lines) if m < 3]
    other_maps = [from_offset(m, "core", CORES, 1) for m in maps]

    ends = jnp.cumsum(prompt_token_length)
    adapter_ids = jnp.arange(adapter_table_row.shape[0], dtype=jnp.int32)
    named = prompt_adapter_index[:, None] == adapter_ids[None, :]
    prompt_row = jnp.sum(jnp.where(named, adapter_table_row[None, :], 0), axis=1)
    prompts = jnp.stack([ends - prompt_token_length, ends, prompt_row])
    router_rows = jnp.pad(router.T, ((0, LANES - num_experts), (0, 0)))
    offsets = line ^ jnp.arange(lines, dtype=jnp.int32)
    bases = (((offsets * los + lo) * exs + ex) * CORES + core) * tok_rows
    number = jnp.arange(slots * rank, dtype=jnp.int32) // rank
    owners = [(ex * CORES + core) * slots + number]
    for i in ex_far:
        for j in range(shares):
            start = ((ex + i) % exs * CORES + core) * slots + (lo + j) % los * share
            owners.append(start + number[: share * rank])
    owner = jnp.concatenate(owners)
    owner = jnp.concatenate([owner, owner + jnp.where(core == 0, slots, -slots)])[None, :]
    small = [bases, prompts, owner, adapter_norm_gain[None], expert_norm_gain[None], router_rows]

    gate, up, small, crossed, ups, tokens = together(gate, up, small, crossed, ups, tokens)
    passed = [from_offset(c, "lo", los, j) for c in crossed for j in range(shares)]
    gates = {(i, 0): from_offset(gate, "ex", exs, i) for i in ex_far}
    if lines == 4:
        tokens = tokens + [across(tokens[2], lines, 1)]

    gate, up, down, passed, gates, tokens = together(gate, up, expert_down_weight, passed, gates, tokens)
    held = [[jnp.concatenate([p[m] for p in passed[i * shares : (i + 1) * shares]]) for m in range(2)] for i in range(exs - 1)]
    held_other = [[from_offset(m, "core", CORES, 1) for m in h] for h in held]
    gates.update({(0, j): from_offset(gate, "lo", los, j) for j in lo_far})
    ups.update({(i, 0): from_offset(up, "ex", exs, i) for i in ex_far})
    down = lax.all_to_all(
        down.reshape(lines, down_rows // lines, cols), "line", split_axis=0, concat_axis=2, tiled=True
    ).reshape(down_rows // lines, lines * cols)
    tables = [m for pair in [maps] + held + [other_maps] + held_other for m in pair]
    mixed, w_own, x_own = front(*small, tables, tokens)

    x_own, w_own, gates, ups, gate, up, down = together(x_own, w_own, gates, ups, gate, up, down)
    gates[0, 0], ups[0, 0] = gate, up
    for i in ex_far:
        for j in lo_far:
            gates[i, j] = from_offset(gates[i, 0], "lo", los, j)
            ups[i, j] = from_offset(ups[0, j], "ex", exs, i)
    x_far = [from_offset(v, "core", CORES, 1) for v in x_own]
    w_far = from_offset(w_own, "core", CORES, 1)
    column = jnp.arange(LANES, dtype=jnp.int32)[None, :]

    def act(i, x, w):
        expert = (ex + i) % exs * CORES + core
        scale = jnp.sum(jnp.where(column == expert, w, 0.0), axis=1, keepdims=True)
        gate, up = (jnp.concatenate([of[i, j] for j in range(los)]) for of in (gates, ups))
        return hidden(jnp.concatenate(x), scale, gate, up)

    near, far = [act(0, x_own, w_own)], [act(0, x_far, w_far)]

    x_own, w_own, x_far, w_far, near, far, gates, ups, down = together(
        x_own, w_own, x_far, w_far, near, far, gates, ups, down
    )
    downs = {(i, 0): from_offset(down, "ex", exs, i) for i in range(exs)}
    downs.update({(0, j): from_offset(down, "lo", los, j) for j in lo_far})
    far += [act(i, x_far, w_far) for i in ex_far]
    near += [act(i, x_own, w_own) for i in ex_far]

    def in_order(piece):
        rows = piece.reshape(los, -1, piece.shape[1])
        picked = []
        for j in range(los):
            value = rows[0]
            for a in range(1, los):
                value = jnp.where((lo + j) % los == a, rows[a], value)
            picked.append(value)
        return jnp.concatenate(picked)

    near, far, downs = together(near, far, downs)
    for i in ex_far:
        for j in lo_far:
            if exs == los == 2:
                half = down.shape[0] // 2
                upper = from_offset(downs[i, 0][:half], "lo", los, j)
                lower = from_offset(downs[0, j][half:], "ex", exs, i)
                downs[i, j] = jnp.concatenate([upper, lower])
            else:
                downs[i, j] = from_offset(downs[i, 0], "lo", los, j)
    parts = []
    for j in range(los):
        pieces = [in_order(downs[i, j]) for i in range(exs)]
        project = lambda acts: sum(dot(a, d) for a, d in zip(acts, pieces))
        sent = project(far).astype(jnp.bfloat16).reshape(lines, tok_rows, -1)
        added = jnp.concatenate([from_offset(sent[k], "core", CORES, 1) for k in range(lines)])
        total = (project(near) + added.astype(jnp.float32)).astype(jnp.bfloat16)
        home = list(total.reshape(lines, tok_rows, -1))
        if lines == 4:
            joined = home[2].astype(jnp.float32) + across(home.pop(), lines, 1).astype(jnp.float32)
            home[2] = joined.astype(jnp.bfloat16)
        parts.append([across(home[m], lines, m) for m in range(len(home))])
    return final(lines, lo[None], mixed, parts)


def solution(mesh):
    dp, expert = mesh.shape["dp"], mesh.shape["expert"]
    lines = 4 if dp % 4 == 0 else 2 if dp % 2 == 0 else 1
    sizes = {"line": lines, "lo": dp // lines, "ex": expert // CORES, "core": CORES}
    inner = Mesh(mesh.devices.reshape(tuple(sizes.values())), tuple(sizes))
    rows = P(("line", "lo", "ex", "core"), None)
    slots = P(("ex", "core"), None, None)
    placed = (
        rows,
        P(),
        P(),
        P(),
        P(),
        slots,
        slots,
        P(),
        P(),
        rows,
        P(("ex", "core"), None, None, ("line", "lo")),
        P(("ex", "core"), None, ("line", "lo")),
    )

    def body(*arrays):
        return on_device(sizes, *arrays)

    return jax.shard_map(body, mesh=inner, in_specs=placed, out_specs=rows, check_vma=False)
```

profile of v0, /device:TPU:0, one launch (start us, length us, event | category | flops | bytes accessed | tf_op | source)
XLA Modules:
  0.0 172.1 jit_solution(1399414343391201780)
XLA Ops:
  1.8 3.1 %collective-permute-start.2 = (bf16[272,1024]{1,0:T(8,128)(2,1)S(1)}, bf16[272,1024]{1,0:T(8,128)(2,1)}, u32[]{:S(2)}, u32[]{:S(2)}) collective-permute-start(bf16[272,1024]{1,0:T(8,128)(2,1)S(1)} %fusion.41.refs_8_), channel_id=1, source_target_pairs={{8,0},{0,8},{24,16},{16,24},{9,1},{1,9},{25,17},{17,25},{10,2},{2,... | collective-permute-start | bytes 1671176 | tf_op jit(solution)/shard_map/ppermute | solution.py:28
  4.9 2.6 %collective-permute-start.3 = (bf16[272,1024]{1,0:T(8,128)(2,1)S(1)}, bf16[272,1024]{1,0:T(8,128)(2,1)}, u32[]{:S(2)}, u32[]{:S(2)}) collective-permute-start(bf16[272,1024]{1,0:T(8,128)(2,1)S(1)} %fusion.41.refs_8_), channel_id=1, source_target_pairs={{16,0},{24,8},{0,16},{8,24},{17,1},{25,9},{1,17},{9,25},{18,2},{26... | collective-permute-start | bytes 1671176 | tf_op jit(solution)/shard_map/ppermute | solution.py:28
  7.5 2.0 %fusion.42 = bf16[2,128,1024]{2,1,0:T(8,128)(2,1)} fusion(s32[]{:T(128)S(6)} %select_n.120, bf16[1,256,1024]{2,1,0:T(8,128)(2,1)} %bitcast.68, bf16[1,256,1024]{2,1,0:T(8,128)(2,1)} %bitcast.71), kind=kLoop, calls=%fused_computation.60 | loop fusion | flops 1048576 | bytes 1572868 | tf_op jit(solution)/shard_map/stack | solution.py:171
  11.1 1.6 collective-permute-start.1
  16.9 6.0 %collective-permute-done = bf16[2,128,1024]{2,1,0:T(8,128)(2,1)} collective-permute-done((bf16[2,128,1024]{2,1,0:T(8,128)(2,1)}, bf16[2,128,1024]{2,1,0:T(8,128)(2,1)}, u32[]{:S(2)}, u32[]{:S(2)}) %collective-permute-start) | collective-permute-done | bytes 524320 | tf_op jit(solution)/shard_map/ppermute | solution.py:20
  22.9 6.5 %collective-permute-done.2.refs_9_ = bf16[272,1024]{1,0:T(8,128)(2,1)} collective-permute-done((bf16[272,1024]{1,0:T(8,128)(2,1)S(1)}, bf16[272,1024]{1,0:T(8,128)(2,1)}, u32[]{:S(2)}, u32[]{:S(2)}) %collective-permute-start.2) | collective-permute-done | bytes 557088 | tf_op jit(solution)/shard_map/ppermute | solution.py:28
  29.4 2.5 %collective-permute-done.3.refs_10_ = bf16[272,1024]{1,0:T(8,128)(2,1)} collective-permute-done((bf16[272,1024]{1,0:T(8,128)(2,1)S(1)}, bf16[272,1024]{1,0:T(8,128)(2,1)}, u32[]{:S(2)}, u32[]{:S(2)}) %collective-permute-start.3) | collective-permute-done | bytes 557088 | tf_op jit(solution)/shard_map/ppermute | solution.py:28
  33.9 1.5 collective-permute-start.4
  35.4 10.9 %collective-permute-done.4 = bf16[2,128,1024]{2,1,0:T(8,128)(2,1)S(1)} collective-permute-done((bf16[2,128,1024]{2,1,0:T(8,128)(2,1)}, bf16[2,128,1024]{2,1,0:T(8,128)(2,1)S(1)}, u32[]{:S(2)}, u32[]{:S(2)}) %collective-permute-start.4) | collective-permute-done | bytes 524320 | tf_op jit(solution)/shard_map/ppermute | solution.py:20
  48.2 3.5 %all-to-all-start = ((bf16[4,704,128]{2,1,0:T(8,128)(2,1)}), bf16[4,704,128]{2,1,0:T(8,128)(2,1)S(1)}, u32[]{:S(2)}, u32[]{:S(2)}) async-start(bf16[4,704,128]{2,1,0:T(8,128)(2,1)} %bitcast.74), calls=%async_computation | async-start | bytes 1441792 | tf_op jit(solution)/shard_map/all_to_all | solution.py:207
  59.4 1.6 collective-permute-done.10.refs_7_
  61.8 12.6 %front.1 = (bf16[256,1024]{1,0:T(8,128)(2,1)}, f32[1024,128]{1,0:T(8,128)}, bf16[256,1024]{1,0:T(8,128)(2,1)}, bf16[256,1024]{1,0:T(8,128)(2,1)}, bf16[256,1024]{1,0:T(8,128)(2,1)}, /*index=5*/bf16[256,1024]{1,0:T(8,128)(2,1)}) custom-call(s32[4]{0:T(128)} %add_multiply_fusion.base_ref, s32[3,48]{1,0:T(4,128)} %pad_add_fusion.1.prompts_ref, ...), custom_call_target="tpu_custom_call" | custom-call | flops 1 | bytes 1 | tf_op jit(solution)/shard_map/front/pallas_call | solution.py:86
  78.5 1.7 fusion.62
  83.4 2.5 %fusion.9 = bf16[1024,704]{0,1:T(8,128)(2,1)S(1)} fusion(f32[1024,704]{0,1:T(8,128)S(1)} %fusion.62, bf16[1024,1024]{1,0:T(8,128)(2,1)S(1)} %constant_dynamic-update-slice_fusion, bf16[704,1024]{1,0:T(8,128)(2,1)S(1)} %constant_dynamic-update-slice_fusion.6, f32[1024]{0:T(1024)S(1)} %get-tuple-element.138), kind=kOutput, calls=%fused_computation.13 | convolution fusion | flops 1484324864 | bytes 7868416 | tf_op jit(solution)/shard_map/dot_general | solution.py:32
  85.9 1.7 fusion.63
  87.6 2.3 %fusion.19 = bf16[1024,704]{0,1:T(8,128)(2,1)S(1)} fusion(f32[1024,704]{0,1:T(8,128)S(1)} %fusion.63, f32[1024]{0:T(1024)S(1)} %get-tuple-element.137, bf16[1024,1024]{1,0:T(8,128)(2,1)S(1)} %constant_dynamic-update-slice_fusion.8, bf16[704,1024]{1,0:T(8,128)(2,1)S(1)} %constant_dynamic-update-slice_fusion.6), kind=kOutput, calls=%fused_computation.23 | convolution fusion | flops 1484324864 | bytes 7868416 | tf_op jit(solution)/shard_map/dot_general | solution.py:32
  89.9 10.4 %collective-permute-done.18 = bf16[352,1024]{1,0:T(8,128)(2,1)S(1)} collective-permute-done((bf16[352,1024]{1,0:T(8,128)(2,1)S(1)}, bf16[352,1024]{1,0:T(8,128)(2,1)S(1)}, u32[]{:S(2)}, u32[]{:S(2)}) %collective-permute-start.18) | collective-permute-done | bytes 720928 | tf_op jit(solution)/shard_map/ppermute | solution.py:20
  103.6 1.7 fusion.64
  105.8 2.3 %fusion.29 = bf16[1024,704]{0,1:T(8,128)(2,1)S(1)} fusion(f32[1024,704]{0,1:T(8,128)S(1)} %fusion.64, bf16[1024,1024]{1,0:T(8,128)(2,1)S(1)} %constant_dynamic-update-slice_fusion.12, bf16[704,1024]{1,0:T(8,128)(2,1)S(1)} %constant_dynamic-update-slice_fusion.18, f32[1024]{0:T(1024)S(1)} %get-tuple-element.136), kind=kOutput, calls=%fused_computation.33 | convolution fusion | flops 1484324864 | bytes 7868416 | tf_op jit(solution)/shard_map/dot_general | solution.py:32
  108.1 1.7 fusion.65
  109.8 2.5 %fusion.39 = bf16[1024,704]{0,1:T(8,128)(2,1)S(1)} fusion(f32[1024,704]{0,1:T(8,128)S(1)} %fusion.65, bf16[1024,1024]{1,0:T(8,128)(2,1)S(1)} %constant_dynamic-update-slice_fusion.20, bf16[704,1024]{1,0:T(8,128)(2,1)S(1)} %constant_dynamic-update-slice_fusion.18, f32[1024]{0:T(1024)S(1)} %get-tuple-element.135), kind=kOutput, calls=%fused_computation.43 | convolution fusion | flops 1484324864 | bytes 7868416 | tf_op jit(solution)/shard_map/dot_general | solution.py:32
  112.3 5.1 %collective-permute-done.20 = bf16[704,512]{1,0:T(8,128)(2,1)S(1)} collective-permute-done((bf16[704,512]{1,0:T(8,128)(2,1)S(1)}, bf16[704,512]{1,0:T(8,128)(2,1)S(1)}, u32[]{:S(2)}, u32[]{:S(2)}) %collective-permute-start.20) | collective-permute-done | bytes 720928 | tf_op jit(solution)/shard_map/ppermute | solution.py:20
  123.3 1.6 collective-permute-start.30
  126.0 2.4 %collective-permute-start.27 = (bf16[256,512]{1,0:T(8,128)(2,1)S(1)}, bf16[256,512]{1,0:T(8,128)(2,1)S(1)}, u32[]{:S(2)}, u32[]{:S(2)}) collective-permute-start(bf16[256,512]{1,0:T(8,128)(2,1)S(1)} %get-tuple-element.148), channel_id=1, source_target_pairs={{8,0},{0,8},{24,16},{16,24},{9,1},{1,9},{25,17},{17,25},{10,2},{2,... | collective-permute-start | bytes 786440 | tf_op jit(solution)/shard_map/ppermute | solution.py:28
  128.4 3.1 %collective-permute-done.29 = bf16[352,512]{1,0:T(8,128)(2,1)S(1)} collective-permute-done((bf16[352,512]{1,0:T(8,128)(2,1)S(1)}, bf16[352,512]{1,0:T(8,128)(2,1)S(1)}, u32[]{:S(2)}, u32[]{:S(2)}) %collective-permute-start.29) | collective-permute-done | bytes 360480 | tf_op jit(solution)/shard_map/ppermute | solution.py:20
  131.5 2.0 %collective-permute-done.30 = bf16[352,512]{1,0:T(8,128)(2,1)S(1)} collective-permute-done((bf16[352,512]{1,0:T(8,128)(2,1)S(1)}, bf16[352,512]{1,0:T(8,128)(2,1)S(1)}, u32[]{:S(2)}, u32[]{:S(2)}) %collective-permute-start.30) | collective-permute-done | bytes 360480 | tf_op jit(solution)/shard_map/ppermute | solution.py:20
  139.5 2.4 %collective-permute-start.36 = (bf16[256,512]{1,0:T(8,128)(2,1)S(1)}, bf16[256,512]{1,0:T(8,128)(2,1)S(1)}, u32[]{:S(2)}, u32[]{:S(2)}) collective-permute-start(bf16[256,512]{1,0:T(8,128)(2,1)S(1)} %get-tuple-element.141), channel_id=1, source_target_pairs={{8,0},{0,8},{24,16},{16,24},{9,1},{1,9},{25,17},{17,25},{10,2},{2,... | collective-permute-start | bytes 786440 | tf_op jit(solution)/shard_map/ppermute | solution.py:28
  142.0 2.6 %collective-permute-start.28 = (bf16[256,512]{1,0:T(8,128)(2,1)S(1)}, bf16[256,512]{1,0:T(8,128)(2,1)S(1)}, u32[]{:S(2)}, u32[]{:S(2)}) collective-permute-start(bf16[256,512]{1,0:T(8,128)(2,1)S(1)} %add_convert_fusion.5), channel_id=1, source_target_pairs={{16,0},{24,8},{0,16},{8,24},{17,1},{25,9},{1,17},{9,25},{18,2},{26... | collective-permute-start | bytes 786440 | tf_op jit(solution)/shard_map/ppermute | solution.py:28
  146.1 8.4 %collective-permute-done.36 = bf16[256,512]{1,0:T(8,128)(2,1)S(1)} collective-permute-done((bf16[256,512]{1,0:T(8,128)(2,1)S(1)}, bf16[256,512]{1,0:T(8,128)(2,1)S(1)}, u32[]{:S(2)}, u32[]{:S(2)}) %collective-permute-start.36) | collective-permute-done | bytes 262176 | tf_op jit(solution)/shard_map/ppermute | solution.py:28
  154.6 1.8 %collective-permute-start.37 = (bf16[256,512]{1,0:T(8,128)(2,1)S(1)}, bf16[256,512]{1,0:T(8,128)(2,1)S(1)}, u32[]{:S(2)}, u32[]{:S(2)}) collective-permute-start(bf16[256,512]{1,0:T(8,128)(2,1)S(1)} %add_convert_fusion.4), channel_id=1, source_target_pairs={{16,0},{24,8},{0,16},{8,24},{17,1},{25,9},{1,17},{9,25},{18,2},{26... | collective-permute-start | bytes 786440 | tf_op jit(solution)/shard_map/ppermute | solution.py:28
  156.4 3.9 %collective-permute-done.26.refs_1_ = bf16[256,512]{1,0:T(8,128)(2,1)S(1)} collective-permute-done((bf16[256,512]{1,0:T(8,128)(2,1)S(1)}, bf16[256,512]{1,0:T(8,128)(2,1)S(1)}, u32[]{:S(2)}, u32[]{:S(2)}) %collective-permute-start.26) | collective-permute-done | bytes 262176 | tf_op jit(solution)/shard_map/ppermute | solution.py:28
  160.3 10.6 %collective-permute-done.35.refs_4_ = bf16[256,512]{1,0:T(8,128)(2,1)S(1)} collective-permute-done((bf16[256,512]{1,0:T(8,128)(2,1)S(1)}, bf16[256,512]{1,0:T(8,128)(2,1)S(1)}, u32[]{:S(2)}, u32[]{:S(2)}) %collective-permute-start.35) | collective-permute-done | bytes 262176 | tf_op jit(solution)/shard_map/ppermute | solution.py:28
  (170 shorter events, 46.3 us)
Async XLA Ops:
  1.8 27.6 %collective-permute-start.2 = (bf16[272,1024]{1,0:T(8,128)(2,1)S(1)}, bf16[272,1024]{1,0:T(8,128)(2,1)}, u32[]{:S(2)}, u32[]{:S(2)}) collective-permute-start(bf16[272,1024]{1,0:T(8,128)(2,1)S(1)} %fusion.41.refs_8_), channel_id=1, source_target_pairs={{8,0},{0,8},{24,16},{16,24},{9,1},{1,9},{25,17},{17,25},{10,2},{2,... | collective-permute-start | bytes 1671176 | tf_op jit(solution)/shard_map/ppermute | solution.py:28
  4.9 27.1 %collective-permute-start.3 = (bf16[272,1024]{1,0:T(8,128)(2,1)S(1)}, bf16[272,1024]{1,0:T(8,128)(2,1)}, u32[]{:S(2)}, u32[]{:S(2)}) collective-permute-start(bf16[272,1024]{1,0:T(8,128)(2,1)S(1)} %fusion.41.refs_8_), channel_id=1, source_target_pairs={{16,0},{24,8},{0,16},{8,24},{17,1},{25,9},{1,17},{9,25},{18,2},{26... | collective-permute-start | bytes 1671176 | tf_op jit(solution)/shard_map/ppermute | solution.py:28
  9.5 13.4 %collective-permute-start = (bf16[2,128,1024]{2,1,0:T(8,128)(2,1)}, bf16[2,128,1024]{2,1,0:T(8,128)(2,1)}, u32[]{:S(2)}, u32[]{:S(2)}) collective-permute-start(bf16[2,128,1024]{2,1,0:T(8,128)(2,1)} %fusion.42), channel_id=1, source_target_pairs={{2,0},{0,2},{3,1},{1,3},{6,4},{4,6},{7,5},{5,7},{10,8},{8,10},{11,... | collective-permute-start | bytes 1572872 | tf_op jit(solution)/shard_map/ppermute | solution.py:20
  11.1 20.9 %collective-permute-start.1 = (bf16[352,1024]{1,0:T(8,128)(2,1)S(1)}, bf16[352,1024]{1,0:T(8,128)(2,1)}, u32[]{:S(2)}, u32[]{:S(2)}) collective-permute-start(bf16[352,1024]{1,0:T(8,128)(2,1)S(1)} %get-tuple-element.106), channel_id=1, source_target_pairs={{4,0},{0,4},{5,1},{1,5},{6,2},{2,6},{7,3},{3,7},{12,8},{8,12},{13,... | collective-permute-start | bytes 2162696 | tf_op jit(solution)/shard_map/ppermute | solution.py:20
  31.9 14.8 %collective-permute-start.5 = (bf16[352,1024]{1,0:T(8,128)(2,1)S(1)}, bf16[352,1024]{1,0:T(8,128)(2,1)S(1)}, u32[]{:S(2)}, u32[]{:S(2)}) collective-permute-start(bf16[352,1024]{1,0:T(8,128)(2,1)S(1)} %get-tuple-element.104), channel_id=1, source_target_pairs={{2,0},{0,2},{3,1},{1,3},{6,4},{4,6},{7,5},{5,7},{10,8},{8,10},{11,... | collective-permute-start | bytes 2162696 | tf_op jit(solution)/shard_map/ppermute | solution.py:20
  33.4 12.8 %collective-permute-start.6 = (bf16[272,1024]{1,0:T(8,128)(2,1)}, bf16[272,1024]{1,0:T(8,128)(2,1)S(1)}, u32[]{:S(2)}, u32[]{:S(2)}) collective-permute-start(bf16[272,1024]{1,0:T(8,128)(2,1)} %collective-permute-done.3.refs_10_), channel_id=1, source_target_pairs={{8,0},{0,8},{24,16},{16,24},{9,1},{1,9},{25,17},{17,25},{10,2},{2,... | collective-permute-start | bytes 1671176 | tf_op jit(solution)/shard_map/ppermute | solution.py:28
  33.9 12.4 %collective-permute-start.4 = (bf16[2,128,1024]{2,1,0:T(8,128)(2,1)}, bf16[2,128,1024]{2,1,0:T(8,128)(2,1)S(1)}, u32[]{:S(2)}, u32[]{:S(2)}) collective-permute-start(bf16[2,128,1024]{2,1,0:T(8,128)(2,1)} %collective-permute-done), channel_id=1, source_target_pairs={{4,0},{0,4},{5,1},{1,5},{6,2},{2,6},{7,3},{3,7},{12,8},{8,12},{13,... | collective-permute-start | bytes 1572872 | tf_op jit(solution)/shard_map/ppermute | solution.py:20
  48.2 26.3 %all-to-all-start = ((bf16[4,704,128]{2,1,0:T(8,128)(2,1)}), bf16[4,704,128]{2,1,0:T(8,128)(2,1)S(1)}, u32[]{:S(2)}, u32[]{:S(2)}) async-start(bf16[4,704,128]{2,1,0:T(8,128)(2,1)} %bitcast.74), calls=%async_computation | async-start | bytes 1441792 | tf_op jit(solution)/shard_map/all_to_all | solution.py:207
  51.7 6.3 %collective-permute-start.7 = (bf16[256,1024]{1,0:T(8,128)(2,1)S(1)}, bf16[256,1024]{1,0:T(8,128)(2,1)S(1)}, u32[]{:S(2)}, u32[]{:S(2)}) collective-permute-start(bf16[256,1024]{1,0:T(8,128)(2,1)S(1)} %bitcast.70), channel_id=1, source_target_pairs={{1,0},{0,1},{3,2},{2,3},{5,4},{4,5},{7,6},{6,7},{9,8},{8,9},{11,10... | collective-permute-start | bytes 1572872 | tf_op jit(solution)/shard_map/ppermute | solution.py:20
  51.8 7.5 %collective-permute-start.8 = (bf16[256,1024]{1,0:T(8,128)(2,1)S(1)}, bf16[256,1024]{1,0:T(8,128)(2,1)}, u32[]{:S(2)}, u32[]{:S(2)}) collective-permute-start(bf16[256,1024]{1,0:T(8,128)(2,1)S(1)} %bitcast.73), channel_id=1, source_target_pairs={{1,0},{0,1},{3,2},{2,3},{5,4},{4,5},{7,6},{6,7},{9,8},{8,9},{11,10... | collective-permute-start | bytes 1572872 | tf_op jit(solution)/shard_map/ppermute | solution.py:20
  52.2 23.0 %collective-permute-start.11 = (bf16[352,1024]{1,0:T(8,128)(2,1)S(1)}, bf16[352,1024]{1,0:T(8,128)(2,1)}, u32[]{:S(2)}, u32[]{:S(2)}) collective-permute-start(bf16[352,1024]{1,0:T(8,128)(2,1)S(1)} %get-tuple-element.104), channel_id=1, source_target_pairs={{4,0},{0,4},{5,1},{1,5},{6,2},{2,6},{7,3},{3,7},{12,8},{8,12},{13,... | collective-permute-start | bytes 2162696 | tf_op jit(solution)/shard_map/ppermute | solution.py:20
  53.8 21.5 %collective-permute-start.12 = (bf16[352,1024]{1,0:T(8,128)(2,1)S(1)}, bf16[352,1024]{1,0:T(8,128)(2,1)}, u32[]{:S(2)}, u32[]{:S(2)}) collective-permute-start(bf16[352,1024]{1,0:T(8,128)(2,1)S(1)} %get-tuple-element.106), channel_id=1, source_target_pairs={{2,0},{0,2},{3,1},{1,3},{6,4},{4,6},{7,5},{5,7},{10,8},{8,10},{11,... | collective-permute-start | bytes 2162696 | tf_op jit(solution)/shard_map/ppermute | solution.py:20
  75.6 5.8 %collective-permute-start.13 = (bf16[256,1024]{1,0:T(8,128)(2,1)S(1)}, bf16[256,1024]{1,0:T(8,128)(2,1)S(1)}, u32[]{:S(2)}, u32[]{:S(2)}) collective-permute-start(bf16[256,1024]{1,0:T(8,128)(2,1)S(1)} %copy-done.7), channel_id=1, source_target_pairs={{1,0},{0,1},{3,2},{2,3},{5,4},{4,5},{7,6},{6,7},{9,8},{8,9},{11,10... | collective-permute-start | bytes 1572872 | tf_op jit(solution)/shard_map/ppermute | solution.py:20
  76.0 6.3 %collective-permute-start.14 = (bf16[256,1024]{1,0:T(8,128)(2,1)S(1)}, bf16[256,1024]{1,0:T(8,128)(2,1)S(1)}, u32[]{:S(2)}, u32[]{:S(2)}) collective-permute-start(bf16[256,1024]{1,0:T(8,128)(2,1)S(1)} %copy-done.6), channel_id=1, source_target_pairs={{1,0},{0,1},{3,2},{2,3},{5,4},{4,5},{7,6},{6,7},{9,8},{8,9},{11,10... | collective-permute-start | bytes 1572872 | tf_op jit(solution)/shard_map/ppermute | solution.py:20
  76.2 7.1 %collective-permute-start.15 = (bf16[256,1024]{1,0:T(8,128)(2,1)S(1)}, bf16[256,1024]{1,0:T(8,128)(2,1)S(1)}, u32[]{:S(2)}, u32[]{:S(2)}) collective-permute-start(bf16[256,1024]{1,0:T(8,128)(2,1)S(1)} %copy-done.5), channel_id=1, source_target_pairs={{1,0},{0,1},{3,2},{2,3},{5,4},{4,5},{7,6},{6,7},{9,8},{8,9},{11,10... | collective-permute-start | bytes 1572872 | tf_op jit(solution)/shard_map/ppermute | solution.py:20
  76.6 9.2 %collective-permute-start.16 = (bf16[256,1024]{1,0:T(8,128)(2,1)S(1)}, bf16[256,1024]{1,0:T(8,128)(2,1)S(1)}, u32[]{:S(2)}, u32[]{:S(2)}) collective-permute-start(bf16[256,1024]{1,0:T(8,128)(2,1)S(1)} %copy-done.4), channel_id=1, source_target_pairs={{1,0},{0,1},{3,2},{2,3},{5,4},{4,5},{7,6},{6,7},{9,8},{8,9},{11,10... | collective-permute-start | bytes 1572872 | tf_op jit(solution)/shard_map/ppermute | solution.py:20
  76.8 6.2 %collective-permute-start.17 = (f32[1024,128]{1,0:T(8,128)S(1)}, f32[1024,128]{1,0:T(8,128)S(1)}, u32[]{:S(2)}, u32[]{:S(2)}) collective-permute-start(f32[1024,128]{1,0:T(8,128)S(1)} %copy-done.8), channel_id=1, source_target_pairs={{1,0},{0,1},{3,2},{2,3},{5,4},{4,5},{7,6},{6,7},{9,8},{8,9},{11,10... | collective-permute-start | bytes 1572872 | tf_op jit(solution)/shard_map/ppermute | solution.py:20
  81.5 18.9 %collective-permute-start.19 = (bf16[352,1024]{1,0:T(8,128)(2,1)}, bf16[352,1024]{1,0:T(8,128)(2,1)S(1)}, u32[]{:S(2)}, u32[]{:S(2)}) collective-permute-start(bf16[352,1024]{1,0:T(8,128)(2,1)} %collective-permute-done.1), channel_id=1, source_target_pairs={{2,0},{0,2},{3,1},{1,3},{6,4},{4,6},{7,5},{5,7},{10,8},{8,10},{11,... | collective-permute-start | bytes 2162696 | tf_op jit(solution)/shard_map/ppermute | solution.py:20
  82.4 18.0 %collective-permute-start.18 = (bf16[352,1024]{1,0:T(8,128)(2,1)S(1)}, bf16[352,1024]{1,0:T(8,128)(2,1)S(1)}, u32[]{:S(2)}, u32[]{:S(2)}) collective-permute-start(bf16[352,1024]{1,0:T(8,128)(2,1)S(1)} %copy-done.11), channel_id=1, source_target_pairs={{4,0},{0,4},{5,1},{1,5},{6,2},{2,6},{7,3},{3,7},{12,8},{8,12},{13,... | collective-permute-start | bytes 2162696 | tf_op jit(solution)/shard_map/ppermute | solution.py:20
  100.3 17.0 %collective-permute-start.20 = (bf16[704,512]{1,0:T(8,128)(2,1)S(1)}, bf16[704,512]{1,0:T(8,128)(2,1)S(1)}, u32[]{:S(2)}, u32[]{:S(2)}) collective-permute-start(bf16[704,512]{1,0:T(8,128)(2,1)S(1)} %bitcast.63), channel_id=1, source_target_pairs={{4,0},{0,4},{5,1},{1,5},{6,2},{2,6},{7,3},{3,7},{12,8},{8,12},{13,... | collective-permute-start | bytes 2162696 | tf_op jit(solution)/shard_map/ppermute | solution.py:20
  100.8 16.8 %collective-permute-start.21 = (bf16[704,512]{1,0:T(8,128)(2,1)S(1)}, bf16[704,512]{1,0:T(8,128)(2,1)S(1)}, u32[]{:S(2)}, u32[]{:S(2)}) collective-permute-start(bf16[704,512]{1,0:T(8,128)(2,1)S(1)} %bitcast.64), channel_id=1, source_target_pairs={{2,0},{0,2},{3,1},{1,3},{6,4},{4,6},{7,5},{5,7},{10,8},{8,10},{11,... | collective-permute-start | bytes 2162696 | tf_op jit(solution)/shard_map/ppermute | solution.py:20
  119.9 5.0 %collective-permute-start.24 = (bf16[256,512]{1,0:T(8,128)(2,1)S(1)}, bf16[256,512]{1,0:T(8,128)(2,1)S(1)}, u32[]{:S(2)}, u32[]{:S(2)}) collective-permute-start(bf16[256,512]{1,0:T(8,128)(2,1)S(1)} %get-tuple-element.153), channel_id=1, source_target_pairs={{1,0},{0,1},{3,2},{2,3},{5,4},{4,5},{7,6},{6,7},{9,8},{8,9},{11,10... | collective-permute-start | bytes 786440 | tf_op jit(solution)/shard_map/ppermute | solution.py:20
  120.4 4.5 %collective-permute-start.23 = (bf16[256,512]{1,0:T(8,128)(2,1)S(1)}, bf16[256,512]{1,0:T(8,128)(2,1)S(1)}, u32[]{:S(2)}, u32[]{:S(2)}) collective-permute-start(bf16[256,512]{1,0:T(8,128)(2,1)S(1)} %get-tuple-element.154), channel_id=1, source_target_pairs={{1,0},{0,1},{3,2},{2,3},{5,4},{4,5},{7,6},{6,7},{9,8},{8,9},{11,10... | collective-permute-start | bytes 786440 | tf_op jit(solution)/shard_map/ppermute | solution.py:20
  120.5 4.4 %collective-permute-start.22 = (bf16[256,512]{1,0:T(8,128)(2,1)S(1)}, bf16[256,512]{1,0:T(8,128)(2,1)S(1)}, u32[]{:S(2)}, u32[]{:S(2)}) collective-permute-start(bf16[256,512]{1,0:T(8,128)(2,1)S(1)} %get-tuple-element.151), channel_id=1, source_target_pairs={{1,0},{0,1},{3,2},{2,3},{5,4},{4,5},{7,6},{6,7},{9,8},{8,9},{11,10... | collective-permute-start | bytes 786440 | tf_op jit(solution)/shard_map/ppermute | solution.py:20
  121.0 10.5 %collective-permute-start.29 = (bf16[352,512]{1,0:T(8,128)(2,1)S(1)}, bf16[352,512]{1,0:T(8,128)(2,1)S(1)}, u32[]{:S(2)}, u32[]{:S(2)}) collective-permute-start(bf16[352,512]{1,0:T(8,128)(2,1)S(1)} %get-tuple-element.157), channel_id=1, source_target_pairs={{2,0},{0,2},{3,1},{1,3},{6,4},{4,6},{7,5},{5,7},{10,8},{8,10},{11,... | collective-permute-start | bytes 1081352 | tf_op jit(solution)/shard_map/ppermute | solution.py:20
  123.3 10.2 %collective-permute-start.30 = (bf16[352,512]{1,0:T(8,128)(2,1)S(1)}, bf16[352,512]{1,0:T(8,128)(2,1)S(1)}, u32[]{:S(2)}, u32[]{:S(2)}) collective-permute-start(bf16[352,512]{1,0:T(8,128)(2,1)S(1)} %get-tuple-element.160), channel_id=1, source_target_pairs={{4,0},{0,4},{5,1},{1,5},{6,2},{2,6},{7,3},{3,7},{12,8},{8,12},{13,... | collective-permute-start | bytes 1081352 | tf_op jit(solution)/shard_map/ppermute | solution.py:20
  126.0 15.9 %collective-permute-start.27 = (bf16[256,512]{1,0:T(8,128)(2,1)S(1)}, bf16[256,512]{1,0:T(8,128)(2,1)S(1)}, u32[]{:S(2)}, u32[]{:S(2)}) collective-permute-start(bf16[256,512]{1,0:T(8,128)(2,1)S(1)} %get-tuple-element.148), channel_id=1, source_target_pairs={{8,0},{0,8},{24,16},{16,24},{9,1},{1,9},{25,17},{17,25},{10,2},{2,... | collective-permute-start | bytes 786440 | tf_op jit(solution)/shard_map/ppermute | solution.py:28
  139.5 15.1 %collective-permute-start.36 = (bf16[256,512]{1,0:T(8,128)(2,1)S(1)}, bf16[256,512]{1,0:T(8,128)(2,1)S(1)}, u32[]{:S(2)}, u32[]{:S(2)}) collective-permute-start(bf16[256,512]{1,0:T(8,128)(2,1)S(1)} %get-tuple-element.141), channel_id=1, source_target_pairs={{8,0},{0,8},{24,16},{16,24},{9,1},{1,9},{25,17},{17,25},{10,2},{2,... | collective-permute-start | bytes 786440 | tf_op jit(solution)/shard_map/ppermute | solution.py:28
  141.8 18.4 %collective-permute-start.26 = (bf16[256,512]{1,0:T(8,128)(2,1)S(1)}, bf16[256,512]{1,0:T(8,128)(2,1)S(1)}, u32[]{:S(2)}, u32[]{:S(2)}) collective-permute-start(bf16[256,512]{1,0:T(8,128)(2,1)S(1)} %get-tuple-element.149), channel_id=1, source_target_pairs={{8,0},{0,8},{24,16},{16,24},{9,1},{1,9},{25,17},{17,25},{10,2},{2,... | collective-permute-start | bytes 786440 | tf_op jit(solution)/shard_map/ppermute | solution.py:28
  142.0 18.3 %collective-permute-start.28 = (bf16[256,512]{1,0:T(8,128)(2,1)S(1)}, bf16[256,512]{1,0:T(8,128)(2,1)S(1)}, u32[]{:S(2)}, u32[]{:S(2)}) collective-permute-start(bf16[256,512]{1,0:T(8,128)(2,1)S(1)} %add_convert_fusion.5), channel_id=1, source_target_pairs={{16,0},{24,8},{0,16},{8,24},{17,1},{25,9},{1,17},{9,25},{18,2},{26... | collective-permute-start | bytes 786440 | tf_op jit(solution)/shard_map/ppermute | solution.py:28
  144.6 26.3 %collective-permute-start.35 = (bf16[256,512]{1,0:T(8,128)(2,1)S(1)}, bf16[256,512]{1,0:T(8,128)(2,1)S(1)}, u32[]{:S(2)}, u32[]{:S(2)}) collective-permute-start(bf16[256,512]{1,0:T(8,128)(2,1)S(1)} %get-tuple-element.142), channel_id=1, source_target_pairs={{8,0},{0,8},{24,16},{16,24},{9,1},{1,9},{25,17},{17,25},{10,2},{2,... | collective-permute-start | bytes 786440 | tf_op jit(solution)/shard_map/ppermute | solution.py:28
  154.6 16.3 %collective-permute-start.37 = (bf16[256,512]{1,0:T(8,128)(2,1)S(1)}, bf16[256,512]{1,0:T(8,128)(2,1)S(1)}, u32[]{:S(2)}, u32[]{:S(2)}) collective-permute-start(bf16[256,512]{1,0:T(8,128)(2,1)S(1)} %add_convert_fusion.4), channel_id=1, source_target_pairs={{16,0},{24,8},{0,16},{8,24},{17,1},{25,9},{1,17},{9,25},{18,2},{26... | collective-permute-start | bytes 786440 | tf_op jit(solution)/shard_map/ppermute | solution.py:28
  (29 other events, 195.4 us)
where the time goes:
time: 172 us
  waiting for transfers between devices  72.6 us (42%)
  starting transfers between devices  39.9 us (23%)
  matrix products  24.4 us (14%)
  Pallas kernels  13.8 us (8%)
  local copies, waits for them, and re-layouts  12.1 us (7%)
  other arithmetic  8.58 us (5%)
    ppermute x29, waiting for transfers between devices, from_offset(): lax.ppermute(value, axis, [((i + offset) % size, i) for i in range(size)])  40.5 us
    ppermute x9, waiting for transfers between devices, across(): lax.ppermute(value, 'line', [(i ^ mask, i) for i in range(size)])  32 us
    dot_general x16, matrix products, dot(): lax.dot_general(a, b, (((1,), (rhs_dim,)), ((), ())), preferred_element_t...  24.4 us
    ppermute x29, starting transfers between devices, from_offset(): lax.ppermute(value, axis, [((i + offset) % size, i) for i in range(size)])  19.6 us
    ppermute x9, starting transfers between devices, across(): lax.ppermute(value, 'line', [(i ^ mask, i) for i in range(size)])  16.8 us
    pallas_call x1, Pallas kernels, front(): pl.pallas_call(functools.partial(front_kernel, len(tables) // 2, blocks,...  12.6 us
    unnamed x61, local copies, waits for them, and re-layouts  5.34 us
    all_to_all x1, starting transfers between devices, on_device(): lax.all_to_all(down.reshape(lines, down_rows // lines, cols), 'line', spl...  3.49 us
  transfers between devices with their start and end apart: 39, of which 17 were waited for; matrix products, arithmetic and copies ran while one was open for 22% of the time, Pallas kernels for 7%

commit v1 on v0

v1 whole, which is shorter than its diff:
```python
import functools

import jax
import jax.numpy as jnp
from jax import lax
from jax.experimental import pallas as pl
from jax.experimental.pallas import tpu as pltpu
from jax.sharding import Mesh
from jax.sharding import PartitionSpec as P

CORES = 2
LANES = 128
EXTRA = 16
VMEM = 56 * 2**20


def from_offset(value, axis, size, offset):
    if offset % size == 0:
        return value
    return lax.ppermute(value, axis, [((i + offset) % size, i) for i in range(size)])


def together(*values):
    return lax.optimization_barrier(values)


def across(value, size, mask):
    return lax.ppermute(value, "line", [(i ^ mask, i) for i in range(size)]) if mask else value


def dot(a, b, rhs_dim=0):
    return lax.dot_general(a, b, (((1,), (rhs_dim,)), ((), ())), preferred_element_type=jnp.float32)


def add(a, b):
    return (a.astype(jnp.float32) + b.astype(jnp.float32)).astype(a.dtype)


def rms_norm(values, gain):
    stat = jnp.mean(values * values, axis=-1, keepdims=True)
    return values * lax.rsqrt(stat + 1e-06) * gain.astype(jnp.float32)


def whole(array):
    return pl.BlockSpec(array.shape, lambda *_: (0,) * len(array.shape))


def brief():
    return pl.CostEstimate(flops=1, transcendentals=0, bytes_accessed=1)


def front_kernel(pairs, pieces, blocks, rows, base_ref, prompts_ref, owner_ref, gain_a_ref, gain_e_ref, router_ref, *refs):
    pair_refs, refs = refs[: 2 * pairs], refs[2 * pairs :]
    piece_refs, refs = refs[:pieces], refs[pieces:]
    token_refs, refs = refs[:blocks], refs[blocks:]
    halves = 2 if blocks % 2 == 0 else 1
    mixed_ref, weight_ref, inner_refs = refs[0], refs[1], refs[2 : 2 + halves]
    downs, ups, normed = refs[2 + halves :]
    first = 0
    for p in range(pairs):
        size = pair_refs[2 * p].shape[0]
        downs[first : first + size, :] = pair_refs[2 * p][...]
        ups[first : first + size, :] = pair_refs[2 * p + 1][...]
        first += size
    for p in range(pieces):
        size = piece_refs[p].shape[1]
        downs[first : first + size, :] = piece_refs[p][0]
        ups[first : first + size, :] = piece_refs[p][1]
        first += size
    for k in range(blocks):
        floats = token_refs[k][0:rows, :].astype(jnp.float32)
        normed[k * rows : (k + 1) * rows, :] = rms_norm(floats, gain_a_ref[...]).astype(jnp.bfloat16)
    group = 2 if blocks % 2 == 0 else 1
    for g in range(0, blocks, group):
        at = [base_ref[k] + lax.broadcasted_iota(jnp.int32, (rows, 1), 0) for k in range(g, g + group)]
        at = jnp.concatenate(at)
        inside = (at >= prompts_ref[0:1, :]) & (at < prompts_ref[1:2, :])
        slot = jnp.sum(jnp.where(inside, prompts_ref[2:3, :], 0), axis=1, keepdims=True)
        low = dot(normed[g * rows : (g + group) * rows, :], downs[...], 1)
        low = jnp.where(owner_ref[...] == slot, low, 0.0).astype(jnp.bfloat16)
        delta = dot(low, ups[...])
        for k in range(g, g + group):
            floats = token_refs[k][0:rows, :].astype(jnp.float32)
            mixed = (floats + 2.0 * delta[(k - g) * rows : (k - g + 1) * rows, :]).astype(jnp.bfloat16)
            if k == 0:
                mixed_ref[...] = mixed
            inner = rms_norm(mixed.astype(jnp.float32), gain_e_ref[...]).astype(jnp.bfloat16)
            place = k % (blocks // halves) * rows
            inner_refs[k * halves // blocks][place : place + rows, :] = inner
            prob = jax.nn.sigmoid(dot(router_ref[...], inner, 1))
            expert = lax.broadcasted_iota(jnp.int32, (LANES, rows), 0).astype(jnp.float32)
            ids = token_refs[k][rows : rows + EXTRA, :].astype(jnp.float32)
            chosen = (ids[0:1, 0:rows] == expert) | (ids[1:2, 0:rows] == expert)
            weight_ref[k * rows : (k + 1) * rows, :] = jnp.where(chosen, prob, 0.0).T


def front(bases, prompts, owner, gain_a, gain_e, router, pairs, pieces, tokens):
    rows = tokens[0].shape[0] - EXTRA
    width = tokens[0].shape[1]
    blocks = len(tokens)
    outs = [
        jax.ShapeDtypeStruct((rows, width), jnp.bfloat16),
        jax.ShapeDtypeStruct((blocks * rows, LANES), jnp.float32),
    ]
    halves = 2 if blocks % 2 == 0 else 1
    outs += [jax.ShapeDtypeStruct((blocks * rows // halves, width), jnp.bfloat16)] * halves
    arrays = [prompts, owner, gain_a, gain_e, router, *pairs, *pieces, *tokens]
    total = owner.shape[1]
    scratch = [pltpu.VMEM((n, width), jnp.bfloat16) for n in (total, total, blocks * rows)]
    mixed, weight, *inner = pl.pallas_call(
        functools.partial(front_kernel, len(pairs) // 2, len(pieces), blocks, rows),
        grid=(1,),
        out_shape=outs,
        in_specs=[pl.BlockSpec(memory_space=pltpu.SMEM)] + [whole(a) for a in arrays],
        out_specs=[whole(a) for a in outs],
        scratch_shapes=scratch,
        compiler_params=pltpu.CompilerParams(vmem_limit_bytes=VMEM),
        cost_estimate=brief(),
        name="front",
    )(bases, *arrays)
    return mixed, weight, inner


def hidden_kernel(los, tiles, at_ref, *refs):
    x_refs, refs = refs[:tiles], refs[tiles:]
    weight_ref, gate_refs, up_refs = refs[0], refs[1 : 1 + los], refs[1 + los : 1 + 2 * los]
    act_ref, gate, up = refs[1 + 2 * los :]
    units = gate_refs[0].shape[0]

    @pl.when(pl.program_id(0) == 0)
    def _():
        for j in range(los):
            place = pl.ds(pl.multiple_of(lax.rem(at_ref[1] + j, los) * units, 16), units)
            gate[place, :] = gate_refs[j][...]
            up[place, :] = up_refs[j][...]

    for t in range(tiles):

        def work(t=t):
            x = x_refs[t][...]
            lane = lax.broadcasted_iota(jnp.int32, (x.shape[0], LANES), 1)
            scale = jnp.sum(jnp.where(lane == at_ref[0], weight_ref[...], 0.0), axis=1, keepdims=True)
            gated = jax.nn.gelu(dot(x, gate[...], 1), approximate=True)
            act_ref[...] = (gated * dot(x, up[...], 1) * scale).astype(jnp.bfloat16)

        pl.when(pl.program_id(0) == t)(work)


def hidden(at, xs, weight, gates, ups):
    tiles, (tile, width) = len(xs), xs[0].shape
    los, units = len(gates), gates[0].shape[0]
    return pl.pallas_call(
        functools.partial(hidden_kernel, los, tiles),
        grid=(tiles,),
        out_shape=jax.ShapeDtypeStruct((tiles * tile, los * units), jnp.bfloat16),
        in_specs=[pl.BlockSpec(memory_space=pltpu.SMEM)]
        + [whole(x) for x in xs]
        + [pl.BlockSpec((tile, LANES), lambda i: (i, 0))]
        + [whole(a) for a in (*gates, *ups)],
        out_specs=pl.BlockSpec((tile, los * units), lambda i: (i, 0)),
        scratch_shapes=[pltpu.VMEM((los * units, width), jnp.bfloat16)] * 2,
        compiler_params=pltpu.CompilerParams(vmem_limit_bytes=VMEM // 2),
        cost_estimate=brief(),
        name="hidden",
    )(at, *xs, weight, *gates, *ups)


def project_kernel(exs, lines, has_added, *refs):
    act_refs, down_refs, refs = refs[:exs], refs[exs : 2 * exs], refs[2 * exs :]
    added_refs, out_refs = (refs[:lines], refs[lines:]) if has_added else (None, refs)
    total = dot(act_refs[0][...], down_refs[0][...])
    for i in range(1, exs):
        total = total + dot(act_refs[i][...], down_refs[i][...])
    for k in range(lines):

        def store(k=k):
            value = total + added_refs[k][...].astype(jnp.float32) if has_added else total
            out_refs[k][...] = value.astype(jnp.bfloat16)

        pl.when(pl.program_id(0) == k)(store)


def project(lines, acts, downs, added):
    units, cols = downs[0].shape
    rows = acts[0].shape[0] // lines
    block = jax.ShapeDtypeStruct((rows, cols), jnp.bfloat16)
    return pl.pallas_call(
        functools.partial(project_kernel, len(acts), lines, bool(added)),
        grid=(lines,),
        out_shape=[block] * lines,
        in_specs=[pl.BlockSpec((rows, units), lambda i: (i, 0))] * len(acts) + [whole(a) for a in (*downs, *added)],
        out_specs=[whole(block)] * lines,
        compiler_params=pltpu.CompilerParams(vmem_limit_bytes=VMEM // 3),
        cost_estimate=brief(),
        name="project",
    )(*acts, *downs, *added)


def final_kernel(los, lines, count, lo_ref, mixed_ref, *refs):
    out_ref = refs[-1]
    cols = mixed_ref.shape[1] // (los * lines)
    for j in range(los):
        parts = refs[j * count : (j + 1) * count]
        total = parts[0][...].astype(jnp.float32)
        for part in parts[1:]:
            total = total + part[...].astype(jnp.float32)
        for h in range(lines):
            first = (h * los + lax.rem(lo_ref[0] + j, los)) * cols
            place = pl.ds(pl.multiple_of(first, LANES), cols)
            own = mixed_ref[:, place].astype(jnp.float32)
            out_ref[:, place] = (own + total[:, h * cols : (h + 1) * cols]).astype(jnp.bfloat16)


def final(lines, lo, mixed, parts):
    los, count = len(parts), len(parts[0])
    rows, width = mixed.shape
    if width // (los * lines) % LANES:
        sums = [sum(p.astype(jnp.float32) for p in group).reshape(rows, lines, -1) for group in parts]
        total = jnp.roll(jnp.stack(sums, axis=2), lo[0], axis=2).reshape(rows, width)
        return (mixed.astype(jnp.float32) + total).astype(jnp.bfloat16)
    flat = [p for group in parts for p in group]
    return pl.pallas_call(
        functools.partial(final_kernel, los, lines, count),
        out_shape=jax.ShapeDtypeStruct(mixed.shape, jnp.bfloat16),
        grid=(1,),
        in_specs=[pl.BlockSpec(memory_space=pltpu.SMEM)] + [whole(a) for a in (mixed, *flat)],
        out_specs=whole(mixed),
        compiler_params=pltpu.CompilerParams(vmem_limit_bytes=VMEM // 4),
        cost_estimate=brief(),
        name="final",
    )(lo, mixed, *flat)


def on_device(
    sizes,
    residual_input,
    prompt_token_length,
    prompt_adapter_index,
    adapter_table_row,
    adapter_norm_gain,
    adapter_down_maps,
    adapter_up_maps,
    expert_norm_gain,
    router,
    token_expert_index,
    expert_gate_up_weight,
    expert_down_weight,
):
    lines, los, exs = sizes["line"], sizes["lo"], sizes["ex"]
    tok_rows, width = residual_input.shape
    num_experts = router.shape[1]
    line, lo, ex, core = (lax.axis_index(n) for n in ("line", "lo", "ex", "core"))

    down_rows = expert_down_weight.shape[1]
    cols = expert_down_weight.shape[2]
    slots, rank, _ = adapter_down_maps.shape
    shares = los if slots % los == 0 else 1
    share = slots // shares
    ex_far, lo_far = range(1, exs), range(1, los)

    ids = token_expert_index.T.astype(jnp.bfloat16)
    ids = jnp.pad(ids, ((0, EXTRA - ids.shape[0]), (0, width - tok_rows)))
    block = jnp.concatenate([residual_input, ids])
    maps = [m.reshape(slots * rank, width) for m in (adapter_down_maps, adapter_up_maps)]
    first = lo * share * rank if shares > 1 else 0
    sent = lax.dynamic_slice_in_dim(jnp.stack(maps), first, share * rank, axis=1)
    crossed = [from_offset(sent, "ex", exs, i) for i in ex_far]
    gate, up = expert_gate_up_weight[0, 0].T, expert_gate_up_weight[0, 1].T
    ups = {(0, j): from_offset(up, "lo", los, j) for j in lo_far}
    tokens = {m: across(block, lines, m) for m in (2, 1, 0) if m < lines}
    other_maps = [from_offset(m, "core", CORES, 1) for m in maps]

    ends = jnp.cumsum(prompt_token_length)
    adapter_ids = jnp.arange(adapter_table_row.shape[0], dtype=jnp.int32)
    named = prompt_adapter_index[:, None] == adapter_ids[None, :]
    prompt_row = jnp.sum(jnp.where(named, adapter_table_row[None, :], 0), axis=1)
    prompts = jnp.stack([ends - prompt_token_length, ends, prompt_row])
    router_rows = jnp.pad(router.T, ((0, LANES - num_experts), (0, 0)))
    offsets = line ^ jnp.arange(lines, dtype=jnp.int32)
    bases = (((offsets * los + lo) * exs + ex) * CORES + core) * tok_rows
    number = jnp.arange(slots * rank, dtype=jnp.int32) // rank
    both = lambda slot: [slot, slot + jnp.where(core == 0, slots, -slots)]
    owners = both((ex * CORES + core) * slots + number)
    for i in ex_far:
        for j in range(shares):
            start = ((ex + i) % exs * CORES + core) * slots + (lo + j) % los * share
            owners += both(start + number[: share * rank])
    owner = jnp.concatenate(owners)[None, :]
    small = [bases, prompts, owner, adapter_norm_gain[None], expert_norm_gain[None], router_rows]

    gate, up, small, crossed, ups, tokens, other_maps = together(gate, up, small, crossed, ups, tokens, other_maps)
    passed = [from_offset(c, "lo", los, j) for c in crossed for j in range(shares)]
    gates = {(i, 0): from_offset(gate, "ex", exs, i) for i in ex_far}
    if lines == 4:
        tokens[3] = across(tokens[2], lines, 1)

    gate, up, passed, gates, tokens, down = together(gate, up, passed, gates, tokens, expert_down_weight)
    down = lax.all_to_all(
        down.reshape(lines, down_rows // lines, cols), "line", split_axis=0, concat_axis=0, tiled=True
    )
    held = [v for p in passed for v in (p, from_offset(p, "core", CORES, 1))]
    held, tokens, gate, up = together(held, tokens, gate, up)
    gates.update({(0, j): from_offset(gate, "lo", los, j) for j in lo_far})
    ups.update({(i, 0): from_offset(up, "ex", exs, i) for i in ex_far})
    mixed, w_own, x_own = front(*small, maps + other_maps, held, [tokens[m] for m in range(lines)])

    gates, ups, gate, up, x_own, w_own = together(gates, ups, gate, up, x_own, w_own)
    gates[0, 0], ups[0, 0] = gate, up
    for i in ex_far:
        for j in lo_far:
            gates[i, j] = from_offset(gates[i, 0], "lo", los, j)
            ups[i, j] = from_offset(ups[0, j], "ex", exs, i)
    x_far = [from_offset(v, "core", CORES, 1) for v in x_own]
    w_far = from_offset(w_own, "core", CORES, 1)

    def act(i, x, w):
        at = jnp.stack([(ex + i) % exs * CORES + core, lo])
        return hidden(at, x, w, *([of[i, j] for j in range(los)] for of in (gates, ups)))

    near, far = [act(0, x_own, w_own)], [act(0, x_far, w_far)]
    down = down.transpose(1, 0, 2).reshape(down_rows // lines, lines * cols)
    downs = {(i, 0): from_offset(down, "ex", exs, i) for i in range(exs)}
    downs.update({(0, j): from_offset(down, "lo", los, j) for j in lo_far})
    places = [(a, b) for a in range(los) for b in range(exs)]
    for i in ex_far:
        for j in lo_far:
            moves = [((a + j) % los * exs + (b + i) % exs, a * exs + b) for a, b in places]
            downs[i, j] = lax.ppermute(down, ("lo", "ex"), moves)

    x_own, w_own, x_far, w_far, near, far, gates, ups = together(x_own, w_own, x_far, w_far, near, far, gates, ups)
    far += [act(i, x_far, w_far) for i in ex_far]
    near += [act(i, x_own, w_own) for i in ex_far]

    direct = [(i, 0) for i in range(exs)] + [(0, j) for j in lo_far]
    near, far, pieces = together(near, far, [downs[k] for k in direct])
    downs.update(zip(direct, pieces))
    parts = []
    joined = None
    for j in range(los):
        of_piece = [downs[i, j] for i in range(exs)]
        if joined is not None:
            near, far, of_piece, joined = together(near, far, of_piece, joined)
            parts[-1].append(across(joined, lines, 2))
        if j == 0:
            sums = lambda acts: sum(dot(a, d) for a, d in zip(acts, of_piece))
            sent = sums(far).astype(jnp.bfloat16).reshape(lines, tok_rows, -1)
            added = jnp.concatenate([from_offset(sent[k], "core", CORES, 1) for k in range(lines)])
            total = (sums(near) + added.astype(jnp.float32)).astype(jnp.bfloat16)
            home = list(total.reshape(lines, tok_rows, -1))
        else:
            sent = project(lines, far, of_piece, [])
            home = project(lines, near, of_piece, [from_offset(v, "core", CORES, 1) for v in sent])
        if lines == 4:
            passing = across(home[3], lines, 1)
            if j > 0:
                passing, parts[-1] = together(passing, parts[-1])
            joined = add(home[2], passing)
            parts.append([home[0], across(home[1], lines, 1)])
        else:
            parts.append([across(home[m], lines, m) for m in range(lines)])
    if lines == 4:
        parts[-1].append(across(joined, lines, 2))
    return final(lines, lo[None], mixed, parts)


def solution(mesh):
    dp, expert = mesh.shape["dp"], mesh.shape["expert"]
    lines = 4 if dp % 4 == 0 else 2 if dp % 2 == 0 else 1
    sizes = {"line": lines, "lo": dp // lines, "ex": expert // CORES, "core": CORES}
    inner = Mesh(mesh.devices.reshape(tuple(sizes.values())), tuple(sizes))
    rows = P(("line", "lo", "ex", "core"), None)
    slots = P(("ex", "core"), None, None)
    placed = (
        rows,
        P(),
        P(),
        P(),
        P(),
        slots,
        slots,
        P(),
        P(),
        rows,
        P(("ex", "core"), None, None, ("line", "lo")),
        P(("ex", "core"), None, ("line", "lo")),
    )

    def body(*arrays):
        return on_device(sizes, *arrays)

    return jax.shard_map(body, mesh=inner, in_specs=placed, out_specs=rows, check_vma=False)
```

time: 172 us -> 165 us (0.959)
  Pallas kernels: 13.8 us -> 40.7 us
  matrix products: 24.4 us -> 8.34 us
  waiting for transfers between devices: 72.6 us -> 64.1 us
  local copies, waits for them, and re-layouts: 12.1 us -> 8.65 us
  starting transfers between devices: 39.9 us -> 36.5 us
  other arithmetic: 8.58 us -> 5.49 us
    pallas_call x1 -> x7, Pallas kernels: 12.6 us -> 39.6 us  [the longest x4 21.8 us: hidden(): pl.pallas_call(functools.partial(hidden_kernel, los, tiles), grid=(tiles,...]
    ppermute x29 -> x25, waiting for transfers between devices: 40.5 us -> 24.2 us  [from_offset(): lax.ppermute(value, axis, [((i + offset) % size, i) for i in range(size)])]
    dot_general x16 -> x4, matrix products: 24.4 us -> 8.34 us  [dot(): lax.dot_general(a, b, (((1,), (rhs_dim,)), ((), ())), preferred_element_t...]
    ppermute x9, waiting for transfers between devices: 32 us -> 36.7 us  [across(): lax.ppermute(value, 'line', [(i ^ mask, i) for i in range(size)])]
    ppermute x29 -> x25, starting transfers between devices: 19.6 us -> 15.7 us  [from_offset(): lax.ppermute(value, axis, [((i + offset) % size, i) for i in range(size)])]
    all_to_all x1, waiting for transfers between devices: 0.01 us -> 3.19 us  [on_device(): lax.all_to_all(down.reshape(lines, down_rows // lines, cols), 'line', spl...]
    concatenate x8 -> x0, local copies, waits for them, and re-layouts: 2.62 us -> none  [the longest x4 2.47 us: act(): jnp.concatenate([of[i, j] for j in range(los)])]
    ppermute x9, starting transfers between devices: 16.8 us -> 14.5 us  [across(): lax.ppermute(value, 'line', [(i ^ mask, i) for i in range(size)])]
  transfers between devices with their start and end apart: 39 -> 36, of which waited for: 17 -> 16; matrix products, arithmetic and copies ran while one was open for 22% -> 10% of each run, Pallas kernels for 7% -> 22%
where the time goes in v1:
time: 165 us; the launch traced here: 164 us
  waiting for transfers between devices  64.1 us (39%)
  Pallas kernels  40.7 us (25%)
  starting transfers between devices  36.5 us (22%)
  local copies, waits for them, and re-layouts  8.65 us (5%)
  matrix products  8.34 us (5%)
  other arithmetic  5.49 us (3%)
    ppermute x9, waiting for transfers between devices, across(): lax.ppermute(value, 'line', [(i ^ mask, i) for i in range(size)])  36.7 us
    ppermute x25, waiting for transfers between devices, from_offset(): lax.ppermute(value, axis, [((i + offset) % size, i) for i in range(size)])  24.2 us
    pallas_call x4, Pallas kernels, hidden(): pl.pallas_call(functools.partial(hidden_kernel, los, tiles), grid=(tiles,...  21.8 us
    ppermute x25, starting transfers between devices, from_offset(): lax.ppermute(value, axis, [((i + offset) % size, i) for i in range(size)])  15.7 us
    ppermute x9, starting transfers between devices, across(): lax.ppermute(value, 'line', [(i ^ mask, i) for i in range(size)])  14.5 us
    pallas_call x1, Pallas kernels, front(): pl.pallas_call(functools.partial(front_kernel, len(pairs) // 2, len(piece...  10.6 us
    dot_general x4, matrix products, dot(): lax.dot_general(a, b, (((1,), (rhs_dim,)), ((), ())), preferred_element_t...  8.34 us
    pallas_call x2, Pallas kernels, project(): pl.pallas_call(functools.partial(project_kernel, len(acts), lines, bool(a...  7.25 us
  transfers between devices with their start and end apart: 36, of which 16 were waited for; matrix products, arithmetic and copies ran while one was open for 10% of the time, Pallas kernels for 22%

profile of v1, /device:TPU:0, one launch (start us, length us, event | category | flops | bytes accessed | tf_op | source)
XLA Modules:
  0.0 164.3 jit_solution(12585114108724456277)
XLA Ops:
  1.8 3.1 %collective-permute-start.2 = (bf16[272,1024]{1,0:T(8,128)(2,1)S(1)}, bf16[272,1024]{1,0:T(8,128)(2,1)}, u32[]{:S(2)}, u32[]{:S(2)}) collective-permute-start(bf16[272,1024]{1,0:T(8,128)(2,1)S(1)} %fusion.1.refs_8_), channel_id=1, source_target_pairs={{8,0},{0,8},{24,16},{16,24},{9,1},{1,9},{25,17},{17,25},{10,2},{2,... | collective-permute-start | bytes 1671176 | tf_op jit(solution)/shard_map/ppermute | solution.py:28
  4.9 2.6 %collective-permute-start.3 = (bf16[272,1024]{1,0:T(8,128)(2,1)S(1)}, bf16[272,1024]{1,0:T(8,128)(2,1)}, u32[]{:S(2)}, u32[]{:S(2)}) collective-permute-start(bf16[272,1024]{1,0:T(8,128)(2,1)S(1)} %fusion.1.refs_8_), channel_id=1, source_target_pairs={{16,0},{24,8},{0,16},{8,24},{17,1},{25,9},{1,17},{9,25},{18,2},{26... | collective-permute-start | bytes 1671176 | tf_op jit(solution)/shard_map/ppermute | solution.py:28
  7.5 2.0 %fusion.2 = bf16[2,128,1024]{2,1,0:T(8,128)(2,1)} fusion(s32[]{:T(128)S(6)} %select_n.55, bf16[1,256,1024]{2,1,0:T(8,128)(2,1)} %bitcast.39, bf16[1,256,1024]{2,1,0:T(8,128)(2,1)} %bitcast.42), kind=kLoop, calls=%fused_computation.10 | loop fusion | flops 1048576 | bytes 1572868 | tf_op jit(solution)/shard_map/stack | solution.py:266
  15.8 7.1 %collective-permute-done.refs_4_ = bf16[2,128,1024]{2,1,0:T(8,128)(2,1)} collective-permute-done((bf16[2,128,1024]{2,1,0:T(8,128)(2,1)}, bf16[2,128,1024]{2,1,0:T(8,128)(2,1)}, u32[]{:S(2)}, u32[]{:S(2)}) %collective-permute-start) | collective-permute-done | bytes 524320 | tf_op jit(solution)/shard_map/ppermute | solution.py:20
  25.1 4.3 %collective-permute-done.2.refs_9_ = bf16[272,1024]{1,0:T(8,128)(2,1)} collective-permute-done((bf16[272,1024]{1,0:T(8,128)(2,1)S(1)}, bf16[272,1024]{1,0:T(8,128)(2,1)}, u32[]{:S(2)}, u32[]{:S(2)}) %collective-permute-start.2) | collective-permute-done | bytes 557088 | tf_op jit(solution)/shard_map/ppermute | solution.py:28
  29.4 2.5 %collective-permute-done.3.refs_10_ = bf16[272,1024]{1,0:T(8,128)(2,1)} collective-permute-done((bf16[272,1024]{1,0:T(8,128)(2,1)S(1)}, bf16[272,1024]{1,0:T(8,128)(2,1)}, u32[]{:S(2)}, u32[]{:S(2)}) %collective-permute-start.3) | collective-permute-done | bytes 557088 | tf_op jit(solution)/shard_map/ppermute | solution.py:28
  35.4 10.9 %collective-permute-done.6.refs_6_ = bf16[2,128,1024]{2,1,0:T(8,128)(2,1)S(1)} collective-permute-done((bf16[2,128,1024]{2,1,0:T(8,128)(2,1)}, bf16[2,128,1024]{2,1,0:T(8,128)(2,1)S(1)}, u32[]{:S(2)}, u32[]{:S(2)}) %collective-permute-start.6) | collective-permute-done | bytes 524320 | tf_op jit(solution)/shard_map/ppermute | solution.py:20
  47.4 2.3 %collective-permute-done.9.refs_5_ = bf16[2,128,1024]{2,1,0:T(8,128)(2,1)S(1)} collective-permute-done((bf16[2,128,1024]{2,1,0:T(8,128)(2,1)}, bf16[2,128,1024]{2,1,0:T(8,128)(2,1)S(1)}, u32[]{:S(2)}, u32[]{:S(2)}) %collective-permute-start.9) | collective-permute-done | bytes 524320 | tf_op jit(solution)/shard_map/ppermute | solution.py:20
  52.7 4.2 %all-to-all-start = ((bf16[4,704,128]{2,1,0:T(8,128)(2,1)}), bf16[4,704,128]{2,1,0:T(8,128)(2,1)}, u32[]{:S(2)}, u32[]{:S(2)}) async-start(bf16[4,704,128]{2,1,0:T(8,128)(2,1)} %bitcast.45), calls=%async_computation | async-start | bytes 1441792 | tf_op jit(solution)/shard_map/all_to_all | solution.py:298
  56.9 10.6 %front.1 = (bf16[256,1024]{1,0:T(8,128)(2,1)}, f32[1024,128]{1,0:T(8,128)}, bf16[512,1024]{1,0:T(8,128)(2,1)}, bf16[512,1024]{1,0:T(8,128)(2,1)}) custom-call(s32[4]{0:T(128)} %add_multiply_fusion.base_ref, s32[3,48]{1,0:T(4,128)} %pad_add_fusion.prompts_ref, s32[1,1024]{1,0:T(1,128)} %bitcast.47, bf16[1,1024]{1,0:T(2,128)(2,1)} %broadcast_in_dim.31.gain_a_ref, ...), custom_call_target="tpu_custom_call" | custom-call | flops 1 | bytes 1 | tf_op jit(solution)/shard_map/front/pallas_call | solution.py:110
  72.5 3.2 %all-to-all-done = bf16[4,704,128]{2,1,0:T(8,128)(2,1)} async-done(((bf16[4,704,128]{2,1,0:T(8,128)(2,1)}), bf16[4,704,128]{2,1,0:T(8,128)(2,1)}, u32[]{:S(2)}, u32[]{:S(2)}) %all-to-all-start) | async-done | bytes 720928 | tf_op jit(solution)/shard_map/all_to_all | solution.py:298
  75.7 2.0 %copy_bitcast_fusion = bf16[704,512]{1,0:T(8,128)(2,1)} fusion(bf16[4,704,128]{2,1,0:T(8,128)(2,1)} %all-to-all-done), kind=kLoop, calls=%fused_computation.6 | loop fusion | bytes 1441792 | tf_op jit(solution)/shard_map/reshape | solution.py:321
  82.7 5.0 %hidden.4.refs_0_ = bf16[1024,704]{1,0:T(8,128)(2,1)S(1)} custom-call(s32[2]{0:T(128)S(1)} %pad_add_fusion.1.at_ref, bf16[512,1024]{1,0:T(8,128)(2,1)S(1)} %copy-done, bf16[512,1024]{1,0:T(8,128)(2,1)S(1)} %copy-done.1, f32[1024,128]{1,0:T(8,128)S(1)} %copy-done.7, bf16[352,1024]{1,0:T(8,128)(2,1)S(1)} %get-tuple-element.132.refs_3_, ...), custom_call_target="tpu_custom_call" | custom-call | flops 1 | bytes 1 | tf_op jit(solution)/shard_map/hidden/pallas_call | solution.py:152
  87.8 2.1 %collective-permute-start.20 = (bf16[704,512]{1,0:T(8,128)(2,1)}, bf16[704,512]{1,0:T(8,128)(2,1)S(1)}, u32[]{:S(2)}, u32[]{:S(2)}) collective-permute-start(bf16[704,512]{1,0:T(8,128)(2,1)} %copy_bitcast_fusion), channel_id=1, source_target_pairs={{6,0},{4,2},{2,4},{0,6},{7,1},{5,3},{3,5},{1,7},{14,8},{12,10},{10... | collective-permute-start | bytes 2162696 | tf_op jit(solution)/shard_map/ppermute | solution.py:328
  89.9 5.4 %hidden.5.refs_0_ = bf16[1024,704]{1,0:T(8,128)(2,1)S(1)} custom-call(s32[2]{0:T(128)S(1)} %pad_add_fusion.1.at_ref, bf16[512,1024]{1,0:T(8,128)(2,1)S(1)} %collective-permute-done.13.refs_0_, bf16[512,1024]{1,0:T(8,128)(2,1)} %collective-permute-done.14.refs_1_, f32[1024,128]{1,0:T(8,128)} %collective-permute-done.15.refs_2_, ...), custom_call_target="tpu_custom_call" | custom-call | flops 1 | bytes 1 | tf_op jit(solution)/shard_map/hidden/pallas_call | solution.py:152
  95.3 5.4 %hidden.6.refs_1_ = bf16[1024,704]{1,0:T(8,128)(2,1)S(1)} custom-call(s32[2]{0:T(128)S(1)} %pad_add_fusion.2.at_ref, bf16[512,1024]{1,0:T(8,128)(2,1)S(1)} %copy-done, bf16[512,1024]{1,0:T(8,128)(2,1)S(1)} %copy-done.1, f32[1024,128]{1,0:T(8,128)S(1)} %copy-done.8, bf16[352,1024]{1,0:T(8,128)(2,1)} %collective-permute-done.7.refs_3_, ...), custom_call_target="tpu_custom_call" | custom-call | flops 1 | bytes 1 | tf_op jit(solution)/shard_map/hidden/pallas_call | solution.py:152
  100.7 6.0 %hidden.7.refs_1_ = bf16[1024,704]{1,0:T(8,128)(2,1)S(1)} custom-call(s32[2]{0:T(128)S(1)} %pad_add_fusion.2.at_ref, bf16[512,1024]{1,0:T(8,128)(2,1)S(1)} %collective-permute-done.13.refs_0_, bf16[512,1024]{1,0:T(8,128)(2,1)} %collective-permute-done.14.refs_1_, f32[1024,128]{1,0:T(8,128)} %collective-permute-done.15.refs_2_, ...), custom_call_target="tpu_custom_call" | custom-call | flops 1 | bytes 1 | tf_op jit(solution)/shard_map/hidden/pallas_call | solution.py:152
  106.8 2.1 %fusion.6 = f32[1024,512]{1,0:T(8,128)S(1)} fusion(bf16[1024,704]{1,0:T(8,128)(2,1)S(1)} %hidden.7.refs_1_, bf16[704,512]{1,0:T(8,128)(2,1)} %collective-permute-done.18), kind=kOutput, calls=%fused_computation.34 | convolution fusion | flops 738197504 | bytes 4259840 | tf_op jit(solution)/shard_map/dot_general | solution.py:32
  108.9 2.1 %add_convert_fusion.1 = bf16[1024,512]{1,0:T(8,128)(2,1)S(1)} fusion(f32[1024,512]{1,0:T(8,128)S(1)} %fusion.6, bf16[1024,704]{1,0:T(8,128)(2,1)S(1)} %hidden.5.refs_0_, bf16[704,512]{1,0:T(8,128)(2,1)} %copy_bitcast_fusion), kind=kOutput, calls=%fused_computation.1 | convolution fusion | flops 739246080 | bytes 5308416 | tf_op jit(solution)/shard_map/dot_general | solution.py:32
  112.2 2.1 %fusion.5 = f32[1024,512]{1,0:T(8,128)S(1)} fusion(bf16[1024,704]{1,0:T(8,128)(2,1)S(1)} %hidden.6.refs_1_, bf16[704,512]{1,0:T(8,128)(2,1)} %collective-permute-done.18), kind=kOutput, calls=%fused_computation.33 | convolution fusion | flops 738197504 | bytes 4259840 | tf_op jit(solution)/shard_map/dot_general | solution.py:32
  114.3 2.1 %add_convert_fusion = bf16[1024,512]{1,0:T(8,128)(2,1)S(1)} fusion(f32[1024,512]{1,0:T(8,128)S(1)} %fusion.5, bf16[256,512]{1,0:T(8,128)(2,1)S(1)} %collective-permute-done.24, bf16[256,512]{1,0:T(8,128)(2,1)S(1)} %collective-permute-done.23, bf16[256,512]{1,0:T(8,128)(2,1)S(1)} %collective-permute-done.22, bf16[256,512]{1,0:T(8,128)(2,1)S(1)} %collective-permute-done.21, ...), kind=kOutput, calls=%fused_computation | convolution fusion | flops 743964672 | bytes 6356992 | tf_op jit(solution)/shard_map/dot_general | solution.py:32
  116.5 1.7 %collective-permute-start.25 = (bf16[256,512]{1,0:T(8,128)(2,1)S(1)}, bf16[256,512]{1,0:T(8,128)(2,1)S(1)}, u32[]{:S(2)}, u32[]{:S(2)}) collective-permute-start(bf16[256,512]{1,0:T(8,128)(2,1)S(1)} %get-tuple-element.181), channel_id=1, source_target_pairs={{8,0},{0,8},{24,16},{16,24},{9,1},{1,9},{25,17},{17,25},{10,2},{2,... | collective-permute-start | bytes 786440 | tf_op jit(solution)/shard_map/ppermute | solution.py:28
  118.2 6.7 %collective-permute-done.25 = bf16[256,512]{1,0:T(8,128)(2,1)S(1)} collective-permute-done((bf16[256,512]{1,0:T(8,128)(2,1)S(1)}, bf16[256,512]{1,0:T(8,128)(2,1)S(1)}, u32[]{:S(2)}, u32[]{:S(2)}) %collective-permute-start.25) | collective-permute-done | bytes 262176 | tf_op jit(solution)/shard_map/ppermute | solution.py:28
  124.9 3.6 %project.2 = (bf16[256,512]{1,0:T(8,128)(2,1)S(1)}, bf16[256,512]{1,0:T(8,128)(2,1)S(1)}, bf16[256,512]{1,0:T(8,128)(2,1)S(1)}, bf16[256,512]{1,0:T(8,128)(2,1)S(1)}) custom-call(bf16[1024,704]{1,0:T(8,128)(2,1)S(1)} %hidden.5.refs_0_, bf16[1024,704]{1,0:T(8,128)(2,1)S(1)} %hidden.7.refs_1_, bf16[704,512]{1,0:T(8,128)(2,1)} %collective-permute-done.19.refs_2_, ...), custom_call_target="tpu_custom_call" | custom-call | flops 1 | bytes 1 | tf_op jit(solution)/shard_map/project/pallas_call | solution.py:187
  129.5 1.6 collective-permute-start.31
  132.5 3.7 %project.3 = (bf16[256,512]{1,0:T(8,128)(2,1)S(1)}, bf16[256,512]{1,0:T(8,128)(2,1)S(1)}, bf16[256,512]{1,0:T(8,128)(2,1)S(1)}, bf16[256,512]{1,0:T(8,128)(2,1)S(1)}) custom-call(bf16[1024,704]{1,0:T(8,128)(2,1)S(1)} %hidden.4.refs_0_, bf16[1024,704]{1,0:T(8,128)(2,1)S(1)} %hidden.6.refs_1_, bf16[704,512]{1,0:T(8,128)(2,1)} %collective-permute-done.19.refs_2_, ...), custom_call_target="tpu_custom_call" | custom-call | flops 1 | bytes 1 | tf_op jit(solution)/shard_map/project/pallas_call | solution.py:187
  138.3 4.8 %collective-permute-done.31.refs_1_ = bf16[256,512]{1,0:T(8,128)(2,1)S(1)} collective-permute-done((bf16[256,512]{1,0:T(8,128)(2,1)S(1)}, bf16[256,512]{1,0:T(8,128)(2,1)S(1)}, u32[]{:S(2)}, u32[]{:S(2)}) %collective-permute-start.31) | collective-permute-done | bytes 262176 | tf_op jit(solution)/shard_map/ppermute | solution.py:28
  143.1 2.8 %collective-permute-done.32.refs_2_ = bf16[256,512]{1,0:T(8,128)(2,1)S(1)} collective-permute-done((bf16[256,512]{1,0:T(8,128)(2,1)S(1)}, bf16[256,512]{1,0:T(8,128)(2,1)S(1)}, u32[]{:S(2)}, u32[]{:S(2)}) %collective-permute-start.32) | collective-permute-done | bytes 262176 | tf_op jit(solution)/shard_map/ppermute | solution.py:28
  145.9 4.1 %collective-permute-done.30 = bf16[256,512]{1,0:T(8,128)(2,1)S(1)} collective-permute-done((bf16[256,512]{1,0:T(8,128)(2,1)S(1)}, bf16[256,512]{1,0:T(8,128)(2,1)S(1)}, u32[]{:S(2)}, u32[]{:S(2)}) %collective-permute-start.30) | collective-permute-done | bytes 262176 | tf_op jit(solution)/shard_map/ppermute | solution.py:28
  150.0 1.6 collective-permute-start.34
  151.6 6.9 %collective-permute-done.33.refs_4_ = bf16[256,512]{1,0:T(8,128)(2,1)S(1)} collective-permute-done((bf16[256,512]{1,0:T(8,128)(2,1)S(1)}, bf16[256,512]{1,0:T(8,128)(2,1)S(1)}, u32[]{:S(2)}, u32[]{:S(2)}) %collective-permute-start.33) | collective-permute-done | bytes 262176 | tf_op jit(solution)/shard_map/ppermute | solution.py:28
  158.5 4.7 %collective-permute-done.34.refs_5_ = bf16[256,512]{1,0:T(8,128)(2,1)S(1)} collective-permute-done((bf16[256,512]{1,0:T(8,128)(2,1)S(1)}, bf16[256,512]{1,0:T(8,128)(2,1)S(1)}, u32[]{:S(2)}, u32[]{:S(2)}) %collective-permute-start.34) | collective-permute-done | bytes 262176 | tf_op jit(solution)/shard_map/ppermute | solution.py:28
  (130 shorter events, 34.7 us)
Async XLA Ops:
  1.8 27.6 %collective-permute-start.2 = (bf16[272,1024]{1,0:T(8,128)(2,1)S(1)}, bf16[272,1024]{1,0:T(8,128)(2,1)}, u32[]{:S(2)}, u32[]{:S(2)}) collective-permute-start(bf16[272,1024]{1,0:T(8,128)(2,1)S(1)} %fusion.1.refs_8_), channel_id=1, source_target_pairs={{8,0},{0,8},{24,16},{16,24},{9,1},{1,9},{25,17},{17,25},{10,2},{2,... | collective-permute-start | bytes 1671176 | tf_op jit(solution)/shard_map/ppermute | solution.py:28
  4.9 27.1 %collective-permute-start.3 = (bf16[272,1024]{1,0:T(8,128)(2,1)S(1)}, bf16[272,1024]{1,0:T(8,128)(2,1)}, u32[]{:S(2)}, u32[]{:S(2)}) collective-permute-start(bf16[272,1024]{1,0:T(8,128)(2,1)S(1)} %fusion.1.refs_8_), channel_id=1, source_target_pairs={{16,0},{24,8},{0,16},{8,24},{17,1},{25,9},{1,17},{9,25},{18,2},{26... | collective-permute-start | bytes 1671176 | tf_op jit(solution)/shard_map/ppermute | solution.py:28
  9.5 13.5 %collective-permute-start = (bf16[2,128,1024]{2,1,0:T(8,128)(2,1)}, bf16[2,128,1024]{2,1,0:T(8,128)(2,1)}, u32[]{:S(2)}, u32[]{:S(2)}) collective-permute-start(bf16[2,128,1024]{2,1,0:T(8,128)(2,1)} %fusion.2), channel_id=1, source_target_pairs={{2,0},{0,2},{3,1},{1,3},{6,4},{4,6},{7,5},{5,7},{10,8},{8,10},{11,... | collective-permute-start | bytes 1572872 | tf_op jit(solution)/shard_map/ppermute | solution.py:20
  11.2 20.8 %collective-permute-start.1 = (bf16[352,1024]{1,0:T(8,128)(2,1)S(1)}, bf16[352,1024]{1,0:T(8,128)(2,1)S(1)}, u32[]{:S(2)}, u32[]{:S(2)}) collective-permute-start(bf16[352,1024]{1,0:T(8,128)(2,1)S(1)} %get-tuple-element.134.refs_5_), channel_id=1, source_target_pairs={{4,0},{0,4},{5,1},{1,5},{6,2},{2,6},{7,3},{3,7},{12,8},{8,12},{13,... | collective-permute-start | bytes 2162696 | tf_op jit(solution)/shard_map/ppermute | solution.py:20
  12.7 10.8 %collective-permute-start.4 = (bf16[256,1024]{1,0:T(8,128)(2,1)S(1)}, bf16[256,1024]{1,0:T(8,128)(2,1)}, u32[]{:S(2)}, u32[]{:S(2)}) collective-permute-start(bf16[256,1024]{1,0:T(8,128)(2,1)S(1)} %bitcast.41), channel_id=1, source_target_pairs={{1,0},{0,1},{3,2},{2,3},{5,4},{4,5},{7,6},{6,7},{9,8},{8,9},{11,10... | collective-permute-start | bytes 1572872 | tf_op jit(solution)/shard_map/ppermute | solution.py:20
  31.9 15.0 %collective-permute-start.7 = (bf16[352,1024]{1,0:T(8,128)(2,1)S(1)}, bf16[352,1024]{1,0:T(8,128)(2,1)}, u32[]{:S(2)}, u32[]{:S(2)}) collective-permute-start(bf16[352,1024]{1,0:T(8,128)(2,1)S(1)} %get-tuple-element.132.refs_3_), channel_id=1, source_target_pairs={{2,0},{0,2},{3,1},{1,3},{6,4},{4,6},{7,5},{5,7},{10,8},{8,10},{11,... | collective-permute-start | bytes 2162696 | tf_op jit(solution)/shard_map/ppermute | solution.py:20
  33.4 12.8 %collective-permute-start.8 = (bf16[272,1024]{1,0:T(8,128)(2,1)}, bf16[272,1024]{1,0:T(8,128)(2,1)S(1)}, u32[]{:S(2)}, u32[]{:S(2)}) collective-permute-start(bf16[272,1024]{1,0:T(8,128)(2,1)} %collective-permute-done.3.refs_10_), channel_id=1, source_target_pairs={{8,0},{0,8},{24,16},{16,24},{9,1},{1,9},{25,17},{17,25},{10,2},{2,... | collective-permute-start | bytes 1671176 | tf_op jit(solution)/shard_map/ppermute | solution.py:28
  33.9 12.4 %collective-permute-start.6 = (bf16[2,128,1024]{2,1,0:T(8,128)(2,1)}, bf16[2,128,1024]{2,1,0:T(8,128)(2,1)S(1)}, u32[]{:S(2)}, u32[]{:S(2)}) collective-permute-start(bf16[2,128,1024]{2,1,0:T(8,128)(2,1)} %collective-permute-done.refs_4_), channel_id=1, source_target_pairs={{4,0},{0,4},{5,1},{1,5},{6,2},{2,6},{7,3},{3,7},{12,8},{8,12},{13,... | collective-permute-start | bytes 1572872 | tf_op jit(solution)/shard_map/ppermute | solution.py:20
  46.9 2.8 %collective-permute-start.9 = (bf16[2,128,1024]{2,1,0:T(8,128)(2,1)}, bf16[2,128,1024]{2,1,0:T(8,128)(2,1)S(1)}, u32[]{:S(2)}, u32[]{:S(2)}) collective-permute-start(bf16[2,128,1024]{2,1,0:T(8,128)(2,1)} %collective-permute-done.refs_4_), channel_id=1, source_target_pairs={{1,0},{0,1},{3,2},{2,3},{5,4},{4,5},{7,6},{6,7},{9,8},{8,9},{11,10... | collective-permute-start | bytes 1572872 | tf_op jit(solution)/shard_map/ppermute | solution.py:20
  46.9 2.8 %collective-permute-start.10 = (bf16[2,128,1024]{2,1,0:T(8,128)(2,1)S(1)}, bf16[2,128,1024]{2,1,0:T(8,128)(2,1)S(1)}, u32[]{:S(2)}, u32[]{:S(2)}) collective-permute-start(bf16[2,128,1024]{2,1,0:T(8,128)(2,1)S(1)} %collective-permute-done.6.refs_6_), channel_id=1, source_target_pairs={{1,0},{0,1},{3,2},{2,3},{5,4},{4,5},{7,6},{6,7},{9,8},{8,9},{11,10... | collective-permute-start | bytes 1572872 | tf_op jit(solution)/shard_map/ppermute | solution.py:20
  49.8 18.3 %collective-permute-start.11 = (bf16[352,1024]{1,0:T(8,128)(2,1)S(1)}, bf16[352,1024]{1,0:T(8,128)(2,1)}, u32[]{:S(2)}, u32[]{:S(2)}) collective-permute-start(bf16[352,1024]{1,0:T(8,128)(2,1)S(1)} %get-tuple-element.132.refs_3_), channel_id=1, source_target_pairs={{4,0},{0,4},{5,1},{1,5},{6,2},{2,6},{7,3},{3,7},{12,8},{8,12},{13,... | collective-permute-start | bytes 2162696 | tf_op jit(solution)/shard_map/ppermute | solution.py:20
  51.2 17.9 %collective-permute-start.12 = (bf16[352,1024]{1,0:T(8,128)(2,1)S(1)}, bf16[352,1024]{1,0:T(8,128)(2,1)S(1)}, u32[]{:S(2)}, u32[]{:S(2)}) collective-permute-start(bf16[352,1024]{1,0:T(8,128)(2,1)S(1)} %get-tuple-element.134.refs_5_), channel_id=1, source_target_pairs={{2,0},{0,2},{3,1},{1,3},{6,4},{4,6},{7,5},{5,7},{10,8},{8,10},{11,... | collective-permute-start | bytes 2162696 | tf_op jit(solution)/shard_map/ppermute | solution.py:20
  52.7 23.0 %all-to-all-start = ((bf16[4,704,128]{2,1,0:T(8,128)(2,1)}), bf16[4,704,128]{2,1,0:T(8,128)(2,1)}, u32[]{:S(2)}, u32[]{:S(2)}) async-start(bf16[4,704,128]{2,1,0:T(8,128)(2,1)} %bitcast.45), calls=%async_computation | async-start | bytes 1441792 | tf_op jit(solution)/shard_map/all_to_all | solution.py:298
  70.0 8.3 %collective-permute-start.13 = (bf16[512,1024]{1,0:T(8,128)(2,1)}, bf16[512,1024]{1,0:T(8,128)(2,1)S(1)}, u32[]{:S(2)}, u32[]{:S(2)}) collective-permute-start(bf16[512,1024]{1,0:T(8,128)(2,1)} %get-tuple-element.139.refs_0_), channel_id=1, source_target_pairs={{1,0},{0,1},{3,2},{2,3},{5,4},{4,5},{7,6},{6,7},{9,8},{8,9},{11,10... | collective-permute-start | bytes 3145736 | tf_op jit(solution)/shard_map/ppermute | solution.py:20
  70.0 7.7 %collective-permute-start.15 = (f32[1024,128]{1,0:T(8,128)}, f32[1024,128]{1,0:T(8,128)}, u32[]{:S(2)}, u32[]{:S(2)}) collective-permute-start(f32[1024,128]{1,0:T(8,128)} %get-tuple-element.141.refs_2_), channel_id=1, source_target_pairs={{1,0},{0,1},{3,2},{2,3},{5,4},{4,5},{7,6},{6,7},{9,8},{8,9},{11,10... | collective-permute-start | bytes 1572872 | tf_op jit(solution)/shard_map/ppermute | solution.py:20
  70.5 17.3 %collective-permute-start.14 = (bf16[512,1024]{1,0:T(8,128)(2,1)}, bf16[512,1024]{1,0:T(8,128)(2,1)}, u32[]{:S(2)}, u32[]{:S(2)}) collective-permute-start(bf16[512,1024]{1,0:T(8,128)(2,1)} %get-tuple-element.140.refs_1_), channel_id=1, source_target_pairs={{1,0},{0,1},{3,2},{2,3},{5,4},{4,5},{7,6},{6,7},{9,8},{8,9},{11,10... | collective-permute-start | bytes 3145736 | tf_op jit(solution)/shard_map/ppermute | solution.py:20
  70.5 24.8 %collective-permute-start.16 = (bf16[352,1024]{1,0:T(8,128)(2,1)}, bf16[352,1024]{1,0:T(8,128)(2,1)}, u32[]{:S(2)}, u32[]{:S(2)}) collective-permute-start(bf16[352,1024]{1,0:T(8,128)(2,1)} %collective-permute-done.7.refs_3_), channel_id=1, source_target_pairs={{4,0},{0,4},{5,1},{1,5},{6,2},{2,6},{7,3},{3,7},{12,8},{8,12},{13,... | collective-permute-start | bytes 2162696 | tf_op jit(solution)/shard_map/ppermute | solution.py:20
  71.2 24.1 %collective-permute-start.17 = (bf16[352,1024]{1,0:T(8,128)(2,1)}, bf16[352,1024]{1,0:T(8,128)(2,1)}, u32[]{:S(2)}, u32[]{:S(2)}) collective-permute-start(bf16[352,1024]{1,0:T(8,128)(2,1)} %copy-done.2), channel_id=1, source_target_pairs={{2,0},{0,2},{3,1},{1,3},{6,4},{4,6},{7,5},{5,7},{10,8},{8,10},{11,... | collective-permute-start | bytes 2162696 | tf_op jit(solution)/shard_map/ppermute | solution.py:20
  77.7 29.1 %collective-permute-start.18 = (bf16[704,512]{1,0:T(8,128)(2,1)}, bf16[704,512]{1,0:T(8,128)(2,1)}, u32[]{:S(2)}, u32[]{:S(2)}) collective-permute-start(bf16[704,512]{1,0:T(8,128)(2,1)} %copy_bitcast_fusion), channel_id=1, source_target_pairs={{2,0},{0,2},{3,1},{1,3},{6,4},{4,6},{7,5},{5,7},{10,8},{8,10},{11,... | collective-permute-start | bytes 2162696 | tf_op jit(solution)/shard_map/ppermute | solution.py:20
  78.3 28.5 %collective-permute-start.19 = (bf16[704,512]{1,0:T(8,128)(2,1)}, bf16[704,512]{1,0:T(8,128)(2,1)}, u32[]{:S(2)}, u32[]{:S(2)}) collective-permute-start(bf16[704,512]{1,0:T(8,128)(2,1)} %copy_bitcast_fusion), channel_id=1, source_target_pairs={{4,0},{0,4},{5,1},{1,5},{6,2},{2,6},{7,3},{3,7},{12,8},{8,12},{13,... | collective-permute-start | bytes 2162696 | tf_op jit(solution)/shard_map/ppermute | solution.py:20
  87.8 37.1 %collective-permute-start.20 = (bf16[704,512]{1,0:T(8,128)(2,1)}, bf16[704,512]{1,0:T(8,128)(2,1)S(1)}, u32[]{:S(2)}, u32[]{:S(2)}) collective-permute-start(bf16[704,512]{1,0:T(8,128)(2,1)} %copy_bitcast_fusion), channel_id=1, source_target_pairs={{6,0},{4,2},{2,4},{0,6},{7,1},{5,3},{3,5},{1,7},{14,8},{12,10},{10... | collective-permute-start | bytes 2162696 | tf_op jit(solution)/shard_map/ppermute | solution.py:328
  111.1 3.2 %collective-permute-start.24 = (bf16[256,512]{1,0:T(8,128)(2,1)S(1)}, bf16[256,512]{1,0:T(8,128)(2,1)S(1)}, u32[]{:S(2)}, u32[]{:S(2)}) collective-permute-start(bf16[256,512]{1,0:T(8,128)(2,1)S(1)} %get-tuple-element.183), channel_id=1, source_target_pairs={{1,0},{0,1},{3,2},{2,3},{5,4},{4,5},{7,6},{6,7},{9,8},{8,9},{11,10... | collective-permute-start | bytes 786440 | tf_op jit(solution)/shard_map/ppermute | solution.py:20
  111.2 3.1 %collective-permute-start.23 = (bf16[256,512]{1,0:T(8,128)(2,1)S(1)}, bf16[256,512]{1,0:T(8,128)(2,1)S(1)}, u32[]{:S(2)}, u32[]{:S(2)}) collective-permute-start(bf16[256,512]{1,0:T(8,128)(2,1)S(1)} %get-tuple-element.184), channel_id=1, source_target_pairs={{1,0},{0,1},{3,2},{2,3},{5,4},{4,5},{7,6},{6,7},{9,8},{8,9},{11,10... | collective-permute-start | bytes 786440 | tf_op jit(solution)/shard_map/ppermute | solution.py:20
  116.5 8.4 %collective-permute-start.25 = (bf16[256,512]{1,0:T(8,128)(2,1)S(1)}, bf16[256,512]{1,0:T(8,128)(2,1)S(1)}, u32[]{:S(2)}, u32[]{:S(2)}) collective-permute-start(bf16[256,512]{1,0:T(8,128)(2,1)S(1)} %get-tuple-element.181), channel_id=1, source_target_pairs={{8,0},{0,8},{24,16},{16,24},{9,1},{1,9},{25,17},{17,25},{10,2},{2,... | collective-permute-start | bytes 786440 | tf_op jit(solution)/shard_map/ppermute | solution.py:28
  128.5 4.0 %collective-permute-start.27 = (bf16[256,512]{1,0:T(8,128)(2,1)S(1)}, bf16[256,512]{1,0:T(8,128)(2,1)S(1)}, u32[]{:S(2)}, u32[]{:S(2)}) collective-permute-start(bf16[256,512]{1,0:T(8,128)(2,1)S(1)} %get-tuple-element.165), channel_id=1, source_target_pairs={{1,0},{0,1},{3,2},{2,3},{5,4},{4,5},{7,6},{6,7},{9,8},{8,9},{11,10... | collective-permute-start | bytes 786440 | tf_op jit(solution)/shard_map/ppermute | solution.py:20
  129.0 3.5 %collective-permute-start.28 = (bf16[256,512]{1,0:T(8,128)(2,1)S(1)}, bf16[256,512]{1,0:T(8,128)(2,1)S(1)}, u32[]{:S(2)}, u32[]{:S(2)}) collective-permute-start(bf16[256,512]{1,0:T(8,128)(2,1)S(1)} %get-tuple-element.166), channel_id=1, source_target_pairs={{1,0},{0,1},{3,2},{2,3},{5,4},{4,5},{7,6},{6,7},{9,8},{8,9},{11,10... | collective-permute-start | bytes 786440 | tf_op jit(solution)/shard_map/ppermute | solution.py:20
  129.1 3.4 %collective-permute-start.29 = (bf16[256,512]{1,0:T(8,128)(2,1)S(1)}, bf16[256,512]{1,0:T(8,128)(2,1)S(1)}, u32[]{:S(2)}, u32[]{:S(2)}) collective-permute-start(bf16[256,512]{1,0:T(8,128)(2,1)S(1)} %get-tuple-element.167), channel_id=1, source_target_pairs={{1,0},{0,1},{3,2},{2,3},{5,4},{4,5},{7,6},{6,7},{9,8},{8,9},{11,10... | collective-permute-start | bytes 786440 | tf_op jit(solution)/shard_map/ppermute | solution.py:20
  129.5 13.5 %collective-permute-start.31 = (bf16[256,512]{1,0:T(8,128)(2,1)S(1)}, bf16[256,512]{1,0:T(8,128)(2,1)S(1)}, u32[]{:S(2)}, u32[]{:S(2)}) collective-permute-start(bf16[256,512]{1,0:T(8,128)(2,1)S(1)} %get-tuple-element.179), channel_id=1, source_target_pairs={{8,0},{0,8},{24,16},{16,24},{9,1},{1,9},{25,17},{17,25},{10,2},{2,... | collective-permute-start | bytes 786440 | tf_op jit(solution)/shard_map/ppermute | solution.py:28
  131.2 14.7 %collective-permute-start.32 = (bf16[256,512]{1,0:T(8,128)(2,1)S(1)}, bf16[256,512]{1,0:T(8,128)(2,1)S(1)}, u32[]{:S(2)}, u32[]{:S(2)}) collective-permute-start(bf16[256,512]{1,0:T(8,128)(2,1)S(1)} %add_convert_fusion.3), channel_id=1, source_target_pairs={{16,0},{24,8},{0,16},{8,24},{17,1},{25,9},{1,17},{9,25},{18,2},{26... | collective-permute-start | bytes 786440 | tf_op jit(solution)/shard_map/ppermute | solution.py:28
  136.2 13.7 %collective-permute-start.30 = (bf16[256,512]{1,0:T(8,128)(2,1)S(1)}, bf16[256,512]{1,0:T(8,128)(2,1)S(1)}, u32[]{:S(2)}, u32[]{:S(2)}) collective-permute-start(bf16[256,512]{1,0:T(8,128)(2,1)S(1)} %get-tuple-element.168), channel_id=1, source_target_pairs={{8,0},{0,8},{24,16},{16,24},{9,1},{1,9},{25,17},{17,25},{10,2},{2,... | collective-permute-start | bytes 786440 | tf_op jit(solution)/shard_map/ppermute | solution.py:28
  136.9 21.6 %collective-permute-start.33 = (bf16[256,512]{1,0:T(8,128)(2,1)S(1)}, bf16[256,512]{1,0:T(8,128)(2,1)S(1)}, u32[]{:S(2)}, u32[]{:S(2)}) collective-permute-start(bf16[256,512]{1,0:T(8,128)(2,1)S(1)} %get-tuple-element.174), channel_id=1, source_target_pairs={{8,0},{0,8},{24,16},{16,24},{9,1},{1,9},{25,17},{17,25},{10,2},{2,... | collective-permute-start | bytes 786440 | tf_op jit(solution)/shard_map/ppermute | solution.py:28
  150.0 13.2 %collective-permute-start.34 = (bf16[256,512]{1,0:T(8,128)(2,1)S(1)}, bf16[256,512]{1,0:T(8,128)(2,1)S(1)}, u32[]{:S(2)}, u32[]{:S(2)}) collective-permute-start(bf16[256,512]{1,0:T(8,128)(2,1)S(1)} %add_convert_fusion.2), channel_id=1, source_target_pairs={{16,0},{24,8},{0,16},{8,24},{17,1},{25,9},{1,17},{9,25},{18,2},{26... | collective-permute-start | bytes 786440 | tf_op jit(solution)/shard_map/ppermute | solution.py:28
  (29 other events, 223.0 us)

commit v2 on v1

--- a/solution.py
+++ b/solution.py
@@ -288,20 +288,19 @@
     owner = jnp.concatenate(owners)[None, :]
     small = [bases, prompts, owner, adapter_norm_gain[None], expert_norm_gain[None], router_rows]
 
-    gate, up, small, crossed, ups, tokens, other_maps = together(gate, up, small, crossed, ups, tokens, other_maps)
     passed = [from_offset(c, "lo", los, j) for c in crossed for j in range(shares)]
+    gate, up, small, ups, tokens, other_maps = together(gate, up, small, ups, tokens, other_maps)
     gates = {(i, 0): from_offset(gate, "ex", exs, i) for i in ex_far}
     if lines == 4:
         tokens[3] = across(tokens[2], lines, 1)
-
-    gate, up, passed, gates, tokens, down = together(gate, up, passed, gates, tokens, expert_down_weight)
+    held = [v for p in passed for v in (p, from_offset(p, "core", CORES, 1))]
+
+    gates, tokens, held, gate, up, down = together(gates, tokens, held, gate, up, expert_down_weight)
+    gates.update({(0, j): from_offset(gate, "lo", los, j) for j in lo_far})
+    ups.update({(i, 0): from_offset(up, "ex", exs, i) for i in ex_far})
     down = lax.all_to_all(
         down.reshape(lines, down_rows // lines, cols), "line", split_axis=0, concat_axis=0, tiled=True
     )
-    held = [v for p in passed for v in (p, from_offset(p, "core", CORES, 1))]
-    held, tokens, gate, up = together(held, tokens, gate, up)
-    gates.update({(0, j): from_offset(gate, "lo", los, j) for j in lo_far})
-    ups.update({(i, 0): from_offset(up, "ex", exs, i) for i in ex_far})
     mixed, w_own, x_own = front(*small, maps + other_maps, held, [tokens[m] for m in range(lines)])
 
     gates, ups, gate, up, x_own, w_own = together(gates, ups, gate, up, x_own, w_own)

time: 165 us -> 161 us (0.976)
  waiting for transfers between devices: 64.1 us -> 57.7 us
    ppermute x25, waiting for transfers between devices: 24.2 us -> 18.2 us  [from_offset(): lax.ppermute(value, axis, [((i + offset) % size, i) for i in range(size)])]
    ppermute x9, starting transfers between devices: 14.5 us -> 16.9 us  [across(): lax.ppermute(value, 'line', [(i ^ mask, i) for i in range(size)])]
    ppermute x25, starting transfers between devices: 15.7 us -> 13.8 us  [from_offset(): lax.ppermute(value, axis, [((i + offset) % size, i) for i in range(size)])]
    unnamed x50 -> x48, local copies, waits for them, and re-layouts: 4.34 us -> 4.35 us
  transfers between devices with their start and end apart: 36 -> 36, of which waited for: 16 -> 13; matrix products, arithmetic and copies ran while one was open for 10% -> 11% of each run, Pallas kernels for 22% -> 23%
where the time goes in v2:
time: 161 us; the launch traced here: 160 us
  waiting for transfers between devices  57.7 us (36%)
  Pallas kernels  40.7 us (25%)
  starting transfers between devices  37.2 us (23%)
  local copies, waits for them, and re-layouts  9.98 us (6%)
  matrix products  8.33 us (5%)
  other arithmetic  5.27 us (3%)
    ppermute x9, waiting for transfers between devices, across(): lax.ppermute(value, 'line', [(i ^ mask, i) for i in range(size)])  36.6 us
    pallas_call x4, Pallas kernels, hidden(): pl.pallas_call(functools.partial(hidden_kernel, los, tiles), grid=(tiles,...  21.8 us
    ppermute x25, waiting for transfers between devices, from_offset(): lax.ppermute(value, axis, [((i + offset) % size, i) for i in range(size)])  18.2 us
    ppermute x9, starting transfers between devices, across(): lax.ppermute(value, 'line', [(i ^ mask, i) for i in range(size)])  16.9 us
    ppermute x25, starting transfers between devices, from_offset(): lax.ppermute(value, axis, [((i + offset) % size, i) for i in range(size)])  13.8 us
    pallas_call x1, Pallas kernels, front(): pl.pallas_call(functools.partial(front_kernel, len(pairs) // 2, len(piece...  10.6 us
    dot_general x4, matrix products, dot(): lax.dot_general(a, b, (((1,), (rhs_dim,)), ((), ())), preferred_element_t...  8.33 us
    pallas_call x2, Pallas kernels, project(): pl.pallas_call(functools.partial(project_kernel, len(acts), lines, bool(a...  7.25 us
  transfers between devices with their start and end apart: 36, of which 13 were waited for; matrix products, arithmetic and copies ran while one was open for 11% of the time, Pallas kernels for 23%

profile of v2, /device:TPU:0, one launch (start us, length us, event | category | flops | bytes accessed | tf_op | source)
XLA Modules:
  0.0 159.8 jit_solution(4967032600099390503)
XLA Ops:
  1.8 3.1 %collective-permute-start.1 = (bf16[272,1024]{1,0:T(8,128)(2,1)S(1)}, bf16[272,1024]{1,0:T(8,128)(2,1)}, u32[]{:S(2)}, u32[]{:S(2)}) collective-permute-start(bf16[272,1024]{1,0:T(8,128)(2,1)S(1)} %fusion.1.refs_8_), channel_id=1, source_target_pairs={{8,0},{0,8},{24,16},{16,24},{9,1},{1,9},{25,17},{17,25},{10,2},{2,... | collective-permute-start | bytes 1671176 | tf_op jit(solution)/shard_map/ppermute | solution.py:28
  4.9 2.6 %collective-permute-start.2 = (bf16[272,1024]{1,0:T(8,128)(2,1)S(1)}, bf16[272,1024]{1,0:T(8,128)(2,1)}, u32[]{:S(2)}, u32[]{:S(2)}) collective-permute-start(bf16[272,1024]{1,0:T(8,128)(2,1)S(1)} %fusion.1.refs_8_), channel_id=1, source_target_pairs={{16,0},{24,8},{0,16},{8,24},{17,1},{25,9},{1,17},{9,25},{18,2},{26... | collective-permute-start | bytes 1671176 | tf_op jit(solution)/shard_map/ppermute | solution.py:28
  10.6 1.8 %fusion.2 = bf16[2,128,1024]{2,1,0:T(8,128)(2,1)} fusion(s32[]{:T(128)S(6)} %select_n.55, bf16[1,256,1024]{2,1,0:T(8,128)(2,1)S(1)} %bitcast.41, bf16[1,256,1024]{2,1,0:T(8,128)(2,1)} %bitcast.42), kind=kLoop, calls=%fused_computation.10 | loop fusion | flops 1048576 | bytes 1572868 | tf_op jit(solution)/shard_map/stack | solution.py:266
  17.2 9.8 %collective-permute-done.7.refs_4_ = bf16[2,128,1024]{2,1,0:T(8,128)(2,1)} collective-permute-done((bf16[2,128,1024]{2,1,0:T(8,128)(2,1)}, bf16[2,128,1024]{2,1,0:T(8,128)(2,1)}, u32[]{:S(2)}, u32[]{:S(2)}) %collective-permute-start.7) | collective-permute-done | bytes 524320 | tf_op jit(solution)/shard_map/ppermute | solution.py:20
  29.4 2.5 %collective-permute-done.2.refs_10_ = bf16[272,1024]{1,0:T(8,128)(2,1)} collective-permute-done((bf16[272,1024]{1,0:T(8,128)(2,1)S(1)}, bf16[272,1024]{1,0:T(8,128)(2,1)}, u32[]{:S(2)}, u32[]{:S(2)}) %collective-permute-start.2) | collective-permute-done | bytes 557088 | tf_op jit(solution)/shard_map/ppermute | solution.py:28
  33.9 6.9 %collective-permute-done.9.refs_6_ = bf16[2,128,1024]{2,1,0:T(8,128)(2,1)S(1)} collective-permute-done((bf16[2,128,1024]{2,1,0:T(8,128)(2,1)}, bf16[2,128,1024]{2,1,0:T(8,128)(2,1)S(1)}, u32[]{:S(2)}, u32[]{:S(2)}) %collective-permute-start.9) | collective-permute-done | bytes 524320 | tf_op jit(solution)/shard_map/ppermute | solution.py:20
  40.8 4.7 %collective-permute-done.6.refs_11_ = bf16[272,1024]{1,0:T(8,128)(2,1)S(1)} collective-permute-done((bf16[272,1024]{1,0:T(8,128)(2,1)}, bf16[272,1024]{1,0:T(8,128)(2,1)S(1)}, u32[]{:S(2)}, u32[]{:S(2)}) %collective-permute-start.6) | collective-permute-done | bytes 557088 | tf_op jit(solution)/shard_map/ppermute | solution.py:28
  47.0 1.8 %collective-permute-start.11 = (bf16[352,1024]{1,0:T(8,128)(2,1)S(1)}, bf16[352,1024]{1,0:T(8,128)(2,1)}, u32[]{:S(2)}, u32[]{:S(2)}) collective-permute-start(bf16[352,1024]{1,0:T(8,128)(2,1)S(1)} %get-tuple-element.114.refs_3_), channel_id=1, source_target_pairs={{4,0},{0,4},{5,1},{1,5},{6,2},{2,6},{7,3},{3,7},{12,8},{8,12},{13,... | collective-permute-start | bytes 2162696 | tf_op jit(solution)/shard_map/ppermute | solution.py:20
  48.8 2.1 %collective-permute-start.12 = (bf16[352,1024]{1,0:T(8,128)(2,1)S(1)}, bf16[352,1024]{1,0:T(8,128)(2,1)S(1)}, u32[]{:S(2)}, u32[]{:S(2)}) collective-permute-start(bf16[352,1024]{1,0:T(8,128)(2,1)S(1)} %get-tuple-element.116.refs_5_), channel_id=1, source_target_pairs={{2,0},{0,2},{3,1},{1,3},{6,4},{4,6},{7,5},{5,7},{10,8},{8,10},{11,... | collective-permute-start | bytes 2162696 | tf_op jit(solution)/shard_map/ppermute | solution.py:20
  50.9 4.2 %all-to-all-start = ((bf16[4,704,128]{2,1,0:T(8,128)(2,1)}), bf16[4,704,128]{2,1,0:T(8,128)(2,1)}, u32[]{:S(2)}, u32[]{:S(2)}) async-start(bf16[4,704,128]{2,1,0:T(8,128)(2,1)} %bitcast.45), calls=%async_computation | async-start | bytes 1441792 | tf_op jit(solution)/shard_map/all_to_all | solution.py:301
  55.1 10.6 %front.1 = (bf16[256,1024]{1,0:T(8,128)(2,1)}, f32[1024,128]{1,0:T(8,128)}, bf16[512,1024]{1,0:T(8,128)(2,1)}, bf16[512,1024]{1,0:T(8,128)(2,1)}) custom-call(s32[4]{0:T(128)} %add_multiply_fusion.base_ref, s32[3,48]{1,0:T(4,128)} %pad_add_fusion.prompts_ref, s32[1,1024]{1,0:T(1,128)} %bitcast.47, bf16[1,1024]{1,0:T(2,128)(2,1)} %broadcast_in_dim.31.gain_a_ref, ...), custom_call_target="tpu_custom_call" | custom-call | flops 1 | bytes 1 | tf_op jit(solution)/shard_map/front/pallas_call | solution.py:110
  67.8 2.9 %all-to-all-done = bf16[4,704,128]{2,1,0:T(8,128)(2,1)} async-done(((bf16[4,704,128]{2,1,0:T(8,128)(2,1)}), bf16[4,704,128]{2,1,0:T(8,128)(2,1)}, u32[]{:S(2)}, u32[]{:S(2)}) %all-to-all-start) | async-done | bytes 720928 | tf_op jit(solution)/shard_map/all_to_all | solution.py:301
  70.7 2.0 %copy_bitcast_fusion = bf16[704,512]{1,0:T(8,128)(2,1)} fusion(bf16[4,704,128]{2,1,0:T(8,128)(2,1)} %all-to-all-done), kind=kLoop, calls=%fused_computation.6 | loop fusion | bytes 1441792 | tf_op jit(solution)/shard_map/reshape | solution.py:320
  77.5 5.0 %hidden.4.refs_0_ = bf16[1024,704]{1,0:T(8,128)(2,1)S(1)} custom-call(s32[2]{0:T(128)S(1)} %pad_add_fusion.1.at_ref, bf16[512,1024]{1,0:T(8,128)(2,1)S(1)} %copy-done, bf16[512,1024]{1,0:T(8,128)(2,1)S(1)} %copy-done.1, f32[1024,128]{1,0:T(8,128)S(1)} %copy-done.7, bf16[352,1024]{1,0:T(8,128)(2,1)S(1)} %get-tuple-element.114.refs_3_, ...), custom_call_target="tpu_custom_call" | custom-call | flops 1 | bytes 1 | tf_op jit(solution)/shard_map/hidden/pallas_call | solution.py:152
  82.6 2.4 %collective-permute-start.20 = (bf16[704,512]{1,0:T(8,128)(2,1)}, bf16[704,512]{1,0:T(8,128)(2,1)S(1)}, u32[]{:S(2)}, u32[]{:S(2)}) collective-permute-start(bf16[704,512]{1,0:T(8,128)(2,1)} %copy_bitcast_fusion), channel_id=1, source_target_pairs={{6,0},{4,2},{2,4},{0,6},{7,1},{5,3},{3,5},{1,7},{14,8},{12,10},{10... | collective-permute-start | bytes 2162696 | tf_op jit(solution)/shard_map/ppermute | solution.py:327
  84.9 5.4 %hidden.5.refs_0_ = bf16[1024,704]{1,0:T(8,128)(2,1)S(1)} custom-call(s32[2]{0:T(128)S(1)} %pad_add_fusion.1.at_ref, bf16[512,1024]{1,0:T(8,128)(2,1)S(1)} %collective-permute-done.13.refs_0_, bf16[512,1024]{1,0:T(8,128)(2,1)} %collective-permute-done.14.refs_1_, f32[1024,128]{1,0:T(8,128)} %collective-permute-done.15.refs_2_, ...), custom_call_target="tpu_custom_call" | custom-call | flops 1 | bytes 1 | tf_op jit(solution)/shard_map/hidden/pallas_call | solution.py:152
  90.4 5.4 %hidden.6.refs_1_ = bf16[1024,704]{1,0:T(8,128)(2,1)S(1)} custom-call(s32[2]{0:T(128)S(1)} %pad_add_fusion.2.at_ref, bf16[512,1024]{1,0:T(8,128)(2,1)S(1)} %copy-done, bf16[512,1024]{1,0:T(8,128)(2,1)S(1)} %copy-done.1, f32[1024,128]{1,0:T(8,128)S(1)} %copy-done.8, bf16[352,1024]{1,0:T(8,128)(2,1)} %collective-permute-done.5.refs_3_, ...), custom_call_target="tpu_custom_call" | custom-call | flops 1 | bytes 1 | tf_op jit(solution)/shard_map/hidden/pallas_call | solution.py:152
  95.8 6.0 %hidden.7.refs_1_ = bf16[1024,704]{1,0:T(8,128)(2,1)S(1)} custom-call(s32[2]{0:T(128)S(1)} %pad_add_fusion.2.at_ref, bf16[512,1024]{1,0:T(8,128)(2,1)S(1)} %collective-permute-done.13.refs_0_, bf16[512,1024]{1,0:T(8,128)(2,1)} %collective-permute-done.14.refs_1_, f32[1024,128]{1,0:T(8,128)} %collective-permute-done.15.refs_2_, ...), custom_call_target="tpu_custom_call" | custom-call | flops 1 | bytes 1 | tf_op jit(solution)/shard_map/hidden/pallas_call | solution.py:152
  101.9 2.1 %fusion.6 = f32[1024,512]{1,0:T(8,128)S(1)} fusion(bf16[1024,704]{1,0:T(8,128)(2,1)S(1)} %hidden.7.refs_1_, bf16[704,512]{1,0:T(8,128)(2,1)} %collective-permute-done.18), kind=kOutput, calls=%fused_computation.34 | convolution fusion | flops 738197504 | bytes 4259840 | tf_op jit(solution)/shard_map/dot_general | solution.py:32
  103.9 2.1 %add_convert_fusion.1 = bf16[1024,512]{1,0:T(8,128)(2,1)S(1)} fusion(f32[1024,512]{1,0:T(8,128)S(1)} %fusion.6, bf16[1024,704]{1,0:T(8,128)(2,1)S(1)} %hidden.5.refs_0_, bf16[704,512]{1,0:T(8,128)(2,1)} %copy_bitcast_fusion), kind=kOutput, calls=%fused_computation.1 | convolution fusion | flops 739246080 | bytes 5308416 | tf_op jit(solution)/shard_map/dot_general | solution.py:32
  107.2 2.1 %fusion.5 = f32[1024,512]{1,0:T(8,128)S(1)} fusion(bf16[1024,704]{1,0:T(8,128)(2,1)S(1)} %hidden.6.refs_1_, bf16[704,512]{1,0:T(8,128)(2,1)} %collective-permute-done.18), kind=kOutput, calls=%fused_computation.33 | convolution fusion | flops 738197504 | bytes 4259840 | tf_op jit(solution)/shard_map/dot_general | solution.py:32
  109.3 2.1 %add_convert_fusion = bf16[1024,512]{1,0:T(8,128)(2,1)S(1)} fusion(f32[1024,512]{1,0:T(8,128)S(1)} %fusion.5, bf16[256,512]{1,0:T(8,128)(2,1)S(1)} %collective-permute-done.24, bf16[256,512]{1,0:T(8,128)(2,1)S(1)} %collective-permute-done.23, bf16[256,512]{1,0:T(8,128)(2,1)S(1)} %collective-permute-done.22, bf16[256,512]{1,0:T(8,128)(2,1)S(1)} %collective-permute-done.21, ...), kind=kOutput, calls=%fused_computation | convolution fusion | flops 743964672 | bytes 6356992 | tf_op jit(solution)/shard_map/dot_general | solution.py:32
  111.5 2.2 %collective-permute-start.25 = (bf16[256,512]{1,0:T(8,128)(2,1)S(1)}, bf16[256,512]{1,0:T(8,128)(2,1)S(1)}, u32[]{:S(2)}, u32[]{:S(2)}) collective-permute-start(bf16[256,512]{1,0:T(8,128)(2,1)S(1)} %get-tuple-element.163), channel_id=1, source_target_pairs={{8,0},{0,8},{24,16},{16,24},{9,1},{1,9},{25,17},{17,25},{10,2},{2,... | collective-permute-start | bytes 786440 | tf_op jit(solution)/shard_map/ppermute | solution.py:28
  113.7 6.5 %collective-permute-done.25 = bf16[256,512]{1,0:T(8,128)(2,1)S(1)} collective-permute-done((bf16[256,512]{1,0:T(8,128)(2,1)S(1)}, bf16[256,512]{1,0:T(8,128)(2,1)S(1)}, u32[]{:S(2)}, u32[]{:S(2)}) %collective-permute-start.25) | collective-permute-done | bytes 262176 | tf_op jit(solution)/shard_map/ppermute | solution.py:28
  120.4 3.6 %project.2 = (bf16[256,512]{1,0:T(8,128)(2,1)S(1)}, bf16[256,512]{1,0:T(8,128)(2,1)S(1)}, bf16[256,512]{1,0:T(8,128)(2,1)S(1)}, bf16[256,512]{1,0:T(8,128)(2,1)S(1)}) custom-call(bf16[1024,704]{1,0:T(8,128)(2,1)S(1)} %hidden.5.refs_0_, bf16[1024,704]{1,0:T(8,128)(2,1)S(1)} %hidden.7.refs_1_, bf16[704,512]{1,0:T(8,128)(2,1)} %collective-permute-done.19.refs_2_, ...), custom_call_target="tpu_custom_call" | custom-call | flops 1 | bytes 1 | tf_op jit(solution)/shard_map/project/pallas_call | solution.py:187
  126.8 2.2 %collective-permute-start.32 = (bf16[256,512]{1,0:T(8,128)(2,1)S(1)}, bf16[256,512]{1,0:T(8,128)(2,1)S(1)}, u32[]{:S(2)}, u32[]{:S(2)}) collective-permute-start(bf16[256,512]{1,0:T(8,128)(2,1)S(1)} %add_convert_fusion.3), channel_id=1, source_target_pairs={{16,0},{24,8},{0,16},{8,24},{17,1},{25,9},{1,17},{9,25},{18,2},{26... | collective-permute-start | bytes 786440 | tf_op jit(solution)/shard_map/ppermute | solution.py:28
  128.9 3.7 %project.3 = (bf16[256,512]{1,0:T(8,128)(2,1)S(1)}, bf16[256,512]{1,0:T(8,128)(2,1)S(1)}, bf16[256,512]{1,0:T(8,128)(2,1)S(1)}, bf16[256,512]{1,0:T(8,128)(2,1)S(1)}) custom-call(bf16[1024,704]{1,0:T(8,128)(2,1)S(1)} %hidden.4.refs_0_, bf16[1024,704]{1,0:T(8,128)(2,1)S(1)} %hidden.6.refs_1_, bf16[704,512]{1,0:T(8,128)(2,1)} %collective-permute-done.19.refs_2_, ...), custom_call_target="tpu_custom_call" | custom-call | flops 1 | bytes 1 | tf_op jit(solution)/shard_map/project/pallas_call | solution.py:187
  134.7 4.6 %collective-permute-done.31.refs_1_ = bf16[256,512]{1,0:T(8,128)(2,1)S(1)} collective-permute-done((bf16[256,512]{1,0:T(8,128)(2,1)S(1)}, bf16[256,512]{1,0:T(8,128)(2,1)S(1)}, u32[]{:S(2)}, u32[]{:S(2)}) %collective-permute-start.31) | collective-permute-done | bytes 262176 | tf_op jit(solution)/shard_map/ppermute | solution.py:28
  140.9 4.5 %collective-permute-done.30 = bf16[256,512]{1,0:T(8,128)(2,1)S(1)} collective-permute-done((bf16[256,512]{1,0:T(8,128)(2,1)S(1)}, bf16[256,512]{1,0:T(8,128)(2,1)S(1)}, u32[]{:S(2)}, u32[]{:S(2)}) %collective-permute-start.30) | collective-permute-done | bytes 262176 | tf_op jit(solution)/shard_map/ppermute | solution.py:28
  145.5 2.5 %collective-permute-start.34 = (bf16[256,512]{1,0:T(8,128)(2,1)S(1)}, bf16[256,512]{1,0:T(8,128)(2,1)S(1)}, u32[]{:S(2)}, u32[]{:S(2)}) collective-permute-start(bf16[256,512]{1,0:T(8,128)(2,1)S(1)} %add_convert_fusion.2), channel_id=1, source_target_pairs={{16,0},{24,8},{0,16},{8,24},{17,1},{25,9},{1,17},{9,25},{18,2},{26... | collective-permute-start | bytes 786440 | tf_op jit(solution)/shard_map/ppermute | solution.py:28
  148.0 6.9 %collective-permute-done.33.refs_4_ = bf16[256,512]{1,0:T(8,128)(2,1)S(1)} collective-permute-done((bf16[256,512]{1,0:T(8,128)(2,1)S(1)}, bf16[256,512]{1,0:T(8,128)(2,1)S(1)}, u32[]{:S(2)}, u32[]{:S(2)}) %collective-permute-start.33) | collective-permute-done | bytes 262176 | tf_op jit(solution)/shard_map/ppermute | solution.py:28
  154.9 3.8 %collective-permute-done.34.refs_5_ = bf16[256,512]{1,0:T(8,128)(2,1)S(1)} collective-permute-done((bf16[256,512]{1,0:T(8,128)(2,1)S(1)}, bf16[256,512]{1,0:T(8,128)(2,1)S(1)}, u32[]{:S(2)}, u32[]{:S(2)}) %collective-permute-start.34) | collective-permute-done | bytes 262176 | tf_op jit(solution)/shard_map/ppermute | solution.py:28
  (128 shorter events, 31.2 us)
Async XLA Ops:
  1.8 27.6 %collective-permute-start.1 = (bf16[272,1024]{1,0:T(8,128)(2,1)S(1)}, bf16[272,1024]{1,0:T(8,128)(2,1)}, u32[]{:S(2)}, u32[]{:S(2)}) collective-permute-start(bf16[272,1024]{1,0:T(8,128)(2,1)S(1)} %fusion.1.refs_8_), channel_id=1, source_target_pairs={{8,0},{0,8},{24,16},{16,24},{9,1},{1,9},{25,17},{17,25},{10,2},{2,... | collective-permute-start | bytes 1671176 | tf_op jit(solution)/shard_map/ppermute | solution.py:28
  4.9 27.1 %collective-permute-start.2 = (bf16[272,1024]{1,0:T(8,128)(2,1)S(1)}, bf16[272,1024]{1,0:T(8,128)(2,1)}, u32[]{:S(2)}, u32[]{:S(2)}) collective-permute-start(bf16[272,1024]{1,0:T(8,128)(2,1)S(1)} %fusion.1.refs_8_), channel_id=1, source_target_pairs={{16,0},{24,8},{0,16},{8,24},{17,1},{25,9},{1,17},{9,25},{18,2},{26... | collective-permute-start | bytes 1671176 | tf_op jit(solution)/shard_map/ppermute | solution.py:28
  9.0 23.0 %collective-permute-start = (bf16[352,1024]{1,0:T(8,128)(2,1)S(1)}, bf16[352,1024]{1,0:T(8,128)(2,1)S(1)}, u32[]{:S(2)}, u32[]{:S(2)}) collective-permute-start(bf16[352,1024]{1,0:T(8,128)(2,1)S(1)} %get-tuple-element.116.refs_5_), channel_id=1, source_target_pairs={{4,0},{0,4},{5,1},{1,5},{6,2},{2,6},{7,3},{3,7},{12,8},{8,12},{13,... | collective-permute-start | bytes 2162696 | tf_op jit(solution)/shard_map/ppermute | solution.py:20
  10.6 6.4 %collective-permute-start.3 = (bf16[256,1024]{1,0:T(8,128)(2,1)S(1)}, bf16[256,1024]{1,0:T(8,128)(2,1)}, u32[]{:S(2)}, u32[]{:S(2)}) collective-permute-start(bf16[256,1024]{1,0:T(8,128)(2,1)S(1)} %bitcast.40), channel_id=1, source_target_pairs={{1,0},{0,1},{3,2},{2,3},{5,4},{4,5},{7,6},{6,7},{9,8},{8,9},{11,10... | collective-permute-start | bytes 1572872 | tf_op jit(solution)/shard_map/ppermute | solution.py:20
  12.4 14.7 %collective-permute-start.7 = (bf16[2,128,1024]{2,1,0:T(8,128)(2,1)}, bf16[2,128,1024]{2,1,0:T(8,128)(2,1)}, u32[]{:S(2)}, u32[]{:S(2)}) collective-permute-start(bf16[2,128,1024]{2,1,0:T(8,128)(2,1)} %fusion.2), channel_id=1, source_target_pairs={{2,0},{0,2},{3,1},{1,3},{6,4},{4,6},{7,5},{5,7},{10,8},{8,10},{11,... | collective-permute-start | bytes 1572872 | tf_op jit(solution)/shard_map/ppermute | solution.py:20
  16.9 11.1 %collective-permute-start.4 = (bf16[256,1024]{1,0:T(8,128)(2,1)}, bf16[256,1024]{1,0:T(8,128)(2,1)S(1)}, u32[]{:S(2)}, u32[]{:S(2)}) collective-permute-start(bf16[256,1024]{1,0:T(8,128)(2,1)} %bitcast.43), channel_id=1, source_target_pairs={{1,0},{0,1},{3,2},{2,3},{5,4},{4,5},{7,6},{6,7},{9,8},{8,9},{11,10... | collective-permute-start | bytes 1572872 | tf_op jit(solution)/shard_map/ppermute | solution.py:20
  27.0 13.8 %collective-permute-start.9 = (bf16[2,128,1024]{2,1,0:T(8,128)(2,1)}, bf16[2,128,1024]{2,1,0:T(8,128)(2,1)S(1)}, u32[]{:S(2)}, u32[]{:S(2)}) collective-permute-start(bf16[2,128,1024]{2,1,0:T(8,128)(2,1)} %collective-permute-done.7.refs_4_), channel_id=1, source_target_pairs={{4,0},{0,4},{5,1},{1,5},{6,2},{2,6},{7,3},{3,7},{12,8},{8,12},{13,... | collective-permute-start | bytes 1572872 | tf_op jit(solution)/shard_map/ppermute | solution.py:20
  32.0 15.0 %collective-permute-start.5 = (bf16[352,1024]{1,0:T(8,128)(2,1)S(1)}, bf16[352,1024]{1,0:T(8,128)(2,1)}, u32[]{:S(2)}, u32[]{:S(2)}) collective-permute-start(bf16[352,1024]{1,0:T(8,128)(2,1)S(1)} %get-tuple-element.114.refs_3_), channel_id=1, source_target_pairs={{2,0},{0,2},{3,1},{1,3},{6,4},{4,6},{7,5},{5,7},{10,8},{8,10},{11,... | collective-permute-start | bytes 2162696 | tf_op jit(solution)/shard_map/ppermute | solution.py:20
  33.5 12.1 %collective-permute-start.6 = (bf16[272,1024]{1,0:T(8,128)(2,1)}, bf16[272,1024]{1,0:T(8,128)(2,1)S(1)}, u32[]{:S(2)}, u32[]{:S(2)}) collective-permute-start(bf16[272,1024]{1,0:T(8,128)(2,1)} %collective-permute-done.2.refs_10_), channel_id=1, source_target_pairs={{8,0},{0,8},{24,16},{16,24},{9,1},{1,9},{25,17},{17,25},{10,2},{2,... | collective-permute-start | bytes 1671176 | tf_op jit(solution)/shard_map/ppermute | solution.py:28
  33.9 6.9 %collective-permute-start.8 = (bf16[2,128,1024]{2,1,0:T(8,128)(2,1)}, bf16[2,128,1024]{2,1,0:T(8,128)(2,1)S(1)}, u32[]{:S(2)}, u32[]{:S(2)}) collective-permute-start(bf16[2,128,1024]{2,1,0:T(8,128)(2,1)} %collective-permute-done.7.refs_4_), channel_id=1, source_target_pairs={{1,0},{0,1},{3,2},{2,3},{5,4},{4,5},{7,6},{6,7},{9,8},{8,9},{11,10... | collective-permute-start | bytes 1572872 | tf_op jit(solution)/shard_map/ppermute | solution.py:20
  40.8 6.2 %collective-permute-start.10 = (bf16[2,128,1024]{2,1,0:T(8,128)(2,1)S(1)}, bf16[2,128,1024]{2,1,0:T(8,128)(2,1)S(1)}, u32[]{:S(2)}, u32[]{:S(2)}) collective-permute-start(bf16[2,128,1024]{2,1,0:T(8,128)(2,1)S(1)} %collective-permute-done.9.refs_6_), channel_id=1, source_target_pairs={{1,0},{0,1},{3,2},{2,3},{5,4},{4,5},{7,6},{6,7},{9,8},{8,9},{11,10... | collective-permute-start | bytes 1572872 | tf_op jit(solution)/shard_map/ppermute | solution.py:20
  47.0 18.7 %collective-permute-start.11 = (bf16[352,1024]{1,0:T(8,128)(2,1)S(1)}, bf16[352,1024]{1,0:T(8,128)(2,1)}, u32[]{:S(2)}, u32[]{:S(2)}) collective-permute-start(bf16[352,1024]{1,0:T(8,128)(2,1)S(1)} %get-tuple-element.114.refs_3_), channel_id=1, source_target_pairs={{4,0},{0,4},{5,1},{1,5},{6,2},{2,6},{7,3},{3,7},{12,8},{8,12},{13,... | collective-permute-start | bytes 2162696 | tf_op jit(solution)/shard_map/ppermute | solution.py:20
  48.8 16.9 %collective-permute-start.12 = (bf16[352,1024]{1,0:T(8,128)(2,1)S(1)}, bf16[352,1024]{1,0:T(8,128)(2,1)S(1)}, u32[]{:S(2)}, u32[]{:S(2)}) collective-permute-start(bf16[352,1024]{1,0:T(8,128)(2,1)S(1)} %get-tuple-element.116.refs_5_), channel_id=1, source_target_pairs={{2,0},{0,2},{3,1},{1,3},{6,4},{4,6},{7,5},{5,7},{10,8},{8,10},{11,... | collective-permute-start | bytes 2162696 | tf_op jit(solution)/shard_map/ppermute | solution.py:20
  50.9 19.8 %all-to-all-start = ((bf16[4,704,128]{2,1,0:T(8,128)(2,1)}), bf16[4,704,128]{2,1,0:T(8,128)(2,1)}, u32[]{:S(2)}, u32[]{:S(2)}) async-start(bf16[4,704,128]{2,1,0:T(8,128)(2,1)} %bitcast.45), calls=%async_computation | async-start | bytes 1441792 | tf_op jit(solution)/shard_map/all_to_all | solution.py:301
  66.5 6.7 %collective-permute-start.13 = (bf16[512,1024]{1,0:T(8,128)(2,1)}, bf16[512,1024]{1,0:T(8,128)(2,1)S(1)}, u32[]{:S(2)}, u32[]{:S(2)}) collective-permute-start(bf16[512,1024]{1,0:T(8,128)(2,1)} %get-tuple-element.121.refs_0_), channel_id=1, source_target_pairs={{1,0},{0,1},{3,2},{2,3},{5,4},{4,5},{7,6},{6,7},{9,8},{8,9},{11,10... | collective-permute-start | bytes 3145736 | tf_op jit(solution)/shard_map/ppermute | solution.py:20
  66.5 6.2 %collective-permute-start.15 = (f32[1024,128]{1,0:T(8,128)}, f32[1024,128]{1,0:T(8,128)}, u32[]{:S(2)}, u32[]{:S(2)}) collective-permute-start(f32[1024,128]{1,0:T(8,128)} %get-tuple-element.123.refs_2_), channel_id=1, source_target_pairs={{1,0},{0,1},{3,2},{2,3},{5,4},{4,5},{7,6},{6,7},{9,8},{8,9},{11,10... | collective-permute-start | bytes 1572872 | tf_op jit(solution)/shard_map/ppermute | solution.py:20
  67.1 15.5 %collective-permute-start.14 = (bf16[512,1024]{1,0:T(8,128)(2,1)}, bf16[512,1024]{1,0:T(8,128)(2,1)}, u32[]{:S(2)}, u32[]{:S(2)}) collective-permute-start(bf16[512,1024]{1,0:T(8,128)(2,1)} %get-tuple-element.122.refs_1_), channel_id=1, source_target_pairs={{1,0},{0,1},{3,2},{2,3},{5,4},{4,5},{7,6},{6,7},{9,8},{8,9},{11,10... | collective-permute-start | bytes 3145736 | tf_op jit(solution)/shard_map/ppermute | solution.py:20
  67.1 23.3 %collective-permute-start.16 = (bf16[352,1024]{1,0:T(8,128)(2,1)}, bf16[352,1024]{1,0:T(8,128)(2,1)}, u32[]{:S(2)}, u32[]{:S(2)}) collective-permute-start(bf16[352,1024]{1,0:T(8,128)(2,1)} %collective-permute-done.5.refs_3_), channel_id=1, source_target_pairs={{4,0},{0,4},{5,1},{1,5},{6,2},{2,6},{7,3},{3,7},{12,8},{8,12},{13,... | collective-permute-start | bytes 2162696 | tf_op jit(solution)/shard_map/ppermute | solution.py:20
  67.1 23.2 %collective-permute-start.17 = (bf16[352,1024]{1,0:T(8,128)(2,1)}, bf16[352,1024]{1,0:T(8,128)(2,1)}, u32[]{:S(2)}, u32[]{:S(2)}) collective-permute-start(bf16[352,1024]{1,0:T(8,128)(2,1)} %copy-done.2), channel_id=1, source_target_pairs={{2,0},{0,2},{3,1},{1,3},{6,4},{4,6},{7,5},{5,7},{10,8},{8,10},{11,... | collective-permute-start | bytes 2162696 | tf_op jit(solution)/shard_map/ppermute | solution.py:20
  72.8 29.1 %collective-permute-start.18 = (bf16[704,512]{1,0:T(8,128)(2,1)}, bf16[704,512]{1,0:T(8,128)(2,1)}, u32[]{:S(2)}, u32[]{:S(2)}) collective-permute-start(bf16[704,512]{1,0:T(8,128)(2,1)} %copy_bitcast_fusion), channel_id=1, source_target_pairs={{2,0},{0,2},{3,1},{1,3},{6,4},{4,6},{7,5},{5,7},{10,8},{8,10},{11,... | collective-permute-start | bytes 2162696 | tf_op jit(solution)/shard_map/ppermute | solution.py:20
  73.3 28.6 %collective-permute-start.19 = (bf16[704,512]{1,0:T(8,128)(2,1)}, bf16[704,512]{1,0:T(8,128)(2,1)}, u32[]{:S(2)}, u32[]{:S(2)}) collective-permute-start(bf16[704,512]{1,0:T(8,128)(2,1)} %copy_bitcast_fusion), channel_id=1, source_target_pairs={{4,0},{0,4},{5,1},{1,5},{6,2},{2,6},{7,3},{3,7},{12,8},{8,12},{13,... | collective-permute-start | bytes 2162696 | tf_op jit(solution)/shard_map/ppermute | solution.py:20
  82.6 37.8 %collective-permute-start.20 = (bf16[704,512]{1,0:T(8,128)(2,1)}, bf16[704,512]{1,0:T(8,128)(2,1)S(1)}, u32[]{:S(2)}, u32[]{:S(2)}) collective-permute-start(bf16[704,512]{1,0:T(8,128)(2,1)} %copy_bitcast_fusion), channel_id=1, source_target_pairs={{6,0},{4,2},{2,4},{0,6},{7,1},{5,3},{3,5},{1,7},{14,8},{12,10},{10... | collective-permute-start | bytes 2162696 | tf_op jit(solution)/shard_map/ppermute | solution.py:327
  106.1 3.2 %collective-permute-start.24 = (bf16[256,512]{1,0:T(8,128)(2,1)S(1)}, bf16[256,512]{1,0:T(8,128)(2,1)S(1)}, u32[]{:S(2)}, u32[]{:S(2)}) collective-permute-start(bf16[256,512]{1,0:T(8,128)(2,1)S(1)} %get-tuple-element.165), channel_id=1, source_target_pairs={{1,0},{0,1},{3,2},{2,3},{5,4},{4,5},{7,6},{6,7},{9,8},{8,9},{11,10... | collective-permute-start | bytes 786440 | tf_op jit(solution)/shard_map/ppermute | solution.py:20
  111.5 8.8 %collective-permute-start.25 = (bf16[256,512]{1,0:T(8,128)(2,1)S(1)}, bf16[256,512]{1,0:T(8,128)(2,1)S(1)}, u32[]{:S(2)}, u32[]{:S(2)}) collective-permute-start(bf16[256,512]{1,0:T(8,128)(2,1)S(1)} %get-tuple-element.163), channel_id=1, source_target_pairs={{8,0},{0,8},{24,16},{16,24},{9,1},{1,9},{25,17},{17,25},{10,2},{2,... | collective-permute-start | bytes 786440 | tf_op jit(solution)/shard_map/ppermute | solution.py:28
  124.0 4.9 %collective-permute-start.27 = (bf16[256,512]{1,0:T(8,128)(2,1)S(1)}, bf16[256,512]{1,0:T(8,128)(2,1)S(1)}, u32[]{:S(2)}, u32[]{:S(2)}) collective-permute-start(bf16[256,512]{1,0:T(8,128)(2,1)S(1)} %get-tuple-element.147), channel_id=1, source_target_pairs={{1,0},{0,1},{3,2},{2,3},{5,4},{4,5},{7,6},{6,7},{9,8},{8,9},{11,10... | collective-permute-start | bytes 786440 | tf_op jit(solution)/shard_map/ppermute | solution.py:20
  124.5 4.4 %collective-permute-start.28 = (bf16[256,512]{1,0:T(8,128)(2,1)S(1)}, bf16[256,512]{1,0:T(8,128)(2,1)S(1)}, u32[]{:S(2)}, u32[]{:S(2)}) collective-permute-start(bf16[256,512]{1,0:T(8,128)(2,1)S(1)} %get-tuple-element.148), channel_id=1, source_target_pairs={{1,0},{0,1},{3,2},{2,3},{5,4},{4,5},{7,6},{6,7},{9,8},{8,9},{11,10... | collective-permute-start | bytes 786440 | tf_op jit(solution)/shard_map/ppermute | solution.py:20
  124.6 4.3 %collective-permute-start.29 = (bf16[256,512]{1,0:T(8,128)(2,1)S(1)}, bf16[256,512]{1,0:T(8,128)(2,1)S(1)}, u32[]{:S(2)}, u32[]{:S(2)}) collective-permute-start(bf16[256,512]{1,0:T(8,128)(2,1)S(1)} %get-tuple-element.149), channel_id=1, source_target_pairs={{1,0},{0,1},{3,2},{2,3},{5,4},{4,5},{7,6},{6,7},{9,8},{8,9},{11,10... | collective-permute-start | bytes 786440 | tf_op jit(solution)/shard_map/ppermute | solution.py:20
  125.0 14.3 %collective-permute-start.31 = (bf16[256,512]{1,0:T(8,128)(2,1)S(1)}, bf16[256,512]{1,0:T(8,128)(2,1)S(1)}, u32[]{:S(2)}, u32[]{:S(2)}) collective-permute-start(bf16[256,512]{1,0:T(8,128)(2,1)S(1)} %get-tuple-element.161), channel_id=1, source_target_pairs={{8,0},{0,8},{24,16},{16,24},{9,1},{1,9},{25,17},{17,25},{10,2},{2,... | collective-permute-start | bytes 786440 | tf_op jit(solution)/shard_map/ppermute | solution.py:28
  126.8 14.2 %collective-permute-start.32 = (bf16[256,512]{1,0:T(8,128)(2,1)S(1)}, bf16[256,512]{1,0:T(8,128)(2,1)S(1)}, u32[]{:S(2)}, u32[]{:S(2)}) collective-permute-start(bf16[256,512]{1,0:T(8,128)(2,1)S(1)} %add_convert_fusion.3), channel_id=1, source_target_pairs={{16,0},{24,8},{0,16},{8,24},{17,1},{25,9},{1,17},{9,25},{18,2},{26... | collective-permute-start | bytes 786440 | tf_op jit(solution)/shard_map/ppermute | solution.py:28
  132.6 12.8 %collective-permute-start.30 = (bf16[256,512]{1,0:T(8,128)(2,1)S(1)}, bf16[256,512]{1,0:T(8,128)(2,1)S(1)}, u32[]{:S(2)}, u32[]{:S(2)}) collective-permute-start(bf16[256,512]{1,0:T(8,128)(2,1)S(1)} %get-tuple-element.150), channel_id=1, source_target_pairs={{8,0},{0,8},{24,16},{16,24},{9,1},{1,9},{25,17},{17,25},{10,2},{2,... | collective-permute-start | bytes 786440 | tf_op jit(solution)/shard_map/ppermute | solution.py:28
  133.3 21.6 %collective-permute-start.33 = (bf16[256,512]{1,0:T(8,128)(2,1)S(1)}, bf16[256,512]{1,0:T(8,128)(2,1)S(1)}, u32[]{:S(2)}, u32[]{:S(2)}) collective-permute-start(bf16[256,512]{1,0:T(8,128)(2,1)S(1)} %get-tuple-element.156), channel_id=1, source_target_pairs={{8,0},{0,8},{24,16},{16,24},{9,1},{1,9},{25,17},{17,25},{10,2},{2,... | collective-permute-start | bytes 786440 | tf_op jit(solution)/shard_map/ppermute | solution.py:28
  145.5 13.2 %collective-permute-start.34 = (bf16[256,512]{1,0:T(8,128)(2,1)S(1)}, bf16[256,512]{1,0:T(8,128)(2,1)S(1)}, u32[]{:S(2)}, u32[]{:S(2)}) collective-permute-start(bf16[256,512]{1,0:T(8,128)(2,1)S(1)} %add_convert_fusion.2), channel_id=1, source_target_pairs={{16,0},{24,8},{0,16},{8,24},{17,1},{25,9},{1,17},{9,25},{18,2},{26... | collective-permute-start | bytes 786440 | tf_op jit(solution)/shard_map/ppermute | solution.py:28
  (28 other events, 237.4 us)

commit v3 on v2

--- a/solution.py
+++ b/solution.py
@@ -165,37 +165,6 @@
     )(at, *xs, weight, *gates, *ups)
 
 
-def project_kernel(exs, lines, has_added, *refs):
-    act_refs, down_refs, refs = refs[:exs], refs[exs : 2 * exs], refs[2 * exs :]
-    added_refs, out_refs = (refs[:lines], refs[lines:]) if has_added else (None, refs)
-    total = dot(act_refs[0][...], down_refs[0][...])
-    for i in range(1, exs):
-        total = total + dot(act_refs[i][...], down_refs[i][...])
-    for k in range(lines):
-
-        def store(k=k):
-            value = total + added_refs[k][...].astype(jnp.float32) if has_added else total
-            out_refs[k][...] = value.astype(jnp.bfloat16)
-
-        pl.when(pl.program_id(0) == k)(store)
-
-
-def project(lines, acts, downs, added):
-    units, cols = downs[0].shape
-    rows = acts[0].shape[0] // lines
-    block = jax.ShapeDtypeStruct((rows, cols), jnp.bfloat16)
-    return pl.pallas_call(
-        functools.partial(project_kernel, len(acts), lines, bool(added)),
-        grid=(lines,),
-        out_shape=[block] * lines,
-        in_specs=[pl.BlockSpec((rows, units), lambda i: (i, 0))] * len(acts) + [whole(a) for a in (*downs, *added)],
-        out_specs=[whole(block)] * lines,
-        compiler_params=pltpu.CompilerParams(vmem_limit_bytes=VMEM // 3),
-        cost_estimate=brief(),
-        name="project",
-    )(*acts, *downs, *added)
-
-
 def final_kernel(los, lines, count, lo_ref, mixed_ref, *refs):
     out_ref = refs[-1]
     cols = mixed_ref.shape[1] // (los * lines)
@@ -340,15 +309,11 @@
         if joined is not None:
             near, far, of_piece, joined = together(near, far, of_piece, joined)
             parts[-1].append(across(joined, lines, 2))
-        if j == 0:
-            sums = lambda acts: sum(dot(a, d) for a, d in zip(acts, of_piece))
-            sent = sums(far).astype(jnp.bfloat16).reshape(lines, tok_rows, -1)
-            added = jnp.concatenate([from_offset(sent[k], "core", CORES, 1) for k in range(lines)])
-            total = (sums(near) + added.astype(jnp.float32)).astype(jnp.bfloat16)
-            home = list(total.reshape(lines, tok_rows, -1))
-        else:
-            sent = project(lines, far, of_piece, [])
-            home = project(lines, near, of_piece, [from_offset(v, "core", CORES, 1) for v in sent])
+        sums = lambda acts: sum(dot(a, d) for a, d in zip(acts, of_piece))
+        sent = sums(far).astype(jnp.bfloat16).reshape(lines, tok_rows, -1)
+        added = jnp.concatenate([from_offset(sent[k], "core", CORES, 1) for k in range(lines)])
+        total = (sums(near) + added.astype(jnp.float32)).astype(jnp.bfloat16)
+        home = list(total.reshape(lines, tok_rows, -1))
         if lines == 4:
             passing = across(home[3], lines, 1)
             if j > 0:

time: 161 us -> 159 us (0.988)
  Pallas kernels: 40.7 us -> 33.5 us
  matrix products: 8.33 us -> 14.4 us
  starting transfers between devices: 37.2 us -> 34.7 us
  waiting for transfers between devices: 57.7 us -> 59.8 us
    pallas_call x2 -> x0, Pallas kernels: 7.25 us -> none  [project(): pl.pallas_call(functools.partial(project_kernel, len(acts), lines, bool(a...]
    dot_general x4 -> x8, matrix products: 8.33 us -> 14.4 us  [dot(): lax.dot_general(a, b, (((1,), (rhs_dim,)), ((), ())), preferred_element_t...]
    ppermute x9, starting transfers between devices: 16.9 us -> 14.3 us  [across(): lax.ppermute(value, 'line', [(i ^ mask, i) for i in range(size)])]
    ppermute x9, waiting for transfers between devices: 36.6 us -> 38.8 us  [across(): lax.ppermute(value, 'line', [(i ^ mask, i) for i in range(size)])]
    unnamed x48 -> x50, local copies, waits for them, and re-layouts: 4.35 us -> 4.34 us
  transfers between devices with their start and end apart: 36 -> 36, of which waited for: 13 -> 13; matrix products, arithmetic and copies ran while one was open for 11% -> 15% of each run, Pallas kernels for 23% -> 20%
where the time goes in v3:
time: 159 us
  waiting for transfers between devices  59.8 us (38%)
  starting transfers between devices  34.7 us (22%)
  Pallas kernels  33.5 us (21%)
  matrix products  14.4 us (9%)
  local copies, waits for them, and re-layouts  10.1 us (6%)
  other arithmetic  5.36 us (3%)
    ppermute x9, waiting for transfers between devices, across(): lax.ppermute(value, 'line', [(i ^ mask, i) for i in range(size)])  38.8 us
    pallas_call x4, Pallas kernels, hidden(): pl.pallas_call(functools.partial(hidden_kernel, los, tiles), grid=(tiles,...  21.8 us
    ppermute x25, waiting for transfers between devices, from_offset(): lax.ppermute(value, axis, [((i + offset) % size, i) for i in range(size)])  18.2 us
    dot_general x8, matrix products, dot(): lax.dot_general(a, b, (((1,), (rhs_dim,)), ((), ())), preferred_element_t...  14.4 us
    ppermute x9, starting transfers between devices, across(): lax.ppermute(value, 'line', [(i ^ mask, i) for i in range(size)])  14.3 us
    ppermute x25, starting transfers between devices, from_offset(): lax.ppermute(value, axis, [((i + offset) % size, i) for i in range(size)])  13.9 us
    pallas_call x1, Pallas kernels, front(): pl.pallas_call(functools.partial(front_kernel, len(pairs) // 2, len(piece...  10.5 us
    unnamed x50, local copies, waits for them, and re-layouts  4.34 us
  transfers between devices with their start and end apart: 36, of which 13 were waited for; matrix products, arithmetic and copies ran while one was open for 15% of the time, Pallas kernels for 20%

profile of v3, /device:TPU:0, one launch (start us, length us, event | category | flops | bytes accessed | tf_op | source)
XLA Modules:
  0.0 158.5 jit_solution(6288974081972733453)
XLA Ops:
  1.9 3.1 %collective-permute-start.1 = (bf16[272,1024]{1,0:T(8,128)(2,1)S(1)}, bf16[272,1024]{1,0:T(8,128)(2,1)}, u32[]{:S(2)}, u32[]{:S(2)}) collective-permute-start(bf16[272,1024]{1,0:T(8,128)(2,1)S(1)} %fusion.1.refs_8_), channel_id=1, source_target_pairs={{8,0},{0,8},{24,16},{16,24},{9,1},{1,9},{25,17},{17,25},{10,2},{2,... | collective-permute-start | bytes 1671176 | tf_op jit(solution)/shard_map/ppermute | solution.py:28
  5.0 2.6 %collective-permute-start.2 = (bf16[272,1024]{1,0:T(8,128)(2,1)S(1)}, bf16[272,1024]{1,0:T(8,128)(2,1)}, u32[]{:S(2)}, u32[]{:S(2)}) collective-permute-start(bf16[272,1024]{1,0:T(8,128)(2,1)S(1)} %fusion.1.refs_8_), channel_id=1, source_target_pairs={{16,0},{24,8},{0,16},{8,24},{17,1},{25,9},{1,17},{9,25},{18,2},{26... | collective-permute-start | bytes 1671176 | tf_op jit(solution)/shard_map/ppermute | solution.py:28
  9.0 1.6 collective-permute-start
  10.6 1.8 %fusion.2 = bf16[2,128,1024]{2,1,0:T(8,128)(2,1)} fusion(s32[]{:T(128)S(6)} %select_n.55, bf16[1,256,1024]{2,1,0:T(8,128)(2,1)S(1)} %bitcast.49, bf16[1,256,1024]{2,1,0:T(8,128)(2,1)} %bitcast.50), kind=kLoop, calls=%fused_computation.12 | loop fusion | flops 1048576 | bytes 1572868 | tf_op jit(solution)/shard_map/stack | solution.py:235
  17.2 9.8 %collective-permute-done.7.refs_4_ = bf16[2,128,1024]{2,1,0:T(8,128)(2,1)} collective-permute-done((bf16[2,128,1024]{2,1,0:T(8,128)(2,1)}, bf16[2,128,1024]{2,1,0:T(8,128)(2,1)}, u32[]{:S(2)}, u32[]{:S(2)}) %collective-permute-start.7) | collective-permute-done | bytes 524320 | tf_op jit(solution)/shard_map/ppermute | solution.py:20
  29.6 2.5 %collective-permute-done.2.refs_10_ = bf16[272,1024]{1,0:T(8,128)(2,1)} collective-permute-done((bf16[272,1024]{1,0:T(8,128)(2,1)S(1)}, bf16[272,1024]{1,0:T(8,128)(2,1)}, u32[]{:S(2)}, u32[]{:S(2)}) %collective-permute-start.2) | collective-permute-done | bytes 557088 | tf_op jit(solution)/shard_map/ppermute | solution.py:28
  34.0 6.8 %collective-permute-done.9.refs_6_ = bf16[2,128,1024]{2,1,0:T(8,128)(2,1)S(1)} collective-permute-done((bf16[2,128,1024]{2,1,0:T(8,128)(2,1)}, bf16[2,128,1024]{2,1,0:T(8,128)(2,1)S(1)}, u32[]{:S(2)}, u32[]{:S(2)}) %collective-permute-start.9) | collective-permute-done | bytes 524320 | tf_op jit(solution)/shard_map/ppermute | solution.py:20
  40.8 4.8 %collective-permute-done.6.refs_11_ = bf16[272,1024]{1,0:T(8,128)(2,1)S(1)} collective-permute-done((bf16[272,1024]{1,0:T(8,128)(2,1)}, bf16[272,1024]{1,0:T(8,128)(2,1)S(1)}, u32[]{:S(2)}, u32[]{:S(2)}) %collective-permute-start.6) | collective-permute-done | bytes 557088 | tf_op jit(solution)/shard_map/ppermute | solution.py:28
  47.1 1.8 %collective-permute-start.11 = (bf16[352,1024]{1,0:T(8,128)(2,1)S(1)}, bf16[352,1024]{1,0:T(8,128)(2,1)}, u32[]{:S(2)}, u32[]{:S(2)}) collective-permute-start(bf16[352,1024]{1,0:T(8,128)(2,1)S(1)} %get-tuple-element.106.refs_3_), channel_id=1, source_target_pairs={{4,0},{0,4},{5,1},{1,5},{6,2},{2,6},{7,3},{3,7},{12,8},{8,12},{13,... | collective-permute-start | bytes 2162696 | tf_op jit(solution)/shard_map/ppermute | solution.py:20
  48.9 2.1 %collective-permute-start.12 = (bf16[352,1024]{1,0:T(8,128)(2,1)S(1)}, bf16[352,1024]{1,0:T(8,128)(2,1)S(1)}, u32[]{:S(2)}, u32[]{:S(2)}) collective-permute-start(bf16[352,1024]{1,0:T(8,128)(2,1)S(1)} %get-tuple-element.108.refs_5_), channel_id=1, source_target_pairs={{2,0},{0,2},{3,1},{1,3},{6,4},{4,6},{7,5},{5,7},{10,8},{8,10},{11,... | collective-permute-start | bytes 2162696 | tf_op jit(solution)/shard_map/ppermute | solution.py:20
  51.0 4.2 %all-to-all-start = ((bf16[4,704,128]{2,1,0:T(8,128)(2,1)}), bf16[4,704,128]{2,1,0:T(8,128)(2,1)}, u32[]{:S(2)}, u32[]{:S(2)}) async-start(bf16[4,704,128]{2,1,0:T(8,128)(2,1)} %bitcast.53), calls=%async_computation | async-start | bytes 1441792 | tf_op jit(solution)/shard_map/all_to_all | solution.py:270
  55.3 10.5 %front.1 = (bf16[256,1024]{1,0:T(8,128)(2,1)}, f32[1024,128]{1,0:T(8,128)}, bf16[512,1024]{1,0:T(8,128)(2,1)}, bf16[512,1024]{1,0:T(8,128)(2,1)}) custom-call(s32[4]{0:T(128)} %add_multiply_fusion.base_ref, s32[3,48]{1,0:T(4,128)} %pad_add_fusion.prompts_ref, s32[1,1024]{1,0:T(1,128)} %bitcast.55, bf16[1,1024]{1,0:T(2,128)(2,1)} %broadcast_in_dim.31.gain_a_ref, ...), custom_call_target="tpu_custom_call" | custom-call | flops 1 | bytes 1 | tf_op jit(solution)/shard_map/front/pallas_call | solution.py:110
  67.9 2.9 %all-to-all-done = bf16[4,704,128]{2,1,0:T(8,128)(2,1)} async-done(((bf16[4,704,128]{2,1,0:T(8,128)(2,1)}), bf16[4,704,128]{2,1,0:T(8,128)(2,1)}, u32[]{:S(2)}, u32[]{:S(2)}) %all-to-all-start) | async-done | bytes 720928 | tf_op jit(solution)/shard_map/all_to_all | solution.py:270
  70.8 2.0 %copy_bitcast_fusion = bf16[704,512]{1,0:T(8,128)(2,1)} fusion(bf16[4,704,128]{2,1,0:T(8,128)(2,1)} %all-to-all-done), kind=kLoop, calls=%fused_computation.8 | loop fusion | bytes 1441792 | tf_op jit(solution)/shard_map/reshape | solution.py:289
  77.6 5.0 %hidden.4 = bf16[1024,704]{1,0:T(8,128)(2,1)S(1)} custom-call(s32[2]{0:T(128)S(1)} %pad_add_fusion.1.at_ref, bf16[512,1024]{1,0:T(8,128)(2,1)S(1)} %copy-done, bf16[512,1024]{1,0:T(8,128)(2,1)S(1)} %copy-done.1, f32[1024,128]{1,0:T(8,128)S(1)} %copy-done.8, bf16[352,1024]{1,0:T(8,128)(2,1)S(1)} %get-tuple-element.106.refs_3_, ...), custom_call_target="tpu_custom_call" | custom-call | flops 1 | bytes 1 | tf_op jit(solution)/shard_map/hidden/pallas_call | solution.py:152
  82.7 2.4 %collective-permute-start.20 = (bf16[704,512]{1,0:T(8,128)(2,1)}, bf16[704,512]{1,0:T(8,128)(2,1)S(1)}, u32[]{:S(2)}, u32[]{:S(2)}) collective-permute-start(bf16[704,512]{1,0:T(8,128)(2,1)} %copy_bitcast_fusion), channel_id=1, source_target_pairs={{6,0},{4,2},{2,4},{0,6},{7,1},{5,3},{3,5},{1,7},{14,8},{12,10},{10... | collective-permute-start | bytes 2162696 | tf_op jit(solution)/shard_map/ppermute | solution.py:296
  85.1 5.4 %hidden.5 = bf16[1024,704]{1,0:T(8,128)(2,1)S(1)} custom-call(s32[2]{0:T(128)S(1)} %pad_add_fusion.1.at_ref, bf16[512,1024]{1,0:T(8,128)(2,1)S(1)} %collective-permute-done.13.refs_0_, bf16[512,1024]{1,0:T(8,128)(2,1)} %collective-permute-done.14.refs_1_, f32[1024,128]{1,0:T(8,128)} %collective-permute-done.15.refs_2_, ...), custom_call_target="tpu_custom_call" | custom-call | flops 1 | bytes 1 | tf_op jit(solution)/shard_map/hidden/pallas_call | solution.py:152
  90.5 5.4 %hidden.6 = bf16[1024,704]{1,0:T(8,128)(2,1)S(1)} custom-call(s32[2]{0:T(128)S(1)} %pad_add_fusion.2.at_ref, bf16[512,1024]{1,0:T(8,128)(2,1)S(1)} %copy-done, bf16[512,1024]{1,0:T(8,128)(2,1)S(1)} %copy-done.2, f32[1024,128]{1,0:T(8,128)S(1)} %copy-done.9, bf16[352,1024]{1,0:T(8,128)(2,1)} %collective-permute-done.5.refs_3_, ...), custom_call_target="tpu_custom_call" | custom-call | flops 1 | bytes 1 | tf_op jit(solution)/shard_map/hidden/pallas_call | solution.py:152
  95.9 6.0 %hidden.7 = bf16[1024,704]{1,0:T(8,128)(2,1)S(1)} custom-call(s32[2]{0:T(128)S(1)} %pad_add_fusion.2.at_ref, bf16[512,1024]{1,0:T(8,128)(2,1)S(1)} %collective-permute-done.13.refs_0_, bf16[512,1024]{1,0:T(8,128)(2,1)} %collective-permute-done.14.refs_1_, f32[1024,128]{1,0:T(8,128)} %collective-permute-done.15.refs_2_, ...), custom_call_target="tpu_custom_call" | custom-call | flops 1 | bytes 1 | tf_op jit(solution)/shard_map/hidden/pallas_call | solution.py:152
  102.0 2.1 %fusion.8 = f32[1024,512]{1,0:T(8,128)S(1)} fusion(bf16[1024,704]{1,0:T(8,128)(2,1)S(1)} %hidden.7, bf16[704,512]{1,0:T(8,128)(2,1)} %collective-permute-done.18), kind=kOutput, calls=%fused_computation.38 | convolution fusion | flops 738197504 | bytes 4259840 | tf_op jit(solution)/shard_map/dot_general | solution.py:32
  104.1 2.1 %add_convert_fusion.3 = bf16[1024,512]{1,0:T(8,128)(2,1)S(1)} fusion(f32[1024,512]{1,0:T(8,128)S(1)} %fusion.8, bf16[1024,704]{1,0:T(8,128)(2,1)S(1)} %hidden.5, bf16[704,512]{1,0:T(8,128)(2,1)} %copy_bitcast_fusion), kind=kOutput, calls=%fused_computation.3 | convolution fusion | flops 739246080 | bytes 5308416 | tf_op jit(solution)/shard_map/dot_general | solution.py:32
  107.4 2.1 %fusion.7 = f32[1024,512]{1,0:T(8,128)S(1)} fusion(bf16[1024,704]{1,0:T(8,128)(2,1)S(1)} %hidden.6, bf16[704,512]{1,0:T(8,128)(2,1)} %collective-permute-done.18), kind=kOutput, calls=%fused_computation.37 | convolution fusion | flops 738197504 | bytes 4259840 | tf_op jit(solution)/shard_map/dot_general | solution.py:32
  109.5 2.1 %add_convert_fusion.2 = bf16[1024,512]{1,0:T(8,128)(2,1)S(1)} fusion(f32[1024,512]{1,0:T(8,128)S(1)} %fusion.7, bf16[256,512]{1,0:T(8,128)(2,1)S(1)} %collective-permute-done.24, bf16[256,512]{1,0:T(8,128)(2,1)S(1)} %collective-permute-done.23, bf16[256,512]{1,0:T(8,128)(2,1)S(1)} %collective-permute-done.22, ...), kind=kOutput, calls=%fused_computation.2 | convolution fusion | flops 743964672 | bytes 6356992 | tf_op jit(solution)/shard_map/dot_general | solution.py:32
  111.7 2.1 %collective-permute-start.25 = (bf16[256,512]{1,0:T(8,128)(2,1)S(1)}, bf16[256,512]{1,0:T(8,128)(2,1)S(1)}, u32[]{:S(2)}, u32[]{:S(2)}) collective-permute-start(bf16[256,512]{1,0:T(8,128)(2,1)S(1)} %get-tuple-element.150), channel_id=1, source_target_pairs={{8,0},{0,8},{24,16},{16,24},{9,1},{1,9},{25,17},{17,25},{10,2},{2,... | collective-permute-start | bytes 786440 | tf_op jit(solution)/shard_map/ppermute | solution.py:28
  113.9 7.0 %collective-permute-done.25 = bf16[256,512]{1,0:T(8,128)(2,1)S(1)} collective-permute-done((bf16[256,512]{1,0:T(8,128)(2,1)S(1)}, bf16[256,512]{1,0:T(8,128)(2,1)S(1)}, u32[]{:S(2)}, u32[]{:S(2)}) %collective-permute-start.25) | collective-permute-done | bytes 262176 | tf_op jit(solution)/shard_map/ppermute | solution.py:28
  121.9 2.1 %add_convert_fusion.1 = bf16[1024,512]{1,0:T(8,128)(2,1)S(1)} fusion(f32[1024,512]{1,0:T(8,128)S(1)} %fusion.10, bf16[1024,704]{1,0:T(8,128)(2,1)S(1)} %hidden.5, bf16[704,512]{1,0:T(8,128)(2,1)} %collective-permute-done.19), kind=kOutput, calls=%fused_computation.1 | convolution fusion | flops 739246080 | bytes 5308416 | tf_op jit(solution)/shard_map/dot_general | solution.py:32
  126.2 2.9 %collective-permute-start.32 = (bf16[256,512]{1,0:T(8,128)(2,1)S(1)}, bf16[256,512]{1,0:T(8,128)(2,1)S(1)}, u32[]{:S(2)}, u32[]{:S(2)}) collective-permute-start(bf16[256,512]{1,0:T(8,128)(2,1)S(1)} %add_convert_fusion.5), channel_id=1, source_target_pairs={{16,0},{24,8},{0,16},{8,24},{17,1},{25,9},{1,17},{9,25},{18,2},{26... | collective-permute-start | bytes 786440 | tf_op jit(solution)/shard_map/ppermute | solution.py:28
  129.1 2.1 %add_convert_fusion = bf16[1024,512]{1,0:T(8,128)(2,1)S(1)} fusion(f32[1024,512]{1,0:T(8,128)S(1)} %fusion.9, bf16[256,512]{1,0:T(8,128)(2,1)S(1)} %collective-permute-done.29, bf16[256,512]{1,0:T(8,128)(2,1)S(1)} %collective-permute-done.28, bf16[256,512]{1,0:T(8,128)(2,1)S(1)} %collective-permute-done.27, bf16[256,512]{1,0:T(8,128)(2,1)S(1)} %collective-permute-done.26, ...), kind=kOutput, calls=%fused_computation | convolution fusion | flops 743964672 | bytes 6356992 | tf_op jit(solution)/shard_map/dot_general | solution.py:32
  133.4 8.0 %collective-permute-done.32.refs_2_ = bf16[256,512]{1,0:T(8,128)(2,1)S(1)} collective-permute-done((bf16[256,512]{1,0:T(8,128)(2,1)S(1)}, bf16[256,512]{1,0:T(8,128)(2,1)S(1)}, u32[]{:S(2)}, u32[]{:S(2)}) %collective-permute-start.32) | collective-permute-done | bytes 262176 | tf_op jit(solution)/shard_map/ppermute | solution.py:28
  141.4 3.4 %collective-permute-done.30 = bf16[256,512]{1,0:T(8,128)(2,1)S(1)} collective-permute-done((bf16[256,512]{1,0:T(8,128)(2,1)S(1)}, bf16[256,512]{1,0:T(8,128)(2,1)S(1)}, u32[]{:S(2)}, u32[]{:S(2)}) %collective-permute-start.30) | collective-permute-done | bytes 262176 | tf_op jit(solution)/shard_map/ppermute | solution.py:28
  145.8 5.5 %collective-permute-done.33.refs_4_ = bf16[256,512]{1,0:T(8,128)(2,1)S(1)} collective-permute-done((bf16[256,512]{1,0:T(8,128)(2,1)S(1)}, bf16[256,512]{1,0:T(8,128)(2,1)S(1)}, u32[]{:S(2)}, u32[]{:S(2)}) %collective-permute-start.33) | collective-permute-done | bytes 262176 | tf_op jit(solution)/shard_map/ppermute | solution.py:28
  151.3 6.0 %collective-permute-done.34.refs_5_ = bf16[256,512]{1,0:T(8,128)(2,1)S(1)} collective-permute-done((bf16[256,512]{1,0:T(8,128)(2,1)S(1)}, bf16[256,512]{1,0:T(8,128)(2,1)S(1)}, u32[]{:S(2)}, u32[]{:S(2)}) %collective-permute-start.34) | collective-permute-done | bytes 262176 | tf_op jit(solution)/shard_map/ppermute | solution.py:28
  (134 shorter events, 29.6 us)
Async XLA Ops:
  1.9 27.6 %collective-permute-start.1 = (bf16[272,1024]{1,0:T(8,128)(2,1)S(1)}, bf16[272,1024]{1,0:T(8,128)(2,1)}, u32[]{:S(2)}, u32[]{:S(2)}) collective-permute-start(bf16[272,1024]{1,0:T(8,128)(2,1)S(1)} %fusion.1.refs_8_), channel_id=1, source_target_pairs={{8,0},{0,8},{24,16},{16,24},{9,1},{1,9},{25,17},{17,25},{10,2},{2,... | collective-permute-start | bytes 1671176 | tf_op jit(solution)/shard_map/ppermute | solution.py:28
  5.0 27.1 %collective-permute-start.2 = (bf16[272,1024]{1,0:T(8,128)(2,1)S(1)}, bf16[272,1024]{1,0:T(8,128)(2,1)}, u32[]{:S(2)}, u32[]{:S(2)}) collective-permute-start(bf16[272,1024]{1,0:T(8,128)(2,1)S(1)} %fusion.1.refs_8_), channel_id=1, source_target_pairs={{16,0},{24,8},{0,16},{8,24},{17,1},{25,9},{1,17},{9,25},{18,2},{26... | collective-permute-start | bytes 1671176 | tf_op jit(solution)/shard_map/ppermute | solution.py:28
  9.0 23.0 %collective-permute-start = (bf16[352,1024]{1,0:T(8,128)(2,1)S(1)}, bf16[352,1024]{1,0:T(8,128)(2,1)S(1)}, u32[]{:S(2)}, u32[]{:S(2)}) collective-permute-start(bf16[352,1024]{1,0:T(8,128)(2,1)S(1)} %get-tuple-element.108.refs_5_), channel_id=1, source_target_pairs={{4,0},{0,4},{5,1},{1,5},{6,2},{2,6},{7,3},{3,7},{12,8},{8,12},{13,... | collective-permute-start | bytes 2162696 | tf_op jit(solution)/shard_map/ppermute | solution.py:20
  10.6 6.4 %collective-permute-start.3 = (bf16[256,1024]{1,0:T(8,128)(2,1)S(1)}, bf16[256,1024]{1,0:T(8,128)(2,1)}, u32[]{:S(2)}, u32[]{:S(2)}) collective-permute-start(bf16[256,1024]{1,0:T(8,128)(2,1)S(1)} %bitcast.48), channel_id=1, source_target_pairs={{1,0},{0,1},{3,2},{2,3},{5,4},{4,5},{7,6},{6,7},{9,8},{8,9},{11,10... | collective-permute-start | bytes 1572872 | tf_op jit(solution)/shard_map/ppermute | solution.py:20
  12.4 14.7 %collective-permute-start.7 = (bf16[2,128,1024]{2,1,0:T(8,128)(2,1)}, bf16[2,128,1024]{2,1,0:T(8,128)(2,1)}, u32[]{:S(2)}, u32[]{:S(2)}) collective-permute-start(bf16[2,128,1024]{2,1,0:T(8,128)(2,1)} %fusion.2), channel_id=1, source_target_pairs={{2,0},{0,2},{3,1},{1,3},{6,4},{4,6},{7,5},{5,7},{10,8},{8,10},{11,... | collective-permute-start | bytes 1572872 | tf_op jit(solution)/shard_map/ppermute | solution.py:20
  17.0 11.1 %collective-permute-start.4 = (bf16[256,1024]{1,0:T(8,128)(2,1)}, bf16[256,1024]{1,0:T(8,128)(2,1)S(1)}, u32[]{:S(2)}, u32[]{:S(2)}) collective-permute-start(bf16[256,1024]{1,0:T(8,128)(2,1)} %bitcast.51), channel_id=1, source_target_pairs={{1,0},{0,1},{3,2},{2,3},{5,4},{4,5},{7,6},{6,7},{9,8},{8,9},{11,10... | collective-permute-start | bytes 1572872 | tf_op jit(solution)/shard_map/ppermute | solution.py:20
  27.1 13.8 %collective-permute-start.9 = (bf16[2,128,1024]{2,1,0:T(8,128)(2,1)}, bf16[2,128,1024]{2,1,0:T(8,128)(2,1)S(1)}, u32[]{:S(2)}, u32[]{:S(2)}) collective-permute-start(bf16[2,128,1024]{2,1,0:T(8,128)(2,1)} %collective-permute-done.7.refs_4_), channel_id=1, source_target_pairs={{4,0},{0,4},{5,1},{1,5},{6,2},{2,6},{7,3},{3,7},{12,8},{8,12},{13,... | collective-permute-start | bytes 1572872 | tf_op jit(solution)/shard_map/ppermute | solution.py:20
  32.1 15.0 %collective-permute-start.5 = (bf16[352,1024]{1,0:T(8,128)(2,1)S(1)}, bf16[352,1024]{1,0:T(8,128)(2,1)}, u32[]{:S(2)}, u32[]{:S(2)}) collective-permute-start(bf16[352,1024]{1,0:T(8,128)(2,1)S(1)} %get-tuple-element.106.refs_3_), channel_id=1, source_target_pairs={{2,0},{0,2},{3,1},{1,3},{6,4},{4,6},{7,5},{5,7},{10,8},{8,10},{11,... | collective-permute-start | bytes 2162696 | tf_op jit(solution)/shard_map/ppermute | solution.py:20
  33.6 12.1 %collective-permute-start.6 = (bf16[272,1024]{1,0:T(8,128)(2,1)}, bf16[272,1024]{1,0:T(8,128)(2,1)S(1)}, u32[]{:S(2)}, u32[]{:S(2)}) collective-permute-start(bf16[272,1024]{1,0:T(8,128)(2,1)} %collective-permute-done.2.refs_10_), channel_id=1, source_target_pairs={{8,0},{0,8},{24,16},{16,24},{9,1},{1,9},{25,17},{17,25},{10,2},{2,... | collective-permute-start | bytes 1671176 | tf_op jit(solution)/shard_map/ppermute | solution.py:28
  34.0 6.8 %collective-permute-start.8 = (bf16[2,128,1024]{2,1,0:T(8,128)(2,1)}, bf16[2,128,1024]{2,1,0:T(8,128)(2,1)S(1)}, u32[]{:S(2)}, u32[]{:S(2)}) collective-permute-start(bf16[2,128,1024]{2,1,0:T(8,128)(2,1)} %collective-permute-done.7.refs_4_), channel_id=1, source_target_pairs={{1,0},{0,1},{3,2},{2,3},{5,4},{4,5},{7,6},{6,7},{9,8},{8,9},{11,10... | collective-permute-start | bytes 1572872 | tf_op jit(solution)/shard_map/ppermute | solution.py:20
  40.8 6.2 %collective-permute-start.10 = (bf16[2,128,1024]{2,1,0:T(8,128)(2,1)S(1)}, bf16[2,128,1024]{2,1,0:T(8,128)(2,1)S(1)}, u32[]{:S(2)}, u32[]{:S(2)}) collective-permute-start(bf16[2,128,1024]{2,1,0:T(8,128)(2,1)S(1)} %collective-permute-done.9.refs_6_), channel_id=1, source_target_pairs={{1,0},{0,1},{3,2},{2,3},{5,4},{4,5},{7,6},{6,7},{9,8},{8,9},{11,10... | collective-permute-start | bytes 1572872 | tf_op jit(solution)/shard_map/ppermute | solution.py:20
  47.1 18.7 %collective-permute-start.11 = (bf16[352,1024]{1,0:T(8,128)(2,1)S(1)}, bf16[352,1024]{1,0:T(8,128)(2,1)}, u32[]{:S(2)}, u32[]{:S(2)}) collective-permute-start(bf16[352,1024]{1,0:T(8,128)(2,1)S(1)} %get-tuple-element.106.refs_3_), channel_id=1, source_target_pairs={{4,0},{0,4},{5,1},{1,5},{6,2},{2,6},{7,3},{3,7},{12,8},{8,12},{13,... | collective-permute-start | bytes 2162696 | tf_op jit(solution)/shard_map/ppermute | solution.py:20
  48.9 16.9 %collective-permute-start.12 = (bf16[352,1024]{1,0:T(8,128)(2,1)S(1)}, bf16[352,1024]{1,0:T(8,128)(2,1)S(1)}, u32[]{:S(2)}, u32[]{:S(2)}) collective-permute-start(bf16[352,1024]{1,0:T(8,128)(2,1)S(1)} %get-tuple-element.108.refs_5_), channel_id=1, source_target_pairs={{2,0},{0,2},{3,1},{1,3},{6,4},{4,6},{7,5},{5,7},{10,8},{8,10},{11,... | collective-permute-start | bytes 2162696 | tf_op jit(solution)/shard_map/ppermute | solution.py:20
  51.0 19.8 %all-to-all-start = ((bf16[4,704,128]{2,1,0:T(8,128)(2,1)}), bf16[4,704,128]{2,1,0:T(8,128)(2,1)}, u32[]{:S(2)}, u32[]{:S(2)}) async-start(bf16[4,704,128]{2,1,0:T(8,128)(2,1)} %bitcast.53), calls=%async_computation | async-start | bytes 1441792 | tf_op jit(solution)/shard_map/all_to_all | solution.py:270
  66.7 6.7 %collective-permute-start.13 = (bf16[512,1024]{1,0:T(8,128)(2,1)}, bf16[512,1024]{1,0:T(8,128)(2,1)S(1)}, u32[]{:S(2)}, u32[]{:S(2)}) collective-permute-start(bf16[512,1024]{1,0:T(8,128)(2,1)} %get-tuple-element.113.refs_0_), channel_id=1, source_target_pairs={{1,0},{0,1},{3,2},{2,3},{5,4},{4,5},{7,6},{6,7},{9,8},{8,9},{11,10... | collective-permute-start | bytes 3145736 | tf_op jit(solution)/shard_map/ppermute | solution.py:20
  66.7 6.1 %collective-permute-start.15 = (f32[1024,128]{1,0:T(8,128)}, f32[1024,128]{1,0:T(8,128)}, u32[]{:S(2)}, u32[]{:S(2)}) collective-permute-start(f32[1024,128]{1,0:T(8,128)} %get-tuple-element.115.refs_2_), channel_id=1, source_target_pairs={{1,0},{0,1},{3,2},{2,3},{5,4},{4,5},{7,6},{6,7},{9,8},{8,9},{11,10... | collective-permute-start | bytes 1572872 | tf_op jit(solution)/shard_map/ppermute | solution.py:20
  67.2 15.5 %collective-permute-start.14 = (bf16[512,1024]{1,0:T(8,128)(2,1)}, bf16[512,1024]{1,0:T(8,128)(2,1)}, u32[]{:S(2)}, u32[]{:S(2)}) collective-permute-start(bf16[512,1024]{1,0:T(8,128)(2,1)} %get-tuple-element.114.refs_1_), channel_id=1, source_target_pairs={{1,0},{0,1},{3,2},{2,3},{5,4},{4,5},{7,6},{6,7},{9,8},{8,9},{11,10... | collective-permute-start | bytes 3145736 | tf_op jit(solution)/shard_map/ppermute | solution.py:20
  67.2 23.2 %collective-permute-start.16 = (bf16[352,1024]{1,0:T(8,128)(2,1)}, bf16[352,1024]{1,0:T(8,128)(2,1)}, u32[]{:S(2)}, u32[]{:S(2)}) collective-permute-start(bf16[352,1024]{1,0:T(8,128)(2,1)} %collective-permute-done.5.refs_3_), channel_id=1, source_target_pairs={{4,0},{0,4},{5,1},{1,5},{6,2},{2,6},{7,3},{3,7},{12,8},{8,12},{13,... | collective-permute-start | bytes 2162696 | tf_op jit(solution)/shard_map/ppermute | solution.py:20
  67.3 23.1 %collective-permute-start.17 = (bf16[352,1024]{1,0:T(8,128)(2,1)}, bf16[352,1024]{1,0:T(8,128)(2,1)}, u32[]{:S(2)}, u32[]{:S(2)}) collective-permute-start(bf16[352,1024]{1,0:T(8,128)(2,1)} %copy-done.3), channel_id=1, source_target_pairs={{2,0},{0,2},{3,1},{1,3},{6,4},{4,6},{7,5},{5,7},{10,8},{8,10},{11,... | collective-permute-start | bytes 2162696 | tf_op jit(solution)/shard_map/ppermute | solution.py:20
  72.9 29.2 %collective-permute-start.18 = (bf16[704,512]{1,0:T(8,128)(2,1)}, bf16[704,512]{1,0:T(8,128)(2,1)}, u32[]{:S(2)}, u32[]{:S(2)}) collective-permute-start(bf16[704,512]{1,0:T(8,128)(2,1)} %copy_bitcast_fusion), channel_id=1, source_target_pairs={{2,0},{0,2},{3,1},{1,3},{6,4},{4,6},{7,5},{5,7},{10,8},{8,10},{11,... | collective-permute-start | bytes 2162696 | tf_op jit(solution)/shard_map/ppermute | solution.py:20
  73.4 28.7 %collective-permute-start.19 = (bf16[704,512]{1,0:T(8,128)(2,1)}, bf16[704,512]{1,0:T(8,128)(2,1)}, u32[]{:S(2)}, u32[]{:S(2)}) collective-permute-start(bf16[704,512]{1,0:T(8,128)(2,1)} %copy_bitcast_fusion), channel_id=1, source_target_pairs={{4,0},{0,4},{5,1},{1,5},{6,2},{2,6},{7,3},{3,7},{12,8},{8,12},{13,... | collective-permute-start | bytes 2162696 | tf_op jit(solution)/shard_map/ppermute | solution.py:20
  82.7 38.3 %collective-permute-start.20 = (bf16[704,512]{1,0:T(8,128)(2,1)}, bf16[704,512]{1,0:T(8,128)(2,1)S(1)}, u32[]{:S(2)}, u32[]{:S(2)}) collective-permute-start(bf16[704,512]{1,0:T(8,128)(2,1)} %copy_bitcast_fusion), channel_id=1, source_target_pairs={{6,0},{4,2},{2,4},{0,6},{7,1},{5,3},{3,5},{1,7},{14,8},{12,10},{10... | collective-permute-start | bytes 2162696 | tf_op jit(solution)/shard_map/ppermute | solution.py:296
  106.3 3.2 %collective-permute-start.24 = (bf16[256,512]{1,0:T(8,128)(2,1)S(1)}, bf16[256,512]{1,0:T(8,128)(2,1)S(1)}, u32[]{:S(2)}, u32[]{:S(2)}) collective-permute-start(bf16[256,512]{1,0:T(8,128)(2,1)S(1)} %get-tuple-element.156), channel_id=1, source_target_pairs={{1,0},{0,1},{3,2},{2,3},{5,4},{4,5},{7,6},{6,7},{9,8},{8,9},{11,10... | collective-permute-start | bytes 786440 | tf_op jit(solution)/shard_map/ppermute | solution.py:20
  111.7 9.2 %collective-permute-start.25 = (bf16[256,512]{1,0:T(8,128)(2,1)S(1)}, bf16[256,512]{1,0:T(8,128)(2,1)S(1)}, u32[]{:S(2)}, u32[]{:S(2)}) collective-permute-start(bf16[256,512]{1,0:T(8,128)(2,1)S(1)} %get-tuple-element.150), channel_id=1, source_target_pairs={{8,0},{0,8},{24,16},{16,24},{9,1},{1,9},{25,17},{17,25},{10,2},{2,... | collective-permute-start | bytes 786440 | tf_op jit(solution)/shard_map/ppermute | solution.py:28
  113.8 19.6 %collective-permute-start.31 = (bf16[256,512]{1,0:T(8,128)(2,1)S(1)}, bf16[256,512]{1,0:T(8,128)(2,1)S(1)}, u32[]{:S(2)}, u32[]{:S(2)}) collective-permute-start(bf16[256,512]{1,0:T(8,128)(2,1)S(1)} %get-tuple-element.148), channel_id=1, source_target_pairs={{8,0},{0,8},{24,16},{16,24},{9,1},{1,9},{25,17},{17,25},{10,2},{2,... | collective-permute-start | bytes 786440 | tf_op jit(solution)/shard_map/ppermute | solution.py:28
  124.2 4.9 %collective-permute-start.28 = (bf16[256,512]{1,0:T(8,128)(2,1)S(1)}, bf16[256,512]{1,0:T(8,128)(2,1)S(1)}, u32[]{:S(2)}, u32[]{:S(2)}) collective-permute-start(bf16[256,512]{1,0:T(8,128)(2,1)S(1)} %get-tuple-element.153), channel_id=1, source_target_pairs={{1,0},{0,1},{3,2},{2,3},{5,4},{4,5},{7,6},{6,7},{9,8},{8,9},{11,10... | collective-permute-start | bytes 786440 | tf_op jit(solution)/shard_map/ppermute | solution.py:20
  124.7 4.4 %collective-permute-start.27 = (bf16[256,512]{1,0:T(8,128)(2,1)S(1)}, bf16[256,512]{1,0:T(8,128)(2,1)S(1)}, u32[]{:S(2)}, u32[]{:S(2)}) collective-permute-start(bf16[256,512]{1,0:T(8,128)(2,1)S(1)} %get-tuple-element.154), channel_id=1, source_target_pairs={{1,0},{0,1},{3,2},{2,3},{5,4},{4,5},{7,6},{6,7},{9,8},{8,9},{11,10... | collective-permute-start | bytes 786440 | tf_op jit(solution)/shard_map/ppermute | solution.py:20
  124.8 4.3 %collective-permute-start.26 = (bf16[256,512]{1,0:T(8,128)(2,1)S(1)}, bf16[256,512]{1,0:T(8,128)(2,1)S(1)}, u32[]{:S(2)}, u32[]{:S(2)}) collective-permute-start(bf16[256,512]{1,0:T(8,128)(2,1)S(1)} %get-tuple-element.151), channel_id=1, source_target_pairs={{1,0},{0,1},{3,2},{2,3},{5,4},{4,5},{7,6},{6,7},{9,8},{8,9},{11,10... | collective-permute-start | bytes 786440 | tf_op jit(solution)/shard_map/ppermute | solution.py:20
  126.2 15.2 %collective-permute-start.32 = (bf16[256,512]{1,0:T(8,128)(2,1)S(1)}, bf16[256,512]{1,0:T(8,128)(2,1)S(1)}, u32[]{:S(2)}, u32[]{:S(2)}) collective-permute-start(bf16[256,512]{1,0:T(8,128)(2,1)S(1)} %add_convert_fusion.5), channel_id=1, source_target_pairs={{16,0},{24,8},{0,16},{8,24},{17,1},{25,9},{1,17},{9,25},{18,2},{26... | collective-permute-start | bytes 786440 | tf_op jit(solution)/shard_map/ppermute | solution.py:28
  131.3 13.5 %collective-permute-start.30 = (bf16[256,512]{1,0:T(8,128)(2,1)S(1)}, bf16[256,512]{1,0:T(8,128)(2,1)S(1)}, u32[]{:S(2)}, u32[]{:S(2)}) collective-permute-start(bf16[256,512]{1,0:T(8,128)(2,1)S(1)} %get-tuple-element.147), channel_id=1, source_target_pairs={{8,0},{0,8},{24,16},{16,24},{9,1},{1,9},{25,17},{17,25},{10,2},{2,... | collective-permute-start | bytes 786440 | tf_op jit(solution)/shard_map/ppermute | solution.py:28
  132.8 18.5 %collective-permute-start.33 = (bf16[256,512]{1,0:T(8,128)(2,1)S(1)}, bf16[256,512]{1,0:T(8,128)(2,1)S(1)}, u32[]{:S(2)}, u32[]{:S(2)}) collective-permute-start(bf16[256,512]{1,0:T(8,128)(2,1)S(1)} %get-tuple-element.145), channel_id=1, source_target_pairs={{8,0},{0,8},{24,16},{16,24},{9,1},{1,9},{25,17},{17,25},{10,2},{2,... | collective-permute-start | bytes 786440 | tf_op jit(solution)/shard_map/ppermute | solution.py:28
  144.9 12.5 %collective-permute-start.34 = (bf16[256,512]{1,0:T(8,128)(2,1)S(1)}, bf16[256,512]{1,0:T(8,128)(2,1)S(1)}, u32[]{:S(2)}, u32[]{:S(2)}) collective-permute-start(bf16[256,512]{1,0:T(8,128)(2,1)S(1)} %add_convert_fusion.4), channel_id=1, source_target_pairs={{16,0},{24,8},{0,16},{8,24},{17,1},{25,9},{1,17},{9,25},{18,2},{26... | collective-permute-start | bytes 786440 | tf_op jit(solution)/shard_map/ppermute | solution.py:28
  (29 other events, 274.7 us)

commit v4 on v3

--- a/solution.py
+++ b/solution.py
@@ -121,10 +121,11 @@
     return mixed, weight, inner
 
 
-def hidden_kernel(los, tiles, at_ref, *refs):
-    x_refs, refs = refs[:tiles], refs[tiles:]
-    weight_ref, gate_refs, up_refs = refs[0], refs[1 : 1 + los], refs[1 + los : 1 + 2 * los]
-    act_ref, gate, up = refs[1 + 2 * los :]
+def hidden_kernel(los, sets, tiles, at_ref, *refs):
+    x_refs, refs = refs[: sets * tiles], refs[sets * tiles :]
+    weight_refs, refs = refs[:sets], refs[sets:]
+    gate_refs, up_refs, refs = refs[:los], refs[los : 2 * los], refs[2 * los :]
+    act_refs, gate, up = refs[:sets], refs[sets], refs[sets + 1]
     units = gate_refs[0].shape[0]
 
     @pl.when(pl.program_id(0) == 0)
@@ -134,35 +135,39 @@
             gate[place, :] = gate_refs[j][...]
             up[place, :] = up_refs[j][...]
 
-    for t in range(tiles):
+    for t in range(sets * tiles):
 
         def work(t=t):
             x = x_refs[t][...]
             lane = lax.broadcasted_iota(jnp.int32, (x.shape[0], LANES), 1)
-            scale = jnp.sum(jnp.where(lane == at_ref[0], weight_ref[...], 0.0), axis=1, keepdims=True)
+            weight = weight_refs[t // tiles][...]
+            scale = jnp.sum(jnp.where(lane == at_ref[0], weight, 0.0), axis=1, keepdims=True)
             gated = jax.nn.gelu(dot(x, gate[...], 1), approximate=True)
-            act_ref[...] = (gated * dot(x, up[...], 1) * scale).astype(jnp.bfloat16)
+            act_refs[t // tiles][...] = (gated * dot(x, up[...], 1) * scale).astype(jnp.bfloat16)
 
         pl.when(pl.program_id(0) == t)(work)
 
 
-def hidden(at, xs, weight, gates, ups):
-    tiles, (tile, width) = len(xs), xs[0].shape
+def hidden(at, groups, gates, ups):
+    sets, tiles, (tile, width) = len(groups), len(groups[0][0]), groups[0][0][0].shape
     los, units = len(gates), gates[0].shape[0]
+    xs = [x for group, _ in groups for x in group]
+    once = lambda a: pl.BlockSpec(a.shape, lambda i: (0, 0), pipeline_mode=pl.Buffered(1))
+    place = lambda n: lambda i: (jnp.clip(i - n * tiles, 0, tiles - 1), 0)
     return pl.pallas_call(
-        functools.partial(hidden_kernel, los, tiles),
-        grid=(tiles,),
-        out_shape=jax.ShapeDtypeStruct((tiles * tile, los * units), jnp.bfloat16),
+        functools.partial(hidden_kernel, los, sets, tiles),
+        grid=(sets * tiles,),
+        out_shape=[jax.ShapeDtypeStruct((tiles * tile, los * units), jnp.bfloat16)] * sets,
         in_specs=[pl.BlockSpec(memory_space=pltpu.SMEM)]
-        + [whole(x) for x in xs]
-        + [pl.BlockSpec((tile, LANES), lambda i: (i, 0))]
-        + [whole(a) for a in (*gates, *ups)],
-        out_specs=pl.BlockSpec((tile, los * units), lambda i: (i, 0)),
+        + [once(x) for x in xs]
+        + [pl.BlockSpec((tile, LANES), place(n)) for n in range(sets)]
+        + [once(a) for a in (*gates, *ups)],
+        out_specs=[pl.BlockSpec((tile, los * units), place(n)) for n in range(sets)],
         scratch_shapes=[pltpu.VMEM((los * units, width), jnp.bfloat16)] * 2,
         compiler_params=pltpu.CompilerParams(vmem_limit_bytes=VMEM // 2),
         cost_estimate=brief(),
         name="hidden",
-    )(at, *xs, weight, *gates, *ups)
+    )(at, *xs, *(w for _, w in groups), *gates, *ups)
 
 
 def final_kernel(los, lines, count, lo_ref, mixed_ref, *refs):
@@ -281,11 +286,11 @@
     x_far = [from_offset(v, "core", CORES, 1) for v in x_own]
     w_far = from_offset(w_own, "core", CORES, 1)
 
-    def act(i, x, w):
+    def act(i, *groups):
         at = jnp.stack([(ex + i) % exs * CORES + core, lo])
-        return hidden(at, x, w, *([of[i, j] for j in range(los)] for of in (gates, ups)))
-
-    near, far = [act(0, x_own, w_own)], [act(0, x_far, w_far)]
+        return hidden(at, groups, *([of[i, j] for j in range(los)] for of in (gates, ups)))
+
+    near, far = act(0, (x_own, w_own)), act(0, (x_far, w_far))
     down = down.transpose(1, 0, 2).reshape(down_rows // lines, lines * cols)
     downs = {(i, 0): from_offset(down, "ex", exs, i) for i in range(exs)}
     downs.update({(0, j): from_offset(down, "lo", los, j) for j in lo_far})
@@ -296,8 +301,9 @@
             downs[i, j] = lax.ppermute(down, ("lo", "ex"), moves)
 
     x_own, w_own, x_far, w_far, near, far, gates, ups = together(x_own, w_own, x_far, w_far, near, far, gates, ups)
-    far += [act(i, x_far, w_far) for i in ex_far]
-    near += [act(i, x_own, w_own) for i in ex_far]
+    for i in ex_far:
+        later = act(i, (x_far, w_far), (x_own, w_own))
+        far, near = [*far, later[0]], [*near, later[1]]
 
     direct = [(i, 0) for i in range(exs)] + [(0, j) for j in lo_far]
     near, far, pieces = together(near, far, [downs[k] for k in direct])

time: 159 us -> 159 us (level)
  Pallas kernels: 33.5 us -> 31.3 us
    pallas_call x4 -> x3, Pallas kernels: 21.8 us -> 19.7 us  [hidden(): pl.pallas_call(functools.partial(hidden_kernel, los, sets, tiles), grid=(...]
    unnamed x50 -> x52, local copies, waits for them, and re-layouts: 4.34 us -> 5.43 us
  transfers between devices with their start and end apart: 36 -> 36, of which waited for: 13 -> 13; matrix products, arithmetic and copies ran while one was open for 15% -> 15% of each run, Pallas kernels for 20% -> 19%
where the time goes in v4:
time: 159 us; the launch traced here: 158 us
  waiting for transfers between devices  60.9 us (38%)
  starting transfers between devices  34.7 us (22%)
  Pallas kernels  31.3 us (20%)
  matrix products  14.4 us (9%)
  local copies, waits for them, and re-layouts  11.2 us (7%)
  other arithmetic  5.39 us (3%)
    ppermute x9, waiting for transfers between devices, across(): lax.ppermute(value, 'line', [(i ^ mask, i) for i in range(size)])  38.8 us
    pallas_call x3, Pallas kernels, hidden(): pl.pallas_call(functools.partial(hidden_kernel, los, sets, tiles), grid=(...  19.7 us
    ppermute x25, waiting for transfers between devices, from_offset(): lax.ppermute(value, axis, [((i + offset) % size, i) for i in range(size)])  19.2 us
    dot_general x8, matrix products, dot(): lax.dot_general(a, b, (((1,), (rhs_dim,)), ((), ())), preferred_element_t...  14.4 us
    ppermute x9, starting transfers between devices, across(): lax.ppermute(value, 'line', [(i ^ mask, i) for i in range(size)])  14.3 us
    ppermute x25, starting transfers between devices, from_offset(): lax.ppermute(value, axis, [((i + offset) % size, i) for i in range(size)])  13.9 us
    pallas_call x1, Pallas kernels, front(): pl.pallas_call(functools.partial(front_kernel, len(pairs) // 2, len(piece...  10.5 us
    unnamed x52, local copies, waits for them, and re-layouts  5.43 us
  transfers between devices with their start and end apart: 36, of which 13 were waited for; matrix products, arithmetic and copies ran while one was open for 15% of the time, Pallas kernels for 19%

profile of v4, /device:TPU:0, one launch (start us, length us, event | category | flops | bytes accessed | tf_op | source)
XLA Modules:
  0.0 158.5 jit_solution(6247343226450589291)
XLA Ops:
  1.9 3.1 %collective-permute-start.1 = (bf16[272,1024]{1,0:T(8,128)(2,1)S(1)}, bf16[272,1024]{1,0:T(8,128)(2,1)}, u32[]{:S(2)}, u32[]{:S(2)}) collective-permute-start(bf16[272,1024]{1,0:T(8,128)(2,1)S(1)} %fusion.1.refs_8_), channel_id=1, source_target_pairs={{8,0},{0,8},{24,16},{16,24},{9,1},{1,9},{25,17},{17,25},{10,2},{2,... | collective-permute-start | bytes 1671176 | tf_op jit(solution)/shard_map/ppermute | solution.py:28
  5.0 2.6 %collective-permute-start.2 = (bf16[272,1024]{1,0:T(8,128)(2,1)S(1)}, bf16[272,1024]{1,0:T(8,128)(2,1)}, u32[]{:S(2)}, u32[]{:S(2)}) collective-permute-start(bf16[272,1024]{1,0:T(8,128)(2,1)S(1)} %fusion.1.refs_8_), channel_id=1, source_target_pairs={{16,0},{24,8},{0,16},{8,24},{17,1},{25,9},{1,17},{9,25},{18,2},{26... | collective-permute-start | bytes 1671176 | tf_op jit(solution)/shard_map/ppermute | solution.py:28
  9.0 1.6 collective-permute-start
  10.6 1.8 %fusion.2 = bf16[2,128,1024]{2,1,0:T(8,128)(2,1)} fusion(s32[]{:T(128)S(6)} %select_n.53, bf16[1,256,1024]{2,1,0:T(8,128)(2,1)S(1)} %bitcast.49, bf16[1,256,1024]{2,1,0:T(8,128)(2,1)} %bitcast.50), kind=kLoop, calls=%fused_computation.12 | loop fusion | flops 1048576 | bytes 1572868 | tf_op jit(solution)/shard_map/stack | solution.py:240
  17.2 9.8 %collective-permute-done.7.refs_4_ = bf16[2,128,1024]{2,1,0:T(8,128)(2,1)} collective-permute-done((bf16[2,128,1024]{2,1,0:T(8,128)(2,1)}, bf16[2,128,1024]{2,1,0:T(8,128)(2,1)}, u32[]{:S(2)}, u32[]{:S(2)}) %collective-permute-start.7) | collective-permute-done | bytes 524320 | tf_op jit(solution)/shard_map/ppermute | solution.py:20
  29.6 2.5 %collective-permute-done.2.refs_10_ = bf16[272,1024]{1,0:T(8,128)(2,1)} collective-permute-done((bf16[272,1024]{1,0:T(8,128)(2,1)S(1)}, bf16[272,1024]{1,0:T(8,128)(2,1)}, u32[]{:S(2)}, u32[]{:S(2)}) %collective-permute-start.2) | collective-permute-done | bytes 557088 | tf_op jit(solution)/shard_map/ppermute | solution.py:28
  34.0 6.8 %collective-permute-done.9.refs_6_ = bf16[2,128,1024]{2,1,0:T(8,128)(2,1)S(1)} collective-permute-done((bf16[2,128,1024]{2,1,0:T(8,128)(2,1)}, bf16[2,128,1024]{2,1,0:T(8,128)(2,1)S(1)}, u32[]{:S(2)}, u32[]{:S(2)}) %collective-permute-start.9) | collective-permute-done | bytes 524320 | tf_op jit(solution)/shard_map/ppermute | solution.py:20
  40.8 4.8 %collective-permute-done.6.refs_11_ = bf16[272,1024]{1,0:T(8,128)(2,1)S(1)} collective-permute-done((bf16[272,1024]{1,0:T(8,128)(2,1)}, bf16[272,1024]{1,0:T(8,128)(2,1)S(1)}, u32[]{:S(2)}, u32[]{:S(2)}) %collective-permute-start.6) | collective-permute-done | bytes 557088 | tf_op jit(solution)/shard_map/ppermute | solution.py:28
  47.1 1.8 %collective-permute-start.11 = (bf16[352,1024]{1,0:T(8,128)(2,1)S(1)}, bf16[352,1024]{1,0:T(8,128)(2,1)S(1)}, u32[]{:S(2)}, u32[]{:S(2)}) collective-permute-start(bf16[352,1024]{1,0:T(8,128)(2,1)S(1)} %get-tuple-element.108.refs_3_), channel_id=1, source_target_pairs={{4,0},{0,4},{5,1},{1,5},{6,2},{2,6},{7,3},{3,7},{12,8},{8,12},{13,... | collective-permute-start | bytes 2162696 | tf_op jit(solution)/shard_map/ppermute | solution.py:20
  48.9 2.2 %collective-permute-start.12 = (bf16[352,1024]{1,0:T(8,128)(2,1)S(1)}, bf16[352,1024]{1,0:T(8,128)(2,1)}, u32[]{:S(2)}, u32[]{:S(2)}) collective-permute-start(bf16[352,1024]{1,0:T(8,128)(2,1)S(1)} %get-tuple-element.110.refs_5_), channel_id=1, source_target_pairs={{2,0},{0,2},{3,1},{1,3},{6,4},{4,6},{7,5},{5,7},{10,8},{8,10},{11,... | collective-permute-start | bytes 2162696 | tf_op jit(solution)/shard_map/ppermute | solution.py:20
  51.0 4.2 %all-to-all-start = ((bf16[4,704,128]{2,1,0:T(8,128)(2,1)}), bf16[4,704,128]{2,1,0:T(8,128)(2,1)}, u32[]{:S(2)}, u32[]{:S(2)}) async-start(bf16[4,704,128]{2,1,0:T(8,128)(2,1)} %bitcast.53), calls=%async_computation | async-start | bytes 1441792 | tf_op jit(solution)/shard_map/all_to_all | solution.py:275
  55.3 10.5 %front.1 = (bf16[256,1024]{1,0:T(8,128)(2,1)}, f32[1024,128]{1,0:T(8,128)}, bf16[512,1024]{1,0:T(8,128)(2,1)}, bf16[512,1024]{1,0:T(8,128)(2,1)}) custom-call(s32[4]{0:T(128)} %add_multiply_fusion.base_ref, s32[3,48]{1,0:T(4,128)} %pad_add_fusion.prompts_ref, s32[1,1024]{1,0:T(1,128)} %bitcast.55, bf16[1,1024]{1,0:T(2,128)(2,1)} %broadcast_in_dim.31.gain_a_ref, ...), custom_call_target="tpu_custom_call" | custom-call | flops 1 | bytes 1 | tf_op jit(solution)/shard_map/front/pallas_call | solution.py:110
  67.9 2.9 %all-to-all-done = bf16[4,704,128]{2,1,0:T(8,128)(2,1)} async-done(((bf16[4,704,128]{2,1,0:T(8,128)(2,1)}), bf16[4,704,128]{2,1,0:T(8,128)(2,1)}, u32[]{:S(2)}, u32[]{:S(2)}) %all-to-all-start) | async-done | bytes 720928 | tf_op jit(solution)/shard_map/all_to_all | solution.py:275
  70.8 2.0 %copy_bitcast_fusion = bf16[704,512]{1,0:T(8,128)(2,1)} fusion(bf16[4,704,128]{2,1,0:T(8,128)(2,1)} %all-to-all-done), kind=kLoop, calls=%fused_computation.8 | loop fusion | bytes 1441792 | tf_op jit(solution)/shard_map/reshape | solution.py:294
  78.8 4.4 %hidden.3 = bf16[1024,704]{1,0:T(8,128)(2,1)S(1)} custom-call(s32[2]{0:T(128)S(1)} %pad_add_fusion.1.at_ref, bf16[512,1024]{1,0:T(8,128)(2,1)S(1)} %copy-done, bf16[512,1024]{1,0:T(8,128)(2,1)S(1)} %copy-done.1, f32[1024,128]{1,0:T(8,128)S(1)} %copy-done.9, bf16[352,1024]{1,0:T(8,128)(2,1)S(1)} %get-tuple-element.108.refs_3_, ...), custom_call_target="tpu_custom_call" | custom-call | flops 1 | bytes 1 | tf_op jit(solution)/shard_map/hidden/pallas_call | solution.py:157
  83.2 2.4 %collective-permute-start.20 = (bf16[704,512]{1,0:T(8,128)(2,1)}, bf16[704,512]{1,0:T(8,128)(2,1)S(1)}, u32[]{:S(2)}, u32[]{:S(2)}) collective-permute-start(bf16[704,512]{1,0:T(8,128)(2,1)} %copy_bitcast_fusion), channel_id=1, source_target_pairs={{6,0},{4,2},{2,4},{0,6},{7,1},{5,3},{3,5},{1,7},{14,8},{12,10},{10... | collective-permute-start | bytes 2162696 | tf_op jit(solution)/shard_map/ppermute | solution.py:301
  85.5 5.2 %hidden.4 = bf16[1024,704]{1,0:T(8,128)(2,1)S(1)} custom-call(s32[2]{0:T(128)S(1)} %pad_add_fusion.1.at_ref, bf16[512,1024]{1,0:T(8,128)(2,1)S(1)} %collective-permute-done.13.refs_0_, bf16[512,1024]{1,0:T(8,128)(2,1)} %collective-permute-done.14.refs_1_, f32[1024,128]{1,0:T(8,128)} %collective-permute-done.15.refs_2_.refs_4_, ...), custom_call_target="tpu_custom_call" | custom-call | flops 1 | bytes 1 | tf_op jit(solution)/shard_map/hidden/pallas_call | solution.py:157
  90.8 10.1 %hidden.5 = (bf16[1024,704]{1,0:T(8,128)(2,1)S(1)}, bf16[1024,704]{1,0:T(8,128)(2,1)S(1)}) custom-call(s32[2]{0:T(128)S(1)} %pad_add_fusion.2.at_ref, bf16[512,1024]{1,0:T(8,128)(2,1)S(1)} %collective-permute-done.13.refs_0_, bf16[512,1024]{1,0:T(8,128)(2,1)} %collective-permute-done.14.refs_1_, bf16[512,1024]{1,0:T(8,128)(2,1)S(1)} %copy-done, ...), custom_call_target="tpu_custom_call" | custom-call | flops 1 | bytes 1 | tf_op jit(solution)/shard_map/hidden/pallas_call | solution.py:157
  102.0 2.1 %fusion.8 = f32[1024,512]{1,0:T(8,128)S(1)} fusion(bf16[1024,704]{1,0:T(8,128)(2,1)S(1)} %get-tuple-element.141, bf16[704,512]{1,0:T(8,128)(2,1)} %collective-permute-done.18), kind=kOutput, calls=%fused_computation.38 | convolution fusion | flops 738197504 | bytes 4259840 | tf_op jit(solution)/shard_map/dot_general | solution.py:32
  104.1 2.1 %add_convert_fusion.3 = bf16[1024,512]{1,0:T(8,128)(2,1)S(1)} fusion(f32[1024,512]{1,0:T(8,128)S(1)} %fusion.8, bf16[1024,704]{1,0:T(8,128)(2,1)S(1)} %hidden.4, bf16[704,512]{1,0:T(8,128)(2,1)} %copy_bitcast_fusion), kind=kOutput, calls=%fused_computation.3 | convolution fusion | flops 739246080 | bytes 5308416 | tf_op jit(solution)/shard_map/dot_general | solution.py:32
  107.4 2.1 %fusion.7 = f32[1024,512]{1,0:T(8,128)S(1)} fusion(bf16[1024,704]{1,0:T(8,128)(2,1)S(1)} %get-tuple-element.138, bf16[704,512]{1,0:T(8,128)(2,1)} %collective-permute-done.18), kind=kOutput, calls=%fused_computation.37 | convolution fusion | flops 738197504 | bytes 4259840 | tf_op jit(solution)/shard_map/dot_general | solution.py:32
  109.5 2.1 %add_convert_fusion.2 = bf16[1024,512]{1,0:T(8,128)(2,1)S(1)} fusion(f32[1024,512]{1,0:T(8,128)S(1)} %fusion.7, bf16[256,512]{1,0:T(8,128)(2,1)S(1)} %collective-permute-done.24, bf16[256,512]{1,0:T(8,128)(2,1)S(1)} %collective-permute-done.23, bf16[256,512]{1,0:T(8,128)(2,1)S(1)} %collective-permute-done.22, ...), kind=kOutput, calls=%fused_computation.2 | convolution fusion | flops 743964672 | bytes 6356992 | tf_op jit(solution)/shard_map/dot_general | solution.py:32
  111.6 2.1 %collective-permute-start.25 = (bf16[256,512]{1,0:T(8,128)(2,1)S(1)}, bf16[256,512]{1,0:T(8,128)(2,1)S(1)}, u32[]{:S(2)}, u32[]{:S(2)}) collective-permute-start(bf16[256,512]{1,0:T(8,128)(2,1)S(1)} %get-tuple-element.154), channel_id=1, source_target_pairs={{8,0},{0,8},{24,16},{16,24},{9,1},{1,9},{25,17},{17,25},{10,2},{2,... | collective-permute-start | bytes 786440 | tf_op jit(solution)/shard_map/ppermute | solution.py:28
  113.8 7.0 %collective-permute-done.25 = bf16[256,512]{1,0:T(8,128)(2,1)S(1)} collective-permute-done((bf16[256,512]{1,0:T(8,128)(2,1)S(1)}, bf16[256,512]{1,0:T(8,128)(2,1)S(1)}, u32[]{:S(2)}, u32[]{:S(2)}) %collective-permute-start.25) | collective-permute-done | bytes 262176 | tf_op jit(solution)/shard_map/ppermute | solution.py:28
  121.9 2.1 %add_convert_fusion.1 = bf16[1024,512]{1,0:T(8,128)(2,1)S(1)} fusion(f32[1024,512]{1,0:T(8,128)S(1)} %fusion.10, bf16[1024,704]{1,0:T(8,128)(2,1)S(1)} %hidden.4, bf16[704,512]{1,0:T(8,128)(2,1)} %collective-permute-done.19), kind=kOutput, calls=%fused_computation.1 | convolution fusion | flops 739246080 | bytes 5308416 | tf_op jit(solution)/shard_map/dot_general | solution.py:32
  126.2 2.9 %collective-permute-start.32 = (bf16[256,512]{1,0:T(8,128)(2,1)S(1)}, bf16[256,512]{1,0:T(8,128)(2,1)S(1)}, u32[]{:S(2)}, u32[]{:S(2)}) collective-permute-start(bf16[256,512]{1,0:T(8,128)(2,1)S(1)} %add_convert_fusion.5), channel_id=1, source_target_pairs={{16,0},{24,8},{0,16},{8,24},{17,1},{25,9},{1,17},{9,25},{18,2},{26... | collective-permute-start | bytes 786440 | tf_op jit(solution)/shard_map/ppermute | solution.py:28
  129.1 2.1 %add_convert_fusion = bf16[1024,512]{1,0:T(8,128)(2,1)S(1)} fusion(f32[1024,512]{1,0:T(8,128)S(1)} %fusion.9, bf16[256,512]{1,0:T(8,128)(2,1)S(1)} %collective-permute-done.29, bf16[256,512]{1,0:T(8,128)(2,1)S(1)} %collective-permute-done.28, bf16[256,512]{1,0:T(8,128)(2,1)S(1)} %collective-permute-done.27, bf16[256,512]{1,0:T(8,128)(2,1)S(1)} %collective-permute-done.26, ...), kind=kOutput, calls=%fused_computation | convolution fusion | flops 743964672 | bytes 6356992 | tf_op jit(solution)/shard_map/dot_general | solution.py:32
  131.3 1.5 collective-permute-start.30
  133.4 8.0 %collective-permute-done.32.refs_2_ = bf16[256,512]{1,0:T(8,128)(2,1)S(1)} collective-permute-done((bf16[256,512]{1,0:T(8,128)(2,1)S(1)}, bf16[256,512]{1,0:T(8,128)(2,1)S(1)}, u32[]{:S(2)}, u32[]{:S(2)}) %collective-permute-start.32) | collective-permute-done | bytes 262176 | tf_op jit(solution)/shard_map/ppermute | solution.py:28
  141.3 3.4 %collective-permute-done.30 = bf16[256,512]{1,0:T(8,128)(2,1)S(1)} collective-permute-done((bf16[256,512]{1,0:T(8,128)(2,1)S(1)}, bf16[256,512]{1,0:T(8,128)(2,1)S(1)}, u32[]{:S(2)}, u32[]{:S(2)}) %collective-permute-start.30) | collective-permute-done | bytes 262176 | tf_op jit(solution)/shard_map/ppermute | solution.py:28
  145.8 5.5 %collective-permute-done.33.refs_4_ = bf16[256,512]{1,0:T(8,128)(2,1)S(1)} collective-permute-done((bf16[256,512]{1,0:T(8,128)(2,1)S(1)}, bf16[256,512]{1,0:T(8,128)(2,1)S(1)}, u32[]{:S(2)}, u32[]{:S(2)}) %collective-permute-start.33) | collective-permute-done | bytes 262176 | tf_op jit(solution)/shard_map/ppermute | solution.py:28
  151.3 6.1 %collective-permute-done.34.refs_5_ = bf16[256,512]{1,0:T(8,128)(2,1)S(1)} collective-permute-done((bf16[256,512]{1,0:T(8,128)(2,1)S(1)}, bf16[256,512]{1,0:T(8,128)(2,1)S(1)}, u32[]{:S(2)}, u32[]{:S(2)}) %collective-permute-start.34) | collective-permute-done | bytes 262176 | tf_op jit(solution)/shard_map/ppermute | solution.py:28
  (135 shorter events, 30.2 us)
Async XLA Ops:
  1.9 27.6 %collective-permute-start.1 = (bf16[272,1024]{1,0:T(8,128)(2,1)S(1)}, bf16[272,1024]{1,0:T(8,128)(2,1)}, u32[]{:S(2)}, u32[]{:S(2)}) collective-permute-start(bf16[272,1024]{1,0:T(8,128)(2,1)S(1)} %fusion.1.refs_8_), channel_id=1, source_target_pairs={{8,0},{0,8},{24,16},{16,24},{9,1},{1,9},{25,17},{17,25},{10,2},{2,... | collective-permute-start | bytes 1671176 | tf_op jit(solution)/shard_map/ppermute | solution.py:28
  5.0 27.1 %collective-permute-start.2 = (bf16[272,1024]{1,0:T(8,128)(2,1)S(1)}, bf16[272,1024]{1,0:T(8,128)(2,1)}, u32[]{:S(2)}, u32[]{:S(2)}) collective-permute-start(bf16[272,1024]{1,0:T(8,128)(2,1)S(1)} %fusion.1.refs_8_), channel_id=1, source_target_pairs={{16,0},{24,8},{0,16},{8,24},{17,1},{25,9},{1,17},{9,25},{18,2},{26... | collective-permute-start | bytes 1671176 | tf_op jit(solution)/shard_map/ppermute | solution.py:28
  9.0 23.0 %collective-permute-start = (bf16[352,1024]{1,0:T(8,128)(2,1)S(1)}, bf16[352,1024]{1,0:T(8,128)(2,1)S(1)}, u32[]{:S(2)}, u32[]{:S(2)}) collective-permute-start(bf16[352,1024]{1,0:T(8,128)(2,1)S(1)} %get-tuple-element.110.refs_5_), channel_id=1, source_target_pairs={{4,0},{0,4},{5,1},{1,5},{6,2},{2,6},{7,3},{3,7},{12,8},{8,12},{13,... | collective-permute-start | bytes 2162696 | tf_op jit(solution)/shard_map/ppermute | solution.py:20
  10.6 6.4 %collective-permute-start.3 = (bf16[256,1024]{1,0:T(8,128)(2,1)S(1)}, bf16[256,1024]{1,0:T(8,128)(2,1)}, u32[]{:S(2)}, u32[]{:S(2)}) collective-permute-start(bf16[256,1024]{1,0:T(8,128)(2,1)S(1)} %bitcast.48), channel_id=1, source_target_pairs={{1,0},{0,1},{3,2},{2,3},{5,4},{4,5},{7,6},{6,7},{9,8},{8,9},{11,10... | collective-permute-start | bytes 1572872 | tf_op jit(solution)/shard_map/ppermute | solution.py:20
  12.4 14.7 %collective-permute-start.7 = (bf16[2,128,1024]{2,1,0:T(8,128)(2,1)}, bf16[2,128,1024]{2,1,0:T(8,128)(2,1)}, u32[]{:S(2)}, u32[]{:S(2)}) collective-permute-start(bf16[2,128,1024]{2,1,0:T(8,128)(2,1)} %fusion.2), channel_id=1, source_target_pairs={{2,0},{0,2},{3,1},{1,3},{6,4},{4,6},{7,5},{5,7},{10,8},{8,10},{11,... | collective-permute-start | bytes 1572872 | tf_op jit(solution)/shard_map/ppermute | solution.py:20
  17.0 11.1 %collective-permute-start.4 = (bf16[256,1024]{1,0:T(8,128)(2,1)}, bf16[256,1024]{1,0:T(8,128)(2,1)S(1)}, u32[]{:S(2)}, u32[]{:S(2)}) collective-permute-start(bf16[256,1024]{1,0:T(8,128)(2,1)} %bitcast.51), channel_id=1, source_target_pairs={{1,0},{0,1},{3,2},{2,3},{5,4},{4,5},{7,6},{6,7},{9,8},{8,9},{11,10... | collective-permute-start | bytes 1572872 | tf_op jit(solution)/shard_map/ppermute | solution.py:20
  27.1 13.8 %collective-permute-start.9 = (bf16[2,128,1024]{2,1,0:T(8,128)(2,1)}, bf16[2,128,1024]{2,1,0:T(8,128)(2,1)S(1)}, u32[]{:S(2)}, u32[]{:S(2)}) collective-permute-start(bf16[2,128,1024]{2,1,0:T(8,128)(2,1)} %collective-permute-done.7.refs_4_), channel_id=1, source_target_pairs={{4,0},{0,4},{5,1},{1,5},{6,2},{2,6},{7,3},{3,7},{12,8},{8,12},{13,... | collective-permute-start | bytes 1572872 | tf_op jit(solution)/shard_map/ppermute | solution.py:20
  32.1 15.0 %collective-permute-start.5 = (bf16[352,1024]{1,0:T(8,128)(2,1)S(1)}, bf16[352,1024]{1,0:T(8,128)(2,1)}, u32[]{:S(2)}, u32[]{:S(2)}) collective-permute-start(bf16[352,1024]{1,0:T(8,128)(2,1)S(1)} %get-tuple-element.108.refs_3_), channel_id=1, source_target_pairs={{2,0},{0,2},{3,1},{1,3},{6,4},{4,6},{7,5},{5,7},{10,8},{8,10},{11,... | collective-permute-start | bytes 2162696 | tf_op jit(solution)/shard_map/ppermute | solution.py:20
  33.6 12.1 %collective-permute-start.6 = (bf16[272,1024]{1,0:T(8,128)(2,1)}, bf16[272,1024]{1,0:T(8,128)(2,1)S(1)}, u32[]{:S(2)}, u32[]{:S(2)}) collective-permute-start(bf16[272,1024]{1,0:T(8,128)(2,1)} %collective-permute-done.2.refs_10_), channel_id=1, source_target_pairs={{8,0},{0,8},{24,16},{16,24},{9,1},{1,9},{25,17},{17,25},{10,2},{2,... | collective-permute-start | bytes 1671176 | tf_op jit(solution)/shard_map/ppermute | solution.py:28
  34.0 6.8 %collective-permute-start.8 = (bf16[2,128,1024]{2,1,0:T(8,128)(2,1)}, bf16[2,128,1024]{2,1,0:T(8,128)(2,1)S(1)}, u32[]{:S(2)}, u32[]{:S(2)}) collective-permute-start(bf16[2,128,1024]{2,1,0:T(8,128)(2,1)} %collective-permute-done.7.refs_4_), channel_id=1, source_target_pairs={{1,0},{0,1},{3,2},{2,3},{5,4},{4,5},{7,6},{6,7},{9,8},{8,9},{11,10... | collective-permute-start | bytes 1572872 | tf_op jit(solution)/shard_map/ppermute | solution.py:20
  40.8 6.2 %collective-permute-start.10 = (bf16[2,128,1024]{2,1,0:T(8,128)(2,1)S(1)}, bf16[2,128,1024]{2,1,0:T(8,128)(2,1)S(1)}, u32[]{:S(2)}, u32[]{:S(2)}) collective-permute-start(bf16[2,128,1024]{2,1,0:T(8,128)(2,1)S(1)} %collective-permute-done.9.refs_6_), channel_id=1, source_target_pairs={{1,0},{0,1},{3,2},{2,3},{5,4},{4,5},{7,6},{6,7},{9,8},{8,9},{11,10... | collective-permute-start | bytes 1572872 | tf_op jit(solution)/shard_map/ppermute | solution.py:20
  47.1 18.8 %collective-permute-start.11 = (bf16[352,1024]{1,0:T(8,128)(2,1)S(1)}, bf16[352,1024]{1,0:T(8,128)(2,1)S(1)}, u32[]{:S(2)}, u32[]{:S(2)}) collective-permute-start(bf16[352,1024]{1,0:T(8,128)(2,1)S(1)} %get-tuple-element.108.refs_3_), channel_id=1, source_target_pairs={{4,0},{0,4},{5,1},{1,5},{6,2},{2,6},{7,3},{3,7},{12,8},{8,12},{13,... | collective-permute-start | bytes 2162696 | tf_op jit(solution)/shard_map/ppermute | solution.py:20
  48.9 17.8 %collective-permute-start.12 = (bf16[352,1024]{1,0:T(8,128)(2,1)S(1)}, bf16[352,1024]{1,0:T(8,128)(2,1)}, u32[]{:S(2)}, u32[]{:S(2)}) collective-permute-start(bf16[352,1024]{1,0:T(8,128)(2,1)S(1)} %get-tuple-element.110.refs_5_), channel_id=1, source_target_pairs={{2,0},{0,2},{3,1},{1,3},{6,4},{4,6},{7,5},{5,7},{10,8},{8,10},{11,... | collective-permute-start | bytes 2162696 | tf_op jit(solution)/shard_map/ppermute | solution.py:20
  51.0 19.8 %all-to-all-start = ((bf16[4,704,128]{2,1,0:T(8,128)(2,1)}), bf16[4,704,128]{2,1,0:T(8,128)(2,1)}, u32[]{:S(2)}, u32[]{:S(2)}) async-start(bf16[4,704,128]{2,1,0:T(8,128)(2,1)} %bitcast.53), calls=%async_computation | async-start | bytes 1441792 | tf_op jit(solution)/shard_map/all_to_all | solution.py:275
  66.7 6.7 %collective-permute-start.13 = (bf16[512,1024]{1,0:T(8,128)(2,1)}, bf16[512,1024]{1,0:T(8,128)(2,1)S(1)}, u32[]{:S(2)}, u32[]{:S(2)}) collective-permute-start(bf16[512,1024]{1,0:T(8,128)(2,1)} %get-tuple-element.117.refs_0_.refs_2_), channel_id=1, source_target_pairs={{1,0},{0,1},{3,2},{2,3},{5,4},{4,5},{7,6},{6,7},{9,8},{8,9},{11,10... | collective-permute-start | bytes 3145736 | tf_op jit(solution)/shard_map/ppermute | solution.py:20
  66.7 6.2 %collective-permute-start.15 = (f32[1024,128]{1,0:T(8,128)}, f32[1024,128]{1,0:T(8,128)}, u32[]{:S(2)}, u32[]{:S(2)}) collective-permute-start(f32[1024,128]{1,0:T(8,128)} %get-tuple-element.120.refs_2_.refs_5_), channel_id=1, source_target_pairs={{1,0},{0,1},{3,2},{2,3},{5,4},{4,5},{7,6},{6,7},{9,8},{8,9},{11,10... | collective-permute-start | bytes 1572872 | tf_op jit(solution)/shard_map/ppermute | solution.py:20
  67.2 16.0 %collective-permute-start.14 = (bf16[512,1024]{1,0:T(8,128)(2,1)}, bf16[512,1024]{1,0:T(8,128)(2,1)}, u32[]{:S(2)}, u32[]{:S(2)}) collective-permute-start(bf16[512,1024]{1,0:T(8,128)(2,1)} %get-tuple-element.118.refs_1_.refs_3_), channel_id=1, source_target_pairs={{1,0},{0,1},{3,2},{2,3},{5,4},{4,5},{7,6},{6,7},{9,8},{8,9},{11,10... | collective-permute-start | bytes 3145736 | tf_op jit(solution)/shard_map/ppermute | solution.py:20
  67.2 23.5 %collective-permute-start.16 = (bf16[352,1024]{1,0:T(8,128)(2,1)}, bf16[352,1024]{1,0:T(8,128)(2,1)}, u32[]{:S(2)}, u32[]{:S(2)}) collective-permute-start(bf16[352,1024]{1,0:T(8,128)(2,1)} %collective-permute-done.5.refs_6_), channel_id=1, source_target_pairs={{4,0},{0,4},{5,1},{1,5},{6,2},{2,6},{7,3},{3,7},{12,8},{8,12},{13,... | collective-permute-start | bytes 2162696 | tf_op jit(solution)/shard_map/ppermute | solution.py:20
  67.3 23.5 %collective-permute-start.17 = (bf16[352,1024]{1,0:T(8,128)(2,1)}, bf16[352,1024]{1,0:T(8,128)(2,1)}, u32[]{:S(2)}, u32[]{:S(2)}) collective-permute-start(bf16[352,1024]{1,0:T(8,128)(2,1)} %copy-done.3), channel_id=1, source_target_pairs={{2,0},{0,2},{3,1},{1,3},{6,4},{4,6},{7,5},{5,7},{10,8},{8,10},{11,... | collective-permute-start | bytes 2162696 | tf_op jit(solution)/shard_map/ppermute | solution.py:20
  72.9 29.1 %collective-permute-start.18 = (bf16[704,512]{1,0:T(8,128)(2,1)}, bf16[704,512]{1,0:T(8,128)(2,1)}, u32[]{:S(2)}, u32[]{:S(2)}) collective-permute-start(bf16[704,512]{1,0:T(8,128)(2,1)} %copy_bitcast_fusion), channel_id=1, source_target_pairs={{2,0},{0,2},{3,1},{1,3},{6,4},{4,6},{7,5},{5,7},{10,8},{8,10},{11,... | collective-permute-start | bytes 2162696 | tf_op jit(solution)/shard_map/ppermute | solution.py:20
  73.4 28.6 %collective-permute-start.19 = (bf16[704,512]{1,0:T(8,128)(2,1)}, bf16[704,512]{1,0:T(8,128)(2,1)}, u32[]{:S(2)}, u32[]{:S(2)}) collective-permute-start(bf16[704,512]{1,0:T(8,128)(2,1)} %copy_bitcast_fusion), channel_id=1, source_target_pairs={{4,0},{0,4},{5,1},{1,5},{6,2},{2,6},{7,3},{3,7},{12,8},{8,12},{13,... | collective-permute-start | bytes 2162696 | tf_op jit(solution)/shard_map/ppermute | solution.py:20
  83.2 37.8 %collective-permute-start.20 = (bf16[704,512]{1,0:T(8,128)(2,1)}, bf16[704,512]{1,0:T(8,128)(2,1)S(1)}, u32[]{:S(2)}, u32[]{:S(2)}) collective-permute-start(bf16[704,512]{1,0:T(8,128)(2,1)} %copy_bitcast_fusion), channel_id=1, source_target_pairs={{6,0},{4,2},{2,4},{0,6},{7,1},{5,3},{3,5},{1,7},{14,8},{12,10},{10... | collective-permute-start | bytes 2162696 | tf_op jit(solution)/shard_map/ppermute | solution.py:301
  106.3 3.2 %collective-permute-start.24 = (bf16[256,512]{1,0:T(8,128)(2,1)S(1)}, bf16[256,512]{1,0:T(8,128)(2,1)S(1)}, u32[]{:S(2)}, u32[]{:S(2)}) collective-permute-start(bf16[256,512]{1,0:T(8,128)(2,1)S(1)} %get-tuple-element.160), channel_id=1, source_target_pairs={{1,0},{0,1},{3,2},{2,3},{5,4},{4,5},{7,6},{6,7},{9,8},{8,9},{11,10... | collective-permute-start | bytes 786440 | tf_op jit(solution)/shard_map/ppermute | solution.py:20
  111.6 9.2 %collective-permute-start.25 = (bf16[256,512]{1,0:T(8,128)(2,1)S(1)}, bf16[256,512]{1,0:T(8,128)(2,1)S(1)}, u32[]{:S(2)}, u32[]{:S(2)}) collective-permute-start(bf16[256,512]{1,0:T(8,128)(2,1)S(1)} %get-tuple-element.154), channel_id=1, source_target_pairs={{8,0},{0,8},{24,16},{16,24},{9,1},{1,9},{25,17},{17,25},{10,2},{2,... | collective-permute-start | bytes 786440 | tf_op jit(solution)/shard_map/ppermute | solution.py:28
  113.8 19.6 %collective-permute-start.31 = (bf16[256,512]{1,0:T(8,128)(2,1)S(1)}, bf16[256,512]{1,0:T(8,128)(2,1)S(1)}, u32[]{:S(2)}, u32[]{:S(2)}) collective-permute-start(bf16[256,512]{1,0:T(8,128)(2,1)S(1)} %get-tuple-element.152), channel_id=1, source_target_pairs={{8,0},{0,8},{24,16},{16,24},{9,1},{1,9},{25,17},{17,25},{10,2},{2,... | collective-permute-start | bytes 786440 | tf_op jit(solution)/shard_map/ppermute | solution.py:28
  124.2 4.9 %collective-permute-start.28 = (bf16[256,512]{1,0:T(8,128)(2,1)S(1)}, bf16[256,512]{1,0:T(8,128)(2,1)S(1)}, u32[]{:S(2)}, u32[]{:S(2)}) collective-permute-start(bf16[256,512]{1,0:T(8,128)(2,1)S(1)} %get-tuple-element.157), channel_id=1, source_target_pairs={{1,0},{0,1},{3,2},{2,3},{5,4},{4,5},{7,6},{6,7},{9,8},{8,9},{11,10... | collective-permute-start | bytes 786440 | tf_op jit(solution)/shard_map/ppermute | solution.py:20
  124.7 4.4 %collective-permute-start.27 = (bf16[256,512]{1,0:T(8,128)(2,1)S(1)}, bf16[256,512]{1,0:T(8,128)(2,1)S(1)}, u32[]{:S(2)}, u32[]{:S(2)}) collective-permute-start(bf16[256,512]{1,0:T(8,128)(2,1)S(1)} %get-tuple-element.158), channel_id=1, source_target_pairs={{1,0},{0,1},{3,2},{2,3},{5,4},{4,5},{7,6},{6,7},{9,8},{8,9},{11,10... | collective-permute-start | bytes 786440 | tf_op jit(solution)/shard_map/ppermute | solution.py:20
  124.7 4.3 %collective-permute-start.26 = (bf16[256,512]{1,0:T(8,128)(2,1)S(1)}, bf16[256,512]{1,0:T(8,128)(2,1)S(1)}, u32[]{:S(2)}, u32[]{:S(2)}) collective-permute-start(bf16[256,512]{1,0:T(8,128)(2,1)S(1)} %get-tuple-element.155), channel_id=1, source_target_pairs={{1,0},{0,1},{3,2},{2,3},{5,4},{4,5},{7,6},{6,7},{9,8},{8,9},{11,10... | collective-permute-start | bytes 786440 | tf_op jit(solution)/shard_map/ppermute | solution.py:20
  126.2 15.2 %collective-permute-start.32 = (bf16[256,512]{1,0:T(8,128)(2,1)S(1)}, bf16[256,512]{1,0:T(8,128)(2,1)S(1)}, u32[]{:S(2)}, u32[]{:S(2)}) collective-permute-start(bf16[256,512]{1,0:T(8,128)(2,1)S(1)} %add_convert_fusion.5), channel_id=1, source_target_pairs={{16,0},{24,8},{0,16},{8,24},{17,1},{25,9},{1,17},{9,25},{18,2},{26... | collective-permute-start | bytes 786440 | tf_op jit(solution)/shard_map/ppermute | solution.py:28
  131.3 13.5 %collective-permute-start.30 = (bf16[256,512]{1,0:T(8,128)(2,1)S(1)}, bf16[256,512]{1,0:T(8,128)(2,1)S(1)}, u32[]{:S(2)}, u32[]{:S(2)}) collective-permute-start(bf16[256,512]{1,0:T(8,128)(2,1)S(1)} %get-tuple-element.151), channel_id=1, source_target_pairs={{8,0},{0,8},{24,16},{16,24},{9,1},{1,9},{25,17},{17,25},{10,2},{2,... | collective-permute-start | bytes 786440 | tf_op jit(solution)/shard_map/ppermute | solution.py:28
  132.8 18.5 %collective-permute-start.33 = (bf16[256,512]{1,0:T(8,128)(2,1)S(1)}, bf16[256,512]{1,0:T(8,128)(2,1)S(1)}, u32[]{:S(2)}, u32[]{:S(2)}) collective-permute-start(bf16[256,512]{1,0:T(8,128)(2,1)S(1)} %get-tuple-element.149), channel_id=1, source_target_pairs={{8,0},{0,8},{24,16},{16,24},{9,1},{1,9},{25,17},{17,25},{10,2},{2,... | collective-permute-start | bytes 786440 | tf_op jit(solution)/shard_map/ppermute | solution.py:28
  144.8 12.5 %collective-permute-start.34 = (bf16[256,512]{1,0:T(8,128)(2,1)S(1)}, bf16[256,512]{1,0:T(8,128)(2,1)S(1)}, u32[]{:S(2)}, u32[]{:S(2)}) collective-permute-start(bf16[256,512]{1,0:T(8,128)(2,1)S(1)} %add_convert_fusion.4), channel_id=1, source_target_pairs={{16,0},{24,8},{0,16},{8,24},{17,1},{25,9},{1,17},{9,25},{18,2},{26... | collective-permute-start | bytes 786440 | tf_op jit(solution)/shard_map/ppermute | solution.py:28
  (30 other events, 273.8 us)
